TPU v7x, 32 devices: a whole 2x2x4 slice. The times are simulated.
32 devices in a mesh: dp: 16 (over z, x, core), tensor: 2 (over y).
Axes of the slice: x: 2, y: 2, z: 4, core: 2. Of those that a mesh axis runs over, the one named last changes fastest.
Arguments:
- tokens: bfloat16 [2, 2048, 2048], P(None, 'dp', 'tensor'), may hold values from -6 to 6
- segments: int32 [2, 2048], P(None, 'dp'), may hold values from 0 to 1, as said below
- cotangent: bfloat16 [2, 2048, 2048], P(None, 'dp', 'tensor'), may hold values from -6 to 6
- norm_gain: bfloat16 [2048], P('dp'), may hold values from 0.5 to 1.5
- w_in: bfloat16 [2048, 2, 4096], P('dp', None, 'tensor'), may hold values from -0.125 to 0.125
- conv_w: bfloat16 [4, 4096], P(None, ('tensor', 'dp')), may hold values from -3 to 3
- conv_b: bfloat16 [4096], P(('tensor', 'dp')), may hold values from -1.5 to 1.5
- w_x: bfloat16 [4096, 160], P(('tensor', 'dp')), may hold values from -0.375 to 0.375
- w_dt: bfloat16 [128, 4096], P('dp', 'tensor'), may hold values from -0.5 to 0.5
- dt_bias: bfloat16 [4096], P(('tensor', 'dp')), may hold values from -7 to -2
- a_log: bfloat16 [4096, 16], P(('tensor', 'dp')), may hold values from -4 to 2.796875
- d_skip: bfloat16 [4096], P(('tensor', 'dp')), may hold values from 0.19921875 to 3.5
- w_out: bfloat16 [4096, 2048], P('tensor', 'dp'), may hold values from -0.1875 to 0.1875
Outputs:
- block_out: bfloat16 [2, 2048, 2048], P(None, 'dp', 'tensor')
- input_grad: float32 [2, 2048, 2048], P(None, 'dp', 'tensor')
- grad_gain: float32 [2048], P('dp')
- grad_w_in: float32 [2048, 2, 4096], P('dp', None, 'tensor')
- grad_conv_w: float32 [4, 4096], P(None, ('tensor', 'dp'))
- grad_conv_b: float32 [4096], P(('tensor', 'dp'))
- grad_w_x: float32 [4096, 160], P(('tensor', 'dp'))
- grad_w_dt: float32 [128, 4096], P('dp', 'tensor')
- grad_dt_bias: float32 [4096], P(('tensor', 'dp'))
- grad_a_log: float32 [4096, 16], P(('tensor', 'dp'))
- grad_skip: float32 [4096], P(('tensor', 'dp'))
- grad_w_out: float32 [4096, 2048], P('tensor', 'dp')
Inputs may be any that keep to these rules, and one draw needn't show every extreme that they name: `segments`: in each sequence the mark is 0 at the first token and switches between 0 and 1 exactly where a new document starts; documents hold 200 to 2000 tokens except the last of a sequence, which may be shorter; one sequence, drawn from the seed, is a single document.
All inputs are finite; a program needn't handle non-finite values.
Results may differ from a plain program's by a relative error of at most 0.007.
The roundings to bfloat16 on the way count: a program that leaves them out, or rounds other values in their place, can miss the bound.
Values may be sent and summed in bfloat16 or wider, within the bound.
No kernel may reach another device: no remote copies, remote signals or barrier semaphores. Data moves between devices by JAX's collectives and lax.ppermute only.
A program may use at most 192 MiB of HBM per device.

v0:
```python
import jax
import jax.numpy as jnp
from jax import lax
from jax.sharding import PartitionSpec as P

NSTATE = 16
RANK = 128


epsilon = 1e-05


def shifted(block, axis, distance):
    devices = range(lax.axis_size(axis))
    route = [(i - distance, i) for i in devices if i - distance in devices]
    return lax.ppermute(block, axis, route)


def entering_2(array, axis, combine, identity, reverse):
    devices, position = (lax.axis_size(axis), lax.axis_index(axis))
    everything = jax.tree.map(lambda part: lax.all_gather(part, axis), array)
    start = jax.tree.map(
        lambda part, zero: jnp.broadcast_to(jnp.asarray(zero, part.dtype), part.shape),
        array,
        identity,
    )

    def lap(k, before):
        at = devices - 1 - k if reverse else k
        reached = at > position if reverse else at < position
        new = combine(before, jax.tree.map(lambda part: part[at], everything))
        return jax.tree.map(lambda a, b: jnp.where(reached, a, b), new, before)

    return lax.fori_loop(0, devices, lap, start)


def silu_slope(values):
    squash = jax.nn.sigmoid(values)
    return squash * (1.0 + values * (1.0 - squash))


def carry_join(earlier, latter):
    return (earlier[0] * latter[0], latter[0] * earlier[1] + latter[1])


def decay_of(delta_blk, keep_blk, a_mat):
    return jnp.exp(delta_blk[:, None, :] * a_mat[None]) * keep_blk[:, None, None]


def as_blocks(tensor_in, block_rows):
    return tensor_in.reshape((tensor_in.shape[0] // block_rows, block_rows) + tensor_in.shape[1:])


def reverse_pair(decay_rows, emitted):
    running, local_part = lax.associative_scan(
        carry_join, (jnp.flip(decay_rows, 0), jnp.flip(decay_rows * emitted, 0)), axis=0
    )
    return (jnp.flip(running, 0), jnp.flip(local_part, 0))


def forward_summary(delta_rows, flow_rows, b_part, keep_rows, a_mat, block_rows):

    def advance(carried, pieces):
        delta_blk, flow_blk, b_blk, keep_blk = pieces
        decay_rows = decay_of(delta_blk, keep_blk, a_mat)
        inflow = flow_blk[:, None, :] * b_blk[:, :, None]
        running, local_part = lax.associative_scan(carry_join, (decay_rows, inflow), axis=0)
        return (carry_join(carried, (running[-1], local_part[-1])), None)

    start_state = (jnp.ones(a_mat.shape, jnp.float32), jnp.zeros(a_mat.shape, jnp.float32))
    pieces = tuple(
        (as_blocks(member, block_rows) for member in (delta_rows, flow_rows, b_part, keep_rows))
    )
    summary, unused = lax.scan(advance, start_state, pieces)
    return summary


def forward_sweep(start_state, delta_rows, flow_rows, b_part, c_part, keep_rows, a_mat, block_rows):

    def advance(state_now, pieces):
        delta_blk, flow_blk, b_blk, c_blk, keep_blk = pieces
        decay_rows = decay_of(delta_blk, keep_blk, a_mat)
        inflow = flow_blk[:, None, :] * b_blk[:, :, None]
        running, local_part = lax.associative_scan(carry_join, (decay_rows, inflow), axis=0)
        states = local_part + running * state_now[None]
        return (states[-1], (jnp.sum(states * c_blk[:, :, None], axis=1), state_now))

    pieces = tuple(
        (
            as_blocks(member, block_rows)
            for member in (delta_rows, flow_rows, b_part, c_part, keep_rows)
        )
    )
    unused, (outputs, starts) = lax.scan(advance, start_state, pieces)
    return (outputs.reshape(delta_rows.shape), starts)


def reverse_summary(delta_rows, keep_rows, grad_ssm, c_part, a_mat, block_rows):

    def advance(carried, pieces):
        delta_blk, keep_blk, grad_blk, c_blk = pieces
        decay_rows = decay_of(delta_blk, keep_blk, a_mat)
        emitted = grad_blk[:, None, :] * c_blk[:, :, None]
        running, local_part = reverse_pair(decay_rows, emitted)
        return (carry_join(carried, (running[0], local_part[0])), None)

    start_state = (jnp.ones(a_mat.shape, jnp.float32), jnp.zeros(a_mat.shape, jnp.float32))
    pieces = tuple(
        (as_blocks(member, block_rows) for member in (delta_rows, keep_rows, grad_ssm, c_part))
    )
    summary, unused = lax.scan(advance, start_state, pieces, reverse=True)
    return summary


def reverse_sweep(
    incoming,
    starts,
    delta_rows,
    flow_rows,
    conv_rows,
    b_part,
    c_part,
    keep_rows,
    grad_ssm,
    a_mat,
    block_rows,
):

    def advance(carried, pieces):
        delta_blk, flow_blk, conv_blk, b_blk, c_blk, keep_blk, grad_blk, start_state = pieces
        decay_rows = decay_of(delta_blk, keep_blk, a_mat)
        inflow = flow_blk[:, None, :] * b_blk[:, :, None]
        running, local_part = lax.associative_scan(carry_join, (decay_rows, inflow), axis=0)
        states = local_part + running * start_state[None]
        previous = jnp.concatenate([start_state[None], states[:-1]], axis=0)
        emitted = grad_blk[:, None, :] * c_blk[:, :, None]
        back_run, back_local = reverse_pair(decay_rows, emitted)
        passed = back_local + back_run * carried[None]
        grad_state = emitted + jnp.concatenate([passed[1:], carried[None]], axis=0)
        decay_term = grad_state * previous * decay_rows
        input_term = jnp.sum(grad_state * b_blk[:, :, None], axis=1)
        grad_delta = jnp.sum(decay_term * a_mat[None], axis=1) + input_term * conv_blk
        grad_conv = input_term * delta_blk
        grad_b = jnp.sum(grad_state * flow_blk[:, None, :], axis=2)
        grad_c = jnp.sum(states * grad_blk[:, None, :], axis=2)
        grad_amat = jnp.sum(decay_term * delta_blk[:, None, :], axis=0)
        return (passed[0], (grad_delta, grad_conv, grad_b, grad_c, grad_amat))

    pieces = tuple(
        (
            as_blocks(member, block_rows)
            for member in (delta_rows, flow_rows, conv_rows, b_part, c_part, keep_rows, grad_ssm)
        )
    ) + (starts,)
    unused, results = lax.scan(advance, incoming, pieces, reverse=True)
    grad_delta, grad_conv, grad_b, grad_c, grad_amat = results
    return (
        grad_delta.reshape(delta_rows.shape),
        grad_conv.reshape(delta_rows.shape),
        grad_b.reshape(b_part.shape),
        grad_c.reshape(c_part.shape),
        jnp.sum(grad_amat, axis=0),
    )


def local(
    tokens,
    segments,
    cotangent,
    norm_gain,
    w_in,
    conv_w,
    conv_b,
    w_x,
    w_dt,
    dt_bias,
    a_log,
    d_skip,
    w_out,
):
    micro_count = tokens.shape[0]
    row_count = tokens.shape[1]
    col_width = tokens.shape[2]
    block_rows = 16
    tap_count = conv_w.shape[0]
    reach_back = tap_count - 1
    whole_tokens, whole_cot = (
        lax.all_gather(tokens, "tensor", axis=2, tiled=True),
        lax.all_gather(cotangent, "tensor", axis=2, tiled=True),
    )
    full_width = whole_tokens.shape[2]
    marks_own = segments + 1
    marks_before = shifted(marks_own[:, row_count - reach_back :], "dp", 1)
    marks_all = jnp.concatenate([marks_before, marks_own], axis=1)
    column = lax.axis_index("tensor") * col_width
    outputs = []
    input_grads = []
    shards = None
    for micro_index in range(micro_count):
        fetched = (
            lax.all_gather(norm_gain, "dp", axis=0, tiled=True),
            lax.all_gather(w_in, "dp", axis=0, tiled=True),
            lax.all_gather(conv_w, "dp", axis=1, tiled=True),
            lax.all_gather(conv_b, "dp", axis=0, tiled=True),
            lax.all_gather(w_x, "dp", axis=0, tiled=True),
            lax.all_gather(w_dt, "dp", axis=0, tiled=True),
            lax.all_gather(dt_bias, "dp", axis=0, tiled=True),
            lax.all_gather(a_log, "dp", axis=0, tiled=True),
            lax.all_gather(d_skip, "dp", axis=0, tiled=True),
            lax.all_gather(w_out, "dp", axis=1, tiled=True),
        )
        (
            gain_full,
            in_full,
            taps_full,
            bias_full,
            xproj_full,
            dtproj_full,
            shift_full,
            alog_full,
            skip_full,
            out_full,
        ) = fetched
        x_rows = whole_tokens[micro_index].astype(jnp.float32)
        scale_rows = lax.rsqrt(jnp.mean(x_rows * x_rows, axis=1, keepdims=True) + epsilon)
        normed = (x_rows * scale_rows * gain_full.astype(jnp.float32)).astype(jnp.bfloat16)
        both_parts = jnp.einsum("td,dkc->tkc", normed, in_full, preferred_element_type=jnp.float32)
        inner_rows = both_parts[:, 0].astype(jnp.bfloat16)
        gate_rows = both_parts[:, 1]
        tail_rows = shifted(inner_rows[row_count - reach_back :], "dp", 1)
        inner_ext = jnp.concatenate([tail_rows, inner_rows], axis=0).astype(jnp.float32)
        mark_row = marks_all[micro_index]
        own_marks = marks_own[micro_index]
        tap_masks = [
            (mark_row[offset : offset + row_count] == own_marks).astype(jnp.float32)[:, None]
            for offset in range(tap_count)
        ]
        taps_f = taps_full.astype(jnp.float32)
        mixed_rows = (
            jnp.zeros(inner_rows.shape, jnp.float32) + bias_full.astype(jnp.float32)[None, :]
        )
        for offset in range(tap_count):
            mixed_rows = (
                mixed_rows
                + taps_f[offset][None, :]
                * inner_ext[offset : offset + row_count]
                * tap_masks[offset]
            )
        conv_out = jax.nn.silu(mixed_rows).astype(jnp.bfloat16)
        conv_rows = conv_out.astype(jnp.float32)
        projected = lax.psum(
            jnp.dot(conv_out, xproj_full, preferred_element_type=jnp.float32), "tensor"
        )
        rank_part = projected[:, :RANK].astype(jnp.bfloat16)
        b_part = projected[:, RANK : RANK + NSTATE]
        c_part = projected[:, RANK + NSTATE :]
        pre_delta = (
            jnp.dot(rank_part, dtproj_full, preferred_element_type=jnp.float32)
            + shift_full.astype(jnp.float32)[None, :]
        )
        delta_rows = jax.nn.softplus(pre_delta)
        keep_rows = (mark_row[reach_back - 1 : reach_back - 1 + row_count] == own_marks).astype(
            jnp.float32
        )
        a_mat = -jnp.exp(alog_full.astype(jnp.float32)).T
        flow_rows = delta_rows * conv_rows
        total_decay, end_state = forward_summary(
            delta_rows, flow_rows, b_part, keep_rows, a_mat, block_rows
        )
        entering = entering_2(
            (total_decay, end_state),
            "dp",
            carry_join,
            (jnp.ones_like(total_decay), jnp.zeros_like(end_state)),
            False,
        )
        readout, starts = forward_sweep(
            entering[1], delta_rows, flow_rows, b_part, c_part, keep_rows, a_mat, block_rows
        )
        skip_f = skip_full.astype(jnp.float32)
        ssm_rows = readout + skip_f[None, :] * conv_rows
        silu_gate = jax.nn.silu(gate_rows)
        gated = (ssm_rows * silu_gate).astype(jnp.bfloat16)
        branch = lax.psum_scatter(
            jnp.dot(gated, out_full, preferred_element_type=jnp.float32),
            "tensor",
            scatter_dimension=1,
            tiled=True,
        )
        outputs.append((tokens[micro_index].astype(jnp.float32) + branch).astype(jnp.bfloat16))
        refetched = (
            lax.all_gather(norm_gain, "dp", axis=0, tiled=True),
            lax.all_gather(w_in, "dp", axis=0, tiled=True),
            lax.all_gather(conv_w, "dp", axis=1, tiled=True),
            lax.all_gather(conv_b, "dp", axis=0, tiled=True),
            lax.all_gather(w_x, "dp", axis=0, tiled=True),
            lax.all_gather(w_dt, "dp", axis=0, tiled=True),
            lax.all_gather(dt_bias, "dp", axis=0, tiled=True),
            lax.all_gather(a_log, "dp", axis=0, tiled=True),
            lax.all_gather(d_skip, "dp", axis=0, tiled=True),
            lax.all_gather(w_out, "dp", axis=1, tiled=True),
        )
        (
            gain_back,
            in_back,
            taps_back,
            bias_back,
            xproj_back,
            dtproj_back,
            shift_back,
            alog_back,
            skip_back,
            out_back,
        ) = refetched
        cot_rows = whole_cot[micro_index]
        grad_out_w = jnp.einsum("tc,td->cd", gated, cot_rows, preferred_element_type=jnp.float32)
        grad_gated = jnp.einsum("td,cd->tc", cot_rows, out_back, preferred_element_type=jnp.float32)
        grad_ssm = grad_gated * silu_gate
        grad_gate = grad_gated * ssm_rows * silu_slope(gate_rows)
        grad_skip = jnp.sum(grad_ssm * conv_rows, axis=0)
        back_decay, back_value = reverse_summary(
            delta_rows, keep_rows, grad_ssm, c_part, a_mat, block_rows
        )
        leaving = entering_2(
            (back_decay, back_value),
            "dp",
            carry_join,
            (jnp.ones_like(back_decay), jnp.zeros_like(back_value)),
            True,
        )
        grad_delta, grad_conv_scan, grad_b, grad_c, grad_amat = reverse_sweep(
            leaving[1],
            starts,
            delta_rows,
            flow_rows,
            conv_rows,
            b_part,
            c_part,
            keep_rows,
            grad_ssm,
            a_mat,
            block_rows,
        )
        grad_pre = grad_delta * jax.nn.sigmoid(pre_delta)
        grad_shift = jnp.sum(grad_pre, axis=0)
        grad_pre_low = grad_pre.astype(jnp.bfloat16)
        grad_dt_w = jnp.einsum(
            "tr,tc->rc", rank_part, grad_pre_low, preferred_element_type=jnp.float32
        )
        grad_rank = jnp.einsum(
            "tc,rc->tr", grad_pre_low, dtproj_back, preferred_element_type=jnp.float32
        )
        grad_proj = lax.psum(jnp.concatenate([grad_rank, grad_b, grad_c], axis=1), "tensor").astype(
            jnp.bfloat16
        )
        grad_xproj = jnp.einsum(
            "tc,tp->cp", conv_out, grad_proj, preferred_element_type=jnp.float32
        )
        grad_conv = (
            grad_conv_scan
            + skip_back.astype(jnp.float32)[None, :] * grad_ssm
            + jnp.einsum("tp,cp->tc", grad_proj, xproj_back, preferred_element_type=jnp.float32)
        )
        grad_mixed = grad_conv * silu_slope(mixed_rows)
        grad_bias = jnp.sum(grad_mixed, axis=0)
        taps_again = taps_back.astype(jnp.float32)
        grad_taps = jnp.stack(
            [
                jnp.sum(
                    grad_mixed * inner_ext[offset : offset + row_count] * tap_masks[offset], axis=0
                )
                for offset in range(tap_count)
            ]
        )
        grad_ext = jnp.zeros((row_count + reach_back, grad_mixed.shape[1]), jnp.float32)
        for offset in range(tap_count):
            grad_ext = grad_ext + jnp.pad(
                taps_again[offset][None, :] * grad_mixed * tap_masks[offset],
                ((offset, reach_back - offset), (0, 0)),
            )
        returned = shifted(grad_ext[:reach_back], "dp", -1)
        grad_inner = grad_ext[reach_back:] + jnp.pad(
            returned, ((row_count - reach_back, 0), (0, 0))
        )
        grad_both = jnp.stack([grad_inner, grad_gate], axis=1).astype(jnp.bfloat16)
        grad_in_w = jnp.einsum("td,tkc->dkc", normed, grad_both, preferred_element_type=jnp.float32)
        grad_normed = lax.psum_scatter(
            jnp.einsum("tkc,dkc->td", grad_both, in_back, preferred_element_type=jnp.float32),
            "tensor",
            scatter_dimension=1,
            tiled=True,
        )
        x_local = tokens[micro_index].astype(jnp.float32)
        gain_local = lax.dynamic_slice_in_dim(gain_back.astype(jnp.float32), column, col_width, 0)
        weighted = grad_normed * gain_local[None, :]
        gain_piece = jnp.sum(grad_normed * x_local * scale_rows, axis=0)
        gain_placed = lax.dynamic_update_slice_in_dim(
            jnp.zeros((full_width,), jnp.float32), gain_piece, column, 0
        )
        row_total, grad_gain = lax.psum(
            (jnp.sum(weighted * x_local, axis=1, keepdims=True), gain_placed), "tensor"
        )
        scale_cube = scale_rows * scale_rows * scale_rows
        grad_rows = scale_rows * weighted - x_local * scale_cube * (row_total / full_width)
        input_grads.append(cotangent[micro_index].astype(jnp.float32) + grad_rows)
        grad_alog = (grad_amat * a_mat).T
        reduced = (
            lax.psum_scatter(grad_gain, "dp", scatter_dimension=0, tiled=True),
            lax.psum_scatter(grad_in_w, "dp", scatter_dimension=0, tiled=True),
            lax.psum_scatter(grad_taps, "dp", scatter_dimension=1, tiled=True),
            lax.psum_scatter(grad_bias, "dp", scatter_dimension=0, tiled=True),
            lax.psum_scatter(grad_xproj, "dp", scatter_dimension=0, tiled=True),
            lax.psum_scatter(grad_dt_w, "dp", scatter_dimension=0, tiled=True),
            lax.psum_scatter(grad_shift, "dp", scatter_dimension=0, tiled=True),
            lax.psum_scatter(grad_alog, "dp", scatter_dimension=0, tiled=True),
            lax.psum_scatter(grad_skip, "dp", scatter_dimension=0, tiled=True),
            lax.psum_scatter(grad_out_w, "dp", scatter_dimension=1, tiled=True),
        )
        shards = reduced if shards is None else jax.tree.map(jnp.add, shards, reduced)
    return (
        jnp.stack(outputs),
        jnp.stack(input_grads),
        shards[0],
        shards[1],
        shards[2],
        shards[3],
        shards[4],
        shards[5],
        shards[6],
        shards[7],
        shards[8],
        shards[9],
    )


def solution(mesh):
    return jax.shard_map(
        local,
        mesh=mesh,
        in_specs=(
            P(None, "dp", "tensor"),
            P(None, "dp"),
            P(None, "dp", "tensor"),
            P("dp"),
            P("dp", None, "tensor"),
            P(None, ("tensor", "dp")),
            P(("tensor", "dp")),
            P(("tensor", "dp"), None),
            P("dp", "tensor"),
            P(("tensor", "dp")),
            P(("tensor", "dp"), None),
            P(("tensor", "dp")),
            P("tensor", "dp"),
        ),
        out_specs=(
            P(None, "dp", "tensor"),
            P(None, "dp", "tensor"),
            P("dp"),
            P("dp", None, "tensor"),
            P(None, ("tensor", "dp")),
            P(("tensor", "dp")),
            P(("tensor", "dp"), None),
            P("dp", "tensor"),
            P(("tensor", "dp")),
            P(("tensor", "dp"), None),
            P(("tensor", "dp")),
            P("tensor", "dp"),
        ),
        check_vma=False,
    )
```

profile of v0, /device:TPU:0, one launch (start us, length us, event | category | flops | bytes accessed | tf_op | source)
XLA Modules:
  0.0 6501.4 jit_solution(76197404996606187)
XLA Ops:
  14.4 22.5 all-gather.9
  37.0 17.3 all-gather.8
  54.4 19.2 all-gather.10
  73.6 17.6 all_gather.109
  91.1 19.6 all_gather.116
  110.7 23.2 all_gather.113
  138.1 32.1 all-gather.27.cloned.1.call-done
  191.2 80.1 %all-gather.29.cloned.1.call-done = bf16[2048,2048]{1,0:T(8,128)(2,1)} async-done(((bf16[2048,128]{1,0:T(8,128)(2,1)}), bf16[2048,2048]{1,0:T(8,128)(2,1)}) %all-gather.29.cloned.1.call-update) | async-done | bytes 8388624 | tf_op jit(solution)/shard_map/all_gather | solution.py:210
  290.9 20.3 all_gather.114
  316.1 238.5 %while.204 = (s32[]{:T(128)}, f32[16,2048]{1,0:T(8,128)}, f32[16,2048]{1,0:T(8,128)}, f32[8,16,2048]{2,1,0:T(8,128)}, f32[16,2048]{1,0:T(8,128)S(1)}, /*index=5*...) while((s32[]{:T(128)}, f32[16,2048]{1,0:T(8,128)}, ...), condition=%wide.region_21.22_spmd.clone, body=%wide.region_20.21_spmd.clone.sunk | while | flops 5799940 | bytes 76680912 | solution.py:111
  556.0 235.5 %while.200 = (s32[]{:T(128)}, f32[16,2048]{1,0:T(8,128)}, f32[16,2048]{1,0:T(8,128)}, f32[8,16,2048]{2,1,0:T(8,128)}, f32[16,2048]{1,0:T(8,128)S(1)}, /*index=5*...) while((s32[]{:T(128)}, f32[16,2048]{1,0:T(8,128)}, ...), condition=%wide.region_3.4_spmd.clone, body=%wide.region_2.3_spmd.clone.sunk | while | flops 5275651 | bytes 68292296 | solution.py:74
  797.5 245.3 %while.206 = (s32[]{:T(128)}, f32[16,2048]{1,0:T(8,128)}, f32[16,2048]{1,0:T(8,128)}, f32[8,16,2048]{2,1,0:T(8,128)}, f32[16,2048]{1,0:T(8,128)S(1)}, /*index=5*...) while((s32[]{:T(128)}, f32[16,2048]{1,0:T(8,128)}, ...), condition=%wide.region_36.37_spmd.clone, body=%wide.region_35.36_spmd.clone.sunk | while | flops 5799940 | bytes 76680912 | solution.py:111
  1043.7 242.7 %while.202 = (s32[]{:T(128)}, f32[16,2048]{1,0:T(8,128)}, f32[16,2048]{1,0:T(8,128)}, f32[8,16,2048]{2,1,0:T(8,128)}, f32[16,2048]{1,0:T(8,128)S(1)}, /*index=5*...) while((s32[]{:T(128)}, f32[16,2048]{1,0:T(8,128)}, ...), condition=%wide.region_13.14_spmd.clone, body=%wide.region_12.13_spmd.clone.sunk | while | flops 5275651 | bytes 68292296 | solution.py:74
  1286.6 21.1 all-gather.11
  1311.7 17.6 while.205
  1329.3 17.5 while.201
  1349.0 620.7 %while.196 = (s32[]{:T(128)}, f32[16,2048]{1,0:T(8,128)S(1)}, f32[8,16,2048]{2,1,0:T(8,128)}, f32[8,16,2048]{2,1,0:T(8,128)}, f32[8,16,2048]{2,1,0:T(8,128)}, /*...) while((s32[]{:T(128)}, f32[16,2048]{1,0:T(8,128)S(1)}, ...), condition=%wide.region_8.9_spmd, body=%wide.region_6.8_spmd.sunk | while | flops 9797634 | bytes 128457448 | solution.py:94
  1974.3 1500.9 %while.198 = (s32[]{:T(128)}, f32[16,2048]{1,0:T(8,128)S(1)}, f32[8,16,2048]{2,1,0:T(8,128)}, f32[8,16,2048]{2,1,0:T(8,128)}, f32[8,16,16]{2,1,0:T(8,128)}, /*in...) while((s32[]{:T(128)}, f32[16,2048]{1,0:T(8,128)S(1)}, ...), condition=%wide.region_30.31_spmd, body=%wide.region_24.30_spmd.sunk | while | flops 28048900 | bytes 300842080 | solution.py:155
  3475.2 17.6 while.207
  3492.8 17.5 while.203
  3512.5 620.8 %while.197 = (s32[]{:T(128)}, f32[16,2048]{1,0:T(8,128)S(1)}, f32[8,16,2048]{2,1,0:T(8,128)}, f32[8,16,2048]{2,1,0:T(8,128)}, f32[8,16,2048]{2,1,0:T(8,128)}, /*...) while((s32[]{:T(128)}, f32[16,2048]{1,0:T(8,128)S(1)}, ...), condition=%wide.region_18.19_spmd, body=%wide.region_16.18_spmd.sunk | while | flops 9797634 | bytes 128457448 | solution.py:94
  4137.9 1480.3 %while.199 = (s32[]{:T(128)}, f32[16,2048]{1,0:T(8,128)S(1)}, f32[8,16,2048]{2,1,0:T(8,128)}, f32[8,16,2048]{2,1,0:T(8,128)}, f32[8,16,16]{2,1,0:T(8,128)}, /*in...) while((s32[]{:T(128)}, f32[16,2048]{1,0:T(8,128)S(1)}, ...), condition=%wide.region_45.46_spmd, body=%wide.region_39.45_spmd.sunk | while | flops 28048900 | bytes 300317760 | solution.py:155
  5653.1 12.8 convolution_bitcast_fusion.1
  5671.1 12.7 convolution_bitcast_fusion
  5695.5 14.7 fusion.102
  5710.2 22.2 convolution_add_fusion
  5758.6 60.2 all-reduce.174
  5830.2 303.8 %reduce-scatter.21.cloned.1.call-done = f32[128,2,2048]{2,0,1:T(8,128)} async-done(((f32[2048,2,2048]{2,0,1:T(8,128)}), f32[128,2,2048]{2,0,1:T(8,128)}) %reduce-scatter.21.cloned.1.call-update) | async-done | bytes 2097168 | tf_op jit(solution)/shard_map/reduce_scatter | solution.py:409
  6138.5 50.8 reduce-scatter.27.cloned.1.call-done
  6189.4 60.6 reduce-scatter.25.cloned.1.call-done
  6250.0 62.0 reduce-scatter.23.cloned.1.call-done
  6312.0 182.4 %reduce-scatter.29.cloned.1.call-done = f32[2048,128]{1,0:T(8,128)} async-done(((f32[2048,2048]{1,0:T(8,128)}), f32[2048,128]{1,0:T(8,128)}) %reduce-scatter.29.cloned.1.call-update) | async-done | bytes 1048592 | tf_op jit(solution)/shard_map/reduce_scatter | solution.py:417
  (6038 shorter events, 5409.6 us)
Async XLA Ops:
  7.2 128.8 %all-gather.25.cloned.1.call-start = ((), (), s32[]{:S(2)}) async-start(), calls=%async_computation.10 | async-start | bytes 1572864 | tf_op jit(solution)/shard_map/all_gather | solution.py:188
  8.0 162.2 %all-gather.27.cloned.1.call-start = ((), (), s32[]{:S(2)}) async-start(), calls=%async_computation.11 | async-start | bytes 17825792 | tf_op jit(solution)/shard_map/all_gather | solution.py:202
  10.6 180.6 %all-gather.31.cloned.1.call-start = ((), (), s32[]{:S(2)}) async-start(), calls=%async_computation.15 | async-start | bytes 1572864 | tf_op jit(solution)/shard_map/all_gather | solution.py:189
  11.3 260.0 %all-gather.29.cloned.1.call-start = ((), (), s32[]{:S(2)}) async-start(), calls=%async_computation.12 | async-start | bytes 8912896 | tf_op jit(solution)/shard_map/all_gather | solution.py:210
  11.9 299.4 %all-reduce.181.cloned.1.call-start = ((), (), s32[]{:S(2)}) async-start(), calls=%async_computation.32 | async-start | bytes 327680 | tf_op jit(solution)/shard_map/psum | solution.py:251
  12.1 122.0 %collective-permute-start.1 = (s32[2,3]{1,0:T(2,128)S(1)}, s32[2,3]{1,0:T(2,128)S(1)}, u32[]{:S(2)}, u32[]{:S(2)}) collective-permute-start(s32[2,3]{1,0:T(2,128)S(1)} %slice.2700), channel_id=1, source_target_pairs={{0,2},{2,4},{4,6},{6,8},{8,10},{10,12},{12,14},{14,16},{16,18},{18... | collective-permute-start | bytes 80 | tf_op jit(solution)/shard_map/ppermute | solution.py:16
  73.6 239.3 %copy-start.181 = (f32[16,1,128]{2,1,0:T(1,128)}, f32[16,1,128]{2,1,0:T(1,128)S(1)}, u32[]{:S(2)}) copy-start(f32[16,1,128]{2,1,0:T(1,128)S(1)} %convert_element_type.297) | copy-start | bytes 24580
  178.9 9.9 collective-permute-start.2
  186.3 96.9 %collective-permute-start = (bf16[3,2048]{1,0:T(4,128)(2,1)S(1)}, bf16[3,2048]{1,0:T(4,128)(2,1)S(1)}, u32[]{:S(2)}, u32[]{:S(2)}) collective-permute-start(bf16[3,2048]{1,0:T(4,128)(2,1)S(1)} %slice_bitcast_fusion.17), channel_id=1, source_target_pairs={{0,2},{2,4},{4,6},{6,8},{8,10},{10,12},{12,14},{14,16},{16,18},{18... | collective-permute-start | bytes 36872 | tf_op jit(solution)/shard_map/ppermute | solution.py:16
  290.8 1020.8 %all-gather.41.cloned.1.call-start = ((), (), s32[]{:S(2)}) async-start(), calls=%async_computation.22 | async-start | bytes 2228224 | tf_op jit(solution)/shard_map/all_gather | solution.py:21
  554.6 757.0 %all-gather.43.cloned.1.call-start = ((), (), s32[]{:S(2)}) async-start(), calls=%async_computation.23 | async-start | bytes 2228224 | tf_op jit(solution)/shard_map/all_gather | solution.py:21
  555.5 773.8 %all-gather.33.cloned.1.call-start = ((), (), s32[]{:S(2)}) async-start(), calls=%async_computation.18 | async-start | bytes 2228224 | tf_op jit(solution)/shard_map/all_gather | solution.py:21
  556.0 237.7 %copy-start.182 = (f32[16,1,128]{2,1,0:T(1,128)S(1)}, f32[16,1,128]{2,1,0:T(1,128)}, u32[]{:S(2)}) copy-start(f32[16,1,128]{2,1,0:T(1,128)} %copy-done.181) | copy-start | bytes 24580
  791.5 537.8 %all-gather.35.cloned.1.call-start = ((), (), s32[]{:S(2)}) async-start(), calls=%async_computation.19 | async-start | bytes 2228224 | tf_op jit(solution)/shard_map/all_gather | solution.py:21
  797.5 2677.7 %all-gather.45.cloned.1.call-start = ((), (), s32[]{:S(2)}) async-start(), calls=%async_computation.24 | async-start | bytes 2228224 | tf_op jit(solution)/shard_map/all_gather | solution.py:21
  1042.9 2432.3 %all-gather.47.cloned.1.call-start = ((), (), s32[]{:S(2)}) async-start(), calls=%async_computation.25 | async-start | bytes 2228224 | tf_op jit(solution)/shard_map/all_gather | solution.py:21
  1043.7 2449.1 %all-gather.37.cloned.1.call-start = ((), (), s32[]{:S(2)}) async-start(), calls=%async_computation.20 | async-start | bytes 2228224 | tf_op jit(solution)/shard_map/all_gather | solution.py:21
  1043.7 242.8 %copy-start.217 = (bf16[128]{0:T(256)(128)(2,1)S(1)}, bf16[128]{0:T(256)(128)(2,1)}, u32[]{:S(2)}) copy-start(bf16[128]{0:T(256)(128)(2,1)} %param.48) | copy-start | bytes 772
  1286.5 2206.4 %all-gather.39.cloned.1.call-start = ((), (), s32[]{:S(2)}) async-start(), calls=%async_computation.21 | async-start | bytes 2228224 | tf_op jit(solution)/shard_map/all_gather | solution.py:21
  1311.6 4443.7 %reduce-scatter.31.cloned.1.call-start = ((), (), s32[]{:S(2)}) async-start(), calls=%async_computation.31 | async-start | bytes 1114112
  1974.3 1500.9 %copy-start.86 = (f32[16,2048]{1,0:T(8,128)S(1)}, f32[16,2048]{1,0:T(8,128)}, u32[]{:S(2)}) copy-start(f32[16,2048]{1,0:T(8,128)} %custom-call.11) | copy-start | bytes 393220
  5643.9 7.0 collective-permute-start.3
  5650.9 105.9 %reduce-scatter.17.cloned.1.call-start = ((), (), s32[]{:S(2)}) async-start(), calls=%async_computation.16 | async-start | bytes 1572864 | tf_op jit(solution)/shard_map/reduce_scatter | solution.py:387
  5665.9 90.8 %reduce-scatter.19.cloned.1.call-start = ((), (), s32[]{:S(2)}) async-start(), calls=%async_computation.17 | async-start | bytes 1572864 | tf_op jit(solution)/shard_map/reduce_scatter | solution.py:387
  5667.1 3.8 collective-permute-start.4
  5683.8 142.2 %reduce-scatter.13.cloned.1.call-start = ((), (), s32[]{:S(2)}) async-start(), calls=%async_computation.13 | async-start | bytes 1572864 | tf_op jit(solution)/shard_map/reduce_scatter | solution.py:284
  5689.6 136.4 %reduce-scatter.15.cloned.1.call-start = ((), (), s32[]{:S(2)}) async-start(), calls=%async_computation.14 | async-start | bytes 1572864 | tf_op jit(solution)/shard_map/reduce_scatter | solution.py:284
  5695.4 438.6 %reduce-scatter.21.cloned.1.call-start = ((), (), s32[]{:S(2)}) async-start(), calls=%async_computation.26 | async-start | bytes 35651584 | tf_op jit(solution)/shard_map/reduce_scatter | solution.py:409
  5732.4 457.0 %reduce-scatter.27.cloned.1.call-start = ((), (), s32[]{:S(2)}) async-start(), calls=%async_computation.29 | async-start | bytes 139264 | tf_op jit(solution)/shard_map/reduce_scatter | solution.py:415
  5738.0 512.0 %reduce-scatter.25.cloned.1.call-start = ((), (), s32[]{:S(2)}) async-start(), calls=%async_computation.28 | async-start | bytes 1114112 | tf_op jit(solution)/shard_map/reduce_scatter | solution.py:413
  5740.6 571.4 %reduce-scatter.23.cloned.1.call-start = ((), (), s32[]{:S(2)}) async-start(), calls=%async_computation.27 | async-start | bytes 1392640 | tf_op jit(solution)/shard_map/reduce_scatter | solution.py:412
  5742.4 752.0 %reduce-scatter.29.cloned.1.call-start = ((), (), s32[]{:S(2)}) async-start(), calls=%async_computation.30 | async-start | bytes 17825792 | tf_op jit(solution)/shard_map/reduce_scatter | solution.py:417
  (1248 other events, 6905.0 us)
Sparse Core Ops, SparseCore 0:
  9.6 23.9 all-gather.24
  36.4 133.7 all-gather.26
  171.7 19.4 all-gather.30
  193.2 78.0 all-gather.28
  291.0 20.2 all-reduce.180
  554.8 41.2 all-gather.40
  598.2 40.1 all-gather.42
  791.6 41.2 all-gather.32
  835.1 40.1 all-gather.34
  1043.0 41.3 all-gather.44
  1086.5 40.1 all-gather.46
  1286.6 41.2 all-gather.36
  1330.0 40.1 all-gather.38
  5651.0 55.0 reduce-scatter.30
  5708.9 19.3 reduce-scatter.16
  5731.0 20.3 reduce-scatter.18
  5753.5 20.3 reduce-scatter.12
  5776.0 20.3 reduce-scatter.14
  5801.2 332.7 reduce-scatter.20
  6138.2 51.1 reduce-scatter.26
  6193.6 56.3 reduce-scatter.24
  6254.6 57.3 reduce-scatter.22
  6316.7 177.6 reduce-scatter.28
where the time goes:
time: 6570 us; the launch traced here: 6500 us
  local copies, waits for them, and re-layouts  3350 us (51%)
  other arithmetic  1950 us (30%)
  waiting for transfers between devices  777 us (12%)
  blocking collectives  236 us (4%)
  matrix products  135 us (2%)
    pad x512, local copies, waits for them, and re-layouts, advance(): lax.associative_scan(carry_join, (decay_rows, inflow), axis=0)  1570 us
    pad x320, local copies, waits for them, and re-layouts, reverse_pair(): lax.associative_scan(carry_join, (jnp.flip(decay_rows, 0), jnp.flip(decay...  967 us
    add x272, other arithmetic, carry_join(): return (earlier[0] * latter[0], latter[0] * earlier[1] + latter[1])  378 us
    add x288, other arithmetic, advance(): lax.associative_scan(carry_join, (decay_rows, inflow), axis=0)  352 us
    while x2320, local copies, waits for them, and re-layouts  313 us
    reduce_scatter x1, waiting for transfers between devices, local(): lax.psum_scatter(grad_in_w, 'dp', scatter_dimension=0, tiled=True)  304 us
    add x224, other arithmetic, reverse_pair(): lax.associative_scan(carry_join, (jnp.flip(decay_rows, 0), jnp.flip(decay...  286 us
    concatenate x256, other arithmetic, advance(): lax.associative_scan(carry_join, (decay_rows, inflow), axis=0)  251 us

commit v1 on v0

v1 whole, which is shorter than its diff:
```python
import functools

import jax
import jax.numpy as jnp
from jax import lax
from jax.experimental import pallas as pl
from jax.experimental.pallas import tpu as pltpu
from jax.sharding import PartitionSpec as P

NSTATE = 16
RANK = 128
LANES = 128
DP = "dp"
TENSOR = "tensor"
GROUP = 8
LOG2E = 1.4426950408889634


def fold(parts, masks):
    width = 1
    while len(parts) > 1:
        joined = []
        for first, second in zip(parts[0::2], parts[1::2]):
            mask = masks[width]
            joined.append(
                jnp.where(mask, first, second) + pltpu.roll(jnp.where(mask, second, first), width, 0)
            )
        parts = joined
        width *= 2
    return parts[0]


def fold_masks():
    row = lax.broadcasted_iota(jnp.int32, (GROUP, LANES), 0)
    return {width: (row & width) == 0 for width in (1, 2, 4)}


def halves(value):
    return value[:GROUP] + value[GROUP:]


def spread(row):
    return jnp.broadcast_to(row, (NSTATE, LANES))


def cols(k):
    return pl.ds(k * LANES, LANES)


def forward_end_kernel(step_ref, flow_ref, b_ref, rate_ref, end_ref):
    groups, unused, width = step_ref.shape
    tiles = width // LANES
    rates = [rate_ref[:, cols(k)] for k in range(tiles)]

    def body(group, states):
        states = list(states)
        for j in range(GROUP):
            t = group * GROUP + j
            b_now = b_ref[t, :NSTATE, :]
            for k in range(tiles):
                decay = jnp.exp2(rates[k] * spread(step_ref[group, j : j + 1, cols(k)]))
                states[k] = decay * states[k] + b_now * spread(flow_ref[group, j : j + 1, cols(k)])
        return tuple(states)

    start = tuple(jnp.zeros((NSTATE, LANES), jnp.float32) for _ in range(tiles))
    ends = lax.fori_loop(0, groups, body, start)
    for k in range(tiles):
        end_ref[:, cols(k)] = ends[k]


def reverse_end_kernel(step_ref, grad_ref, c_ref, rate_ref, end_ref):
    groups, unused, width = step_ref.shape
    tiles = width // LANES
    rates = [rate_ref[:, cols(k)] for k in range(tiles)]

    def body(lap, states):
        states = list(states)
        group = groups - 1 - lap
        for j in reversed(range(GROUP)):
            t = group * GROUP + j
            c_now = c_ref[t, NSTATE:, :]
            for k in range(tiles):
                decay = jnp.exp2(rates[k] * spread(step_ref[group, j : j + 1, cols(k)]))
                states[k] = decay * (states[k] + c_now * spread(grad_ref[group, j : j + 1, cols(k)]))
        return tuple(states)

    start = tuple(jnp.zeros((NSTATE, LANES), jnp.float32) for _ in range(tiles))
    ends = lax.fori_loop(0, groups, body, start)
    for k in range(tiles):
        end_ref[:, cols(k)] = ends[k]


def forward_kernel(step_ref, flow_ref, bc_ref, rate_ref, enter_ref, out_ref):
    groups, unused, width = step_ref.shape
    tiles = width // LANES
    rates = [rate_ref[:, cols(k)] for k in range(tiles)]
    masks = fold_masks()

    def body(group, states):
        states = list(states)
        parts = [[] for _ in range(tiles)]
        for j in range(GROUP):
            t = group * GROUP + j
            b_now, c_now = bc_ref[t, :NSTATE, :], bc_ref[t, NSTATE:, :]
            for k in range(tiles):
                decay = jnp.exp2(rates[k] * spread(step_ref[group, j : j + 1, cols(k)]))
                states[k] = decay * states[k] + b_now * spread(flow_ref[group, j : j + 1, cols(k)])
                parts[k].append(halves(states[k] * c_now))
        for k in range(tiles):
            out_ref[group, :, cols(k)] = fold(parts[k], masks)
        return tuple(states)

    start = tuple(enter_ref[:, cols(k)] for k in range(tiles))
    lax.fori_loop(0, groups, body, start)


def reverse_kernel(
    held,
    step_ref,
    delta_ref,
    flow_ref,
    conv_ref,
    grad_ref,
    bc_ref,
    rate_ref,
    a_ref,
    enter_ref,
    leave_ref,
    *refs,
):
    gdelta_ref, gconv_ref, gbc_ref, ga_ref, decay_scr, state_scr = refs[held:]
    groups, unused, width = step_ref.shape
    tiles = width // LANES
    rates = [rate_ref[:, cols(k)] for k in range(tiles)]
    masks = fold_masks()

    def ahead(group, states):
        states = list(states)
        for j in range(GROUP):
            t = group * GROUP + j
            b_now = bc_ref[t, :NSTATE, :]
            for k in range(tiles):
                decay = jnp.exp2(rates[k] * spread(step_ref[group, j : j + 1, cols(k)]))
                state_scr[t, :, cols(k)] = states[k]
                decay_scr[t, :, cols(k)] = decay
                states[k] = decay * states[k] + b_now * spread(flow_ref[group, j : j + 1, cols(k)])
        return tuple(states)

    start = tuple(enter_ref[:, cols(k)] for k in range(tiles))
    ends = lax.fori_loop(0, groups, ahead, start)
    for k in range(tiles):
        state_scr[groups * GROUP, :, cols(k)] = ends[k]

    @pl.when(pl.program_id(0) == 0)
    def clear():
        gbc_ref[...] = jnp.zeros_like(gbc_ref)

    def back(lap, carried):
        carried, totals = list(carried[0]), list(carried[1])
        group = groups - 1 - lap
        inputs = [[] for _ in range(tiles)]
        drifts = [[] for _ in range(tiles)]
        for j in reversed(range(GROUP)):
            t = group * GROUP + j
            b_now, c_now = bc_ref[t, :NSTATE, :], bc_ref[t, NSTATE:, :]
            sum_b = sum_c = None
            for k in range(tiles):
                grad = spread(grad_ref[group, j : j + 1, cols(k)])
                flow = spread(flow_ref[group, j : j + 1, cols(k)])
                step = spread(delta_ref[group, j : j + 1, cols(k)])
                state_grad = carried[k] + grad * c_now
                inputs[k].insert(0, halves(state_grad * b_now))
                term_b = state_grad * flow
                term_c = state_scr[t + 1, :, cols(k)] * grad
                sum_b = term_b if sum_b is None else sum_b + term_b
                sum_c = term_c if sum_c is None else sum_c + term_c
                carried[k] = decay_scr[t, :, cols(k)] * state_grad
                term = carried[k] * state_scr[t, :, cols(k)]
                drifts[k].insert(0, halves(term * a_ref[:, cols(k)]))
                totals[k] = totals[k] + term * step
            gbc_ref[t, :NSTATE, :] = gbc_ref[t, :NSTATE, :] + sum_b
            gbc_ref[t, NSTATE:, :] = gbc_ref[t, NSTATE:, :] + sum_c
        for k in range(tiles):
            entry = fold(inputs[k], masks)
            gdelta_ref[group, :, cols(k)] = fold(drifts[k], masks) + entry * conv_ref[group, :, cols(k)]
            gconv_ref[group, :, cols(k)] = entry * delta_ref[group, :, cols(k)]
        return (tuple(carried), tuple(totals))

    start = tuple(leave_ref[:, cols(k)] for k in range(tiles))
    zeros = tuple(jnp.zeros((NSTATE, LANES), jnp.float32) for _ in range(tiles))
    unused, totals = lax.fori_loop(0, groups, back, (start, zeros))
    for k in range(tiles):
        ga_ref[:, cols(k)] = totals[k]


def row_spec(rows, width):
    return pl.BlockSpec((None, rows // GROUP, GROUP, width), lambda s, c: (s, 0, 0, c))


def grouped(*arrays):
    return tuple(a.reshape(a.shape[0], -1, GROUP, a.shape[-1]) for a in arrays)


def bc_spec(rows):
    return pl.BlockSpec((None, rows, 2 * NSTATE, LANES), lambda s, c: (s, 0, 0, 0))


def rate_spec(width):
    return pl.BlockSpec((NSTATE, width), lambda s, c: (0, c))


def state_spec(width):
    return pl.BlockSpec((None, NSTATE, width), lambda s, c: (s, 0, c))


def f32(*shape):
    return jax.ShapeDtypeStruct(shape, jnp.float32)


def limits(mb):
    return pltpu.CompilerParams(vmem_limit_bytes=mb * 2**20)


def forward_end(step, flow, bc, rate, width):
    seqs, rows, channels = step.shape
    return pl.pallas_call(
        forward_end_kernel,
        grid=(seqs, channels // width),
        in_specs=[row_spec(rows, width)] * 2 + [bc_spec(rows), rate_spec(width)],
        out_specs=state_spec(width),
        out_shape=f32(seqs, NSTATE, channels),
        compiler_params=limits(40),
        name="forward_end",
    )(*grouped(step, flow), bc, rate)


def reverse_end(step, grad, bc, rate, width):
    seqs, rows, channels = step.shape
    return pl.pallas_call(
        reverse_end_kernel,
        grid=(seqs, channels // width),
        in_specs=[row_spec(rows, width)] * 2 + [bc_spec(rows), rate_spec(width)],
        out_specs=state_spec(width),
        out_shape=f32(seqs, NSTATE, channels),
        compiler_params=limits(40),
        name="reverse_end",
    )(*grouped(step, grad), bc, rate)


def forward_main(step, flow, bc, rate, enter, width):
    seqs, rows, channels = step.shape
    return pl.pallas_call(
        forward_kernel,
        grid=(seqs, channels // width),
        in_specs=[row_spec(rows, width)] * 2 + [bc_spec(rows), rate_spec(width), state_spec(width)],
        out_specs=row_spec(rows, width),
        out_shape=f32(seqs, rows // GROUP, GROUP, channels),
        compiler_params=limits(40),
        name="forward_main",
    )(*grouped(step, flow), bc, rate, enter).reshape(step.shape)


def reverse_main(step, delta, flow, conv, grad, bc, rate, a_mat, enter, leave, width, seq, into=()):
    seqs, rows, channels = step.shape

    def of_seq(*block):
        return pl.BlockSpec((None,) + block, lambda c: (seq,) + (0,) * (len(block) - 1) + (c,))

    row = of_seq(rows // GROUP, GROUP, width)
    state = of_seq(NSTATE, width)
    pairs = pl.BlockSpec((None, rows, 2 * NSTATE, LANES), lambda c: (seq, 0, 0, 0))
    rates = pl.BlockSpec((NSTATE, width), lambda c: (0, c))
    return pl.pallas_call(
        functools.partial(reverse_kernel, len(into)),
        grid=(channels // width,),
        in_specs=[row] * 5
        + [pairs, rates, rates, state, state]
        + [pl.BlockSpec(memory_space=pl.ANY)] * len(into),
        out_specs=[row, row, pairs, state],
        out_shape=[f32(seqs, rows // GROUP, GROUP, channels)] * 2
        + [f32(seqs, rows, 2 * NSTATE, LANES), f32(seqs, NSTATE, channels)],
        input_output_aliases={10 + n: n for n in range(len(into))},
        scratch_shapes=[
            pltpu.VMEM((rows, NSTATE, width), jnp.float32),
            pltpu.VMEM((rows + 1, NSTATE, width), jnp.float32),
        ],
        compiler_params=limits(56),
        name="reverse_main",
    )(*grouped(step, delta, flow, conv, grad), bc, rate, a_mat, enter, leave, *into)


def place_of(piece):
    width = LANES
    return pl.ds(pl.multiple_of((lax.axis_index(DP) ^ piece) * width, width), width)


def piece_spec(n, width, piece=0):
    if n is None:
        return pl.BlockSpec((LANES, width), lambda j: (lax.axis_index(DP) ^ piece, j))
    return pl.BlockSpec((LANES, width), lambda j: (n, j))


def up_kernel(x_ref, *refs):
    pieces, out_ref, x_scr = refs[:-2], refs[-2], refs[-1]

    @pl.when(pl.program_id(0) == 0)
    def order():
        for p in range(len(pieces)):
            x_scr[:, cols(p)] = x_ref[:, place_of(p)]

    weights = jnp.concatenate([ref[...] for ref in pieces], axis=0)
    out_ref[...] = jnp.dot(x_scr[...], weights, preferred_element_type=jnp.float32).astype(
        out_ref.dtype
    )


def up(x, pieces, kind, width=512):
    rows, features = x.shape
    channels = pieces[0][0].shape[1]
    return pl.pallas_call(
        up_kernel,
        grid=(channels // width,),
        in_specs=[pl.BlockSpec((rows, features), lambda j: (0, 0))]
        + [piece_spec(n, width) for unused, n in pieces],
        out_specs=pl.BlockSpec((rows, width), lambda j: (0, j)),
        out_shape=jax.ShapeDtypeStruct((rows, channels), kind),
        scratch_shapes=[pltpu.VMEM((rows, features), x.dtype)],
        compiler_params=limits(40),
        name="up",
    )(x, *[array for array, unused in pieces])


def down_kernel(groups, *refs):
    inputs, pieces = refs[:groups], refs[groups:-3]
    own_ref, other_ref, total = refs[-3:]
    count = len(pieces) // groups
    new = None
    for g, y_ref in enumerate(inputs):
        weights = jnp.concatenate([ref[...] for ref in pieces[g * count : (g + 1) * count]], axis=0)
        term = lax.dot_general(
            y_ref[...], weights, (((1,), (1,)), ((), ())), preferred_element_type=jnp.float32
        )
        new = term if new is None else new + term

    @pl.when(pl.program_id(0) == 0)
    def first():
        total[...] = new

    @pl.when(pl.program_id(0) > 0)
    def later():
        total[...] += new

    @pl.when(pl.program_id(0) == pl.num_programs(0) - 1)
    def last():
        half = count // 2
        mine = lax.axis_index(TENSOR) * half
        for r in range(half):
            own_ref[:, cols(r)] = total[:, place_of(mine + r)]
            other_ref[:, cols(r)] = total[:, place_of((half - mine) + r)].astype(other_ref.dtype)


def down(pairs, kind, width=512):
    rows, channels = pairs[0][0].shape
    count = len(pairs[0][1])
    features = count * LANES
    half = pl.BlockSpec((rows, features // 2), lambda j: (0, 0))
    return pl.pallas_call(
        functools.partial(down_kernel, len(pairs)),
        grid=(channels // width,),
        in_specs=[pl.BlockSpec((rows, width), lambda j: (0, j))] * len(pairs)
        + [
            piece_spec(n, width, piece)
            for unused, pieces in pairs
            for piece, (array, n) in enumerate(pieces)
        ],
        out_specs=[half, half],
        out_shape=[
            jax.ShapeDtypeStruct((rows, features // 2), jnp.float32),
            jax.ShapeDtypeStruct((rows, features // 2), kind),
        ],
        scratch_shapes=[pltpu.VMEM((rows, features), jnp.float32)],
        compiler_params=limits(48),
        name="down",
    )(*[y for y, unused in pairs], *[array for unused, pieces in pairs for array, n in pieces])


def outer_kernel(x_ref, y_ref, *refs):
    outs, x_scr = refs[:-1], refs[-1]

    @pl.when(pl.program_id(0) == 0)
    def order():
        for p in range(x_ref.shape[1] // LANES):
            part = x_ref[:, place_of(p)].astype(jnp.float32)
            x_scr[pl.ds(p * LANES, LANES), :] = part.T.astype(x_scr.dtype)

    product = jnp.dot(x_scr[...], y_ref[...], preferred_element_type=jnp.float32)
    for p in range(product.shape[0] // LANES):
        row = (0, 2, 1, 3)[p // len(outs)] * LANES
        part = product[p * LANES : (p + 1) * LANES]
        outs[p % len(outs)][row : row + LANES, :] = part.astype(outs[0].dtype)


def outer(x, y, width=512):
    rows, features = x.shape
    channels = y.shape[1]
    stacked = features // 4
    return pl.pallas_call(
        outer_kernel,
        grid=(channels // width,),
        in_specs=[
            pl.BlockSpec((rows, features), lambda j: (0, 0)),
            pl.BlockSpec((rows, width), lambda j: (0, j)),
        ],
        out_specs=[pl.BlockSpec((stacked, width), lambda j: (0, j))] * 4,
        out_shape=[jax.ShapeDtypeStruct((stacked, channels), jnp.bfloat16)] * 4,
        scratch_shapes=[pltpu.VMEM((features, rows), x.dtype)],
        compiler_params=limits(48),
        name="outer",
    )(x, y)


def assemble_kernel(blocks, extra_ref, proj_ref, rest_ref, dt_ref):
    depth = dt_ref.shape[0] // (dt_ref.shape[1] // LANES)
    proj_blocks = proj_ref.shape[0] // NSTATE
    odd = lax.rem(lax.axis_index(DP), 2) == 1
    for p in range(0, 16, 2):
        slot = (p >> 2) + (p & 2) * 2
        for core in range(2):
            here = place_of(p + core)
            for b in range(blocks):
                block = extra_ref[core, slot, :NSTATE, cols(b)]
                row = (b if b < proj_blocks else b - proj_blocks) * NSTATE
                if b < proj_blocks:
                    proj_ref[row : row + NSTATE, here] = block
                else:
                    rest_ref[row : row + NSTATE, here] = block.astype(jnp.float32)
        own = extra_ref[0, slot, NSTATE:, :].astype(jnp.float32)[:depth]
        other = extra_ref[1, slot, NSTATE:, :].astype(jnp.float32)[:depth]
        pair = jnp.concatenate(
            [jnp.where(odd, other, own), jnp.where(odd, own, other)], axis=0
        ).astype(dt_ref.dtype)
        first = (lax.axis_index(DP) ^ p) // 2
        dt_ref[pl.ds(pl.multiple_of(first * 2 * depth, 2 * depth), 2 * depth), :] = pair


def assemble(extra, proj_rows, rest_rows):
    channels = extra.shape[-1]
    return pl.pallas_call(
        functools.partial(assemble_kernel, (proj_rows + rest_rows) // NSTATE),
        out_shape=[
            jax.ShapeDtypeStruct((proj_rows, channels), extra.dtype),
            f32(rest_rows, channels),
            jax.ShapeDtypeStruct((RANK, channels), extra.dtype),
        ],
        compiler_params=limits(40),
        name="assemble",
    )(extra)


def deal_kernel(proj_ref, dt_ref, rest_ref, out_ref):
    count = out_ref.shape[0]
    bits = count.bit_length() - 1
    depth = dt_ref.shape[0] // count
    proj_rows = proj_ref.shape[0]
    rest_row = proj_rows + dt_ref.shape[0]
    for n in range(count):
        piece = sum(1 << (bits - 1 - b) for b in range(bits) if n >> b & 1)
        out_ref[n, :proj_rows, :] = proj_ref[:, place_of(piece)].astype(out_ref.dtype)
        out_ref[n, rest_row:, :] = rest_ref[:, place_of(piece)].astype(out_ref.dtype)
        place = pl.ds(pl.multiple_of((lax.axis_index(DP) ^ piece) * depth, depth), depth)
        for k in range(0, count, 2):
            both = jnp.concatenate([dt_ref[place, cols(k)], dt_ref[place, cols(k + 1)]], axis=0)
            row = proj_rows + k * depth
            out_ref[n, row : row + 2 * depth, :] = both.astype(out_ref.dtype)


def deal(proj, dt, rest):
    rows = proj.shape[0] + dt.shape[0] + rest.shape[0]
    return pl.pallas_call(
        deal_kernel,
        out_shape=jax.ShapeDtypeStruct((proj.shape[1] // LANES, rows, LANES), jnp.bfloat16),
        compiler_params=limits(40),
        name="deal",
    )(proj, dt, rest)


EPSILON = 1e-05
RESET = 1e30


def shifted(block, axis, distance):
    devices = range(lax.axis_size(axis))
    route = [(i - distance, i) for i in devices if i - distance in devices]
    return lax.ppermute(block, axis, route)


def swapped(block, axis):
    return lax.ppermute(block, axis, [(0, 1), (1, 0)])


def exchanged(block, mask):
    return lax.ppermute(block, DP, [(i, i ^ mask) for i in range(lax.axis_size(DP))])


def after(block, *earlier):
    return lax.optimization_barrier((block, *earlier))[0] if earlier else block


def sent(block, mask, name, *earlier):
    with jax.named_scope(f"{name}_to_{mask}"):
        return exchanged(after(block, *earlier), mask)


def round_masks():
    return [1 << n for n in range(lax.axis_size(DP).bit_length() - 1)]


def total(*blocks):
    result = blocks[0].astype(jnp.float32)
    for block in blocks[1:]:
        result = result + block.astype(jnp.float32)
    return result


def silu_slope(values):
    squash = jax.nn.sigmoid(values)
    return squash * (1.0 + values * (1.0 - squash))


def dot(left, right, dims):
    return lax.dot_general(left, right, (dims, ((), ())), preferred_element_type=jnp.float32)


def joined(block, axis):
    if lax.axis_size(axis) != 2:
        return lax.all_gather(block, axis, axis=block.ndim - 1, tiled=True)
    other = swapped(block, axis)
    first = lax.axis_index(axis) == 0
    return jnp.concatenate(
        [jnp.where(first, block, other), jnp.where(first, other, block)], axis=-1
    )


def summed(block, axis):
    if lax.axis_size(axis) != 2:
        return lax.psum(block, axis)
    return block + swapped(block, axis)


def sum_scattered(block, axis):
    last = block.ndim - 1
    if lax.axis_size(axis) != 2:
        return lax.psum_scatter(block, axis, scatter_dimension=last, tiled=True)
    width = block.shape[-1] // 2
    place = lax.axis_index(axis)
    own = lax.dynamic_slice_in_dim(block, place * width, width, last)
    other = lax.dynamic_slice_in_dim(block, (1 - place) * width, width, last)
    return own + swapped(other, axis)


def entering(value, span, rate, axis, direction):
    value = shifted(value, axis, direction)
    span = shifted(span, axis, direction)
    distance = 1
    while distance < lax.axis_size(axis):
        further = shifted(value, axis, direction * distance)
        further_span = shifted(span, axis, direction * distance)
        value = value + jnp.exp2(rate[None] * span[:, None, :]) * further
        span = span + further_span
        distance *= 2
    return value


def local_whole(
    tokens, segments, cotangent, norm_gain, w_in, conv_w, conv_b, w_x, w_dt, dt_bias, a_log, d_skip, w_out
):
    seqs, rows, part = tokens.shape
    features, channels = part * lax.axis_size(TENSOR), w_in.shape[2]
    devices = lax.axis_size(DP)
    shard = channels // devices
    taps = conv_w.shape[0]
    reach = taps - 1
    block = min(512, channels)
    count = seqs * rows
    low = jnp.bfloat16

    small = jnp.concatenate(
        [
            conv_w,
            conv_b[None],
            dt_bias[None],
            d_skip[None],
            a_log.T,
            w_x.T,
            w_dt.reshape(-1, shard),
            norm_gain.reshape(-1, shard),
        ],
        axis=0,
    )
    small = lax.all_gather(small, DP)
    w_in_x = lax.all_gather(w_in[:, 0], DP, axis=0, tiled=True)
    w_in_gate = lax.all_gather(w_in[:, 1], DP, axis=0, tiled=True)
    w_out_t = lax.all_gather(w_out.T, DP, axis=0, tiled=True)
    channel_rows = taps + 3 + NSTATE + w_x.shape[1]
    by_channel = small[:, :channel_rows].transpose(1, 0, 2).reshape(channel_rows, channels)
    taps_f = by_channel[:taps].astype(jnp.float32)
    bias_f, shift_f, skip_f = (by_channel[taps + i].astype(jnp.float32)[None] for i in range(3))
    a_mat = -jnp.exp(by_channel[taps + 3 : taps + 3 + NSTATE].astype(jnp.float32))
    rate = a_mat * LOG2E
    w_x_t = by_channel[taps + 3 + NSTATE :]
    dt_full = small[:, channel_rows : channel_rows + RANK].reshape(RANK, channels)
    gain_f = small[:, channel_rows + RANK :].reshape(features).astype(jnp.float32)

    marks_own = segments + 1
    marks_before = shifted(marks_own[:, rows - reach :], DP, 1)
    marks = jnp.concatenate([marks_before, marks_own], axis=1)
    tail = shifted(tokens[:, rows - reach :], DP, 1)
    wanted = jnp.concatenate(
        [tokens.reshape(count, part), tail.reshape(seqs * reach, part)], axis=0
    )
    x_rows = joined(wanted, TENSOR).astype(jnp.float32)
    cot = joined(cotangent.reshape(count, part), TENSOR)
    scale_all = lax.rsqrt(jnp.mean(x_rows * x_rows, axis=1, keepdims=True) + EPSILON)
    normed_all = (x_rows * scale_all * gain_f[None]).astype(low)
    normed, scale = normed_all[:count], scale_all[:count]

    inner_all = dot(normed_all, w_in_x, ((1,), (0,))).astype(low)
    inner_ext = jnp.concatenate(
        [
            inner_all[count:].reshape(seqs, reach, channels),
            inner_all[:count].reshape(seqs, rows, channels),
        ],
        axis=1,
    ).astype(jnp.float32)
    tap_masks = [
        (marks[:, k : k + rows] == marks_own).astype(jnp.float32)[:, :, None] for k in range(taps)
    ]
    mixed = bias_f[None]
    for k in range(taps):
        mixed = mixed + taps_f[k][None, None] * inner_ext[:, k : k + rows] * tap_masks[k]
    conv_low = jax.nn.silu(mixed).astype(low)
    conv = conv_low.astype(jnp.float32)
    conv_flat = conv_low.reshape(count, channels)
    proj = summed(dot(conv_flat, w_x_t, ((1,), (1,))), TENSOR)
    rank_part = proj[:, :RANK].astype(low)
    bc = jnp.broadcast_to(
        proj[:, RANK:].reshape(seqs, rows, 2 * NSTATE, 1), (seqs, rows, 2 * NSTATE, LANES)
    )
    pre = (dot(rank_part, dt_full, ((1,), (0,))) + shift_f).reshape(seqs, rows, channels)
    delta = jax.nn.softplus(pre)
    step = jnp.where(tap_masks[reach - 1] > 0, delta, RESET)
    flow = delta * conv
    span = jnp.sum(step, axis=1)

    end = forward_end(step, flow, bc, rate, block)
    enter = entering(end, span, rate, DP, 1)
    readout = forward_main(step, flow, bc, rate, enter, block)
    ssm = readout + skip_f[None] * conv

    gate = dot(normed, w_in_gate, ((1,), (0,))).reshape(seqs, rows, channels)
    silu_gate = jax.nn.silu(gate)
    gated = (ssm * silu_gate).astype(low).reshape(count, channels)
    branch = sum_scattered(dot(gated, w_out_t, ((1,), (1,))), TENSOR)
    tokens_f = tokens.reshape(count, part).astype(jnp.float32)
    block_out = (tokens_f + branch).astype(low).reshape(seqs, rows, part)
    grad_out_t = dot(cot, gated, ((0,), (0,))).astype(low)
    grad_out_t = lax.psum_scatter(grad_out_t, DP, scatter_dimension=0, tiled=True)
    grad_gated = dot(cot, w_out_t, ((1,), (0,))).reshape(seqs, rows, channels)
    grad_ssm = grad_gated * silu_gate
    grad_gate = (grad_gated * ssm * silu_slope(gate)).astype(low).reshape(count, channels)
    grad_in_gate = dot(normed, grad_gate, ((0,), (0,))).astype(low)
    grad_in_gate = lax.psum_scatter(grad_in_gate, DP, scatter_dimension=0, tiled=True)
    grad_skip = jnp.sum(grad_ssm * conv, axis=(0, 1))

    back_end = reverse_end(step, grad_ssm, bc, rate, block)
    leave = entering(back_end, span, rate, DP, -1)
    back = ()
    for n in range(seqs):
        back = reverse_main(
            step, delta, flow, conv, grad_ssm, bc, rate, a_mat, enter, leave, block, n, back
        )
    grad_delta, grad_conv_scan, grad_bc, grad_a = back
    grad_delta, grad_conv_scan = (part.reshape(step.shape) for part in (grad_delta, grad_conv_scan))
    grad_alog = jnp.sum(grad_a, axis=0) * a_mat
    grad_pre = grad_delta * jax.nn.sigmoid(pre)
    grad_shift = jnp.sum(grad_pre, axis=(0, 1))
    grad_pre_low = grad_pre.astype(low).reshape(count, channels)
    grad_dt = dot(rank_part, grad_pre_low, ((0,), (0,)))
    grad_rank = dot(grad_pre_low, dt_full, ((1,), (1,)))
    grad_proj = jnp.concatenate(
        [grad_rank, jnp.sum(grad_bc, axis=-1).reshape(count, 2 * NSTATE)], axis=1
    )
    grad_proj = summed(grad_proj, TENSOR).astype(low)
    grad_x_t = dot(grad_proj, conv_flat, ((0,), (0,)))
    grad_conv = (
        grad_conv_scan
        + skip_f[None] * grad_ssm
        + dot(grad_proj, w_x_t, ((1,), (0,))).reshape(seqs, rows, channels)
    )
    grad_mixed = grad_conv * silu_slope(mixed)
    grad_bias = jnp.sum(grad_mixed, axis=(0, 1))
    grad_taps = jnp.stack(
        [
            jnp.sum(grad_mixed * inner_ext[:, k : k + rows] * tap_masks[k], axis=(0, 1))
            for k in range(taps)
        ]
    )
    grad_ext = jnp.zeros((seqs, rows + reach, channels), jnp.float32)
    for k in range(taps):
        grad_ext = grad_ext + jnp.pad(
            taps_f[k][None, None] * grad_mixed * tap_masks[k], ((0, 0), (k, reach - k), (0, 0))
        )
    returned = shifted(grad_ext[:, :reach], DP, -1)
    grad_inner = grad_ext[:, reach:] + jnp.pad(returned, ((0, 0), (rows - reach, 0), (0, 0)))
    grad_inner = grad_inner.astype(low).reshape(count, channels)
    grad_in_x = dot(normed, grad_inner, ((0,), (0,))).astype(low)
    grad_in_x = lax.psum_scatter(grad_in_x, DP, scatter_dimension=0, tiled=True)

    grad_normed = sum_scattered(
        dot(grad_inner, w_in_x, ((1,), (1,))) + dot(grad_gate, w_in_gate, ((1,), (1,))), TENSOR
    )
    column = lax.axis_index(TENSOR) * part
    gain_local = lax.dynamic_slice_in_dim(gain_f, column, part, 0)
    weighted = grad_normed * gain_local[None]
    grad_gain = jnp.sum(grad_normed * tokens_f * scale, axis=0)
    grad_gain = lax.dynamic_update_slice_in_dim(
        jnp.zeros((features,), jnp.float32), grad_gain, column, 0
    )
    row_total = summed(jnp.sum(weighted * tokens_f, axis=1, keepdims=True), TENSOR)
    input_grad = (
        cotangent.reshape(count, part).astype(jnp.float32)
        + scale * weighted
        - tokens_f * (scale * scale * scale) * (row_total / features)
    ).reshape(seqs, rows, part)

    by_channel = jnp.concatenate(
        [grad_taps, grad_bias[None], grad_shift[None], grad_skip[None], grad_alog, grad_x_t], axis=0
    )
    by_channel = by_channel.reshape(channel_rows, devices, shard).transpose(1, 0, 2)
    packed = jnp.concatenate(
        [
            by_channel,
            grad_dt.reshape(devices, RANK, shard),
            grad_gain.reshape(devices, -1, shard),
        ],
        axis=1,
    )
    packed = lax.psum_scatter(packed, DP, scatter_dimension=0)
    by_channel = packed[:channel_rows]
    grad_dt = packed[channel_rows : channel_rows + RANK].reshape(-1, channels)
    grad_gain = summed(packed[channel_rows + RANK :], TENSOR).reshape(-1)
    grad_in = jnp.stack([grad_in_x, grad_in_gate], axis=1).astype(jnp.float32)
    return (
        block_out,
        input_grad,
        grad_gain,
        grad_in,
        by_channel[:taps],
        by_channel[taps],
        by_channel[taps + 3 + NSTATE :].T,
        grad_dt,
        by_channel[taps + 1],
        by_channel[taps + 3 : taps + 3 + NSTATE].T,
        by_channel[taps + 2],
        grad_out_t.astype(jnp.float32).T,
    )


class Names:
    def __getattr__(self, name):
        return name


N = Names()


class Plan:
    def __init__(self, waits):
        self.waits, self.steps, self.values, self.open = waits, {}, {}, set()

    def add(self, name, step):
        self.steps[name] = step

    def get(self, name):
        if name not in self.values:
            if name in self.open:
                raise ValueError(f"cycle at {name}")
            self.open.add(name)
            self.values[name] = self.steps[name]()
            self.open.remove(name)
        return self.values[name]

    def first(self, name):
        value = self.get(name)
        return value[0] if isinstance(value, (tuple, list)) else value

    def tied(self, name, block):
        return after(block, *(self.first(other) for other in self.waits.get(name, ())))

    def send(self, name, block, mask):
        def step():
            with jax.named_scope(name):
                return exchanged(self.tied(name, block()), mask)

        self.add(name, step)

    def swap(self, name, block):
        def step():
            with jax.named_scope(name):
                return swapped(self.tied(name, block()), TENSOR)

        self.add(name, step)


def gather_steps(plan, chunk, shard, groups, rows):
    places = {}

    def block(pieces):
        parts = []
        for n, piece in enumerate(pieces):
            name, row = places[piece]
            array = plan.get(name) if name else shard()
            part = array[row * LANES : row * LANES + rows] if array.shape[0] != rows else array
            parts.append(part)
        return parts[0] if len(parts) == 1 else jnp.concatenate(parts, axis=0)

    def move(name, pieces, mask):
        def start():
            return block(pieces)

        plan.send(name, start, mask)
        for n, piece in enumerate(pieces):
            places[piece + mask] = (name, n)

    places[0] = (None, 0)
    move(f"{chunk}4", (0,), 4)
    move(f"{chunk}8", (0,), 8)
    move(f"{chunk}12", (8,), 4)
    for group in groups:
        move(f"{chunk}x{group[0]}", group, 2)

    def core(name, pieces):
        first, *others = (block((p,))[:LANES] for p in pieces)
        return jnp.concatenate([plan.tied(name, first), *others], axis=0)

    for x in (0, 2):
        name, pieces = f"{chunk}s{x}", [z + x for z in (0, 4, 8, 12)]
        plan.send(name, lambda name=name, pieces=pieces: core(name, pieces), 1)
        for n, piece in enumerate(pieces):
            places[piece + 1] = (name, n)

    def pieces():
        return [(plan.get(places[p][0]) if places[p][0] else shard(), places[p][1]) for p in range(16)]

    def extra():
        return jnp.stack([block((p,))[LANES:] for p in (0, 4, 8, 12, 2, 6, 10, 14)])

    plan.add(chunk, pieces)
    if rows > LANES:
        plan.add(f"{chunk}own", extra)
        plan.send(f"{chunk}e", lambda: plan.get(f"{chunk}own"), 1)


ROWS = {0: 0, 8: 1, 4: 2, 12: 3}


def scatter_steps(plan, name, outer_name, groups, near_groups):
    crossed, neared = {}, {}

    def rows_of(group):
        first = ROWS[group[0]]
        return slice(first * LANES, (first + len(group)) * LANES)

    def chip(x, group):
        return [plan.get(outer_name)[x][rows_of(group)], plan.get(f"{name}s{x}")[rows_of(group)]]

    def pick(table, z):
        step, n = table[z]
        return plan.get(step)[n * LANES : (n + 1) * LANES]

    for x in (2, 0):
        plan.send(f"{name}s{x}", lambda x=x: plan.get(outer_name)[x + 1], 1)
    for group in groups:
        ready, step = f"{name}p{group[0]}", f"{name}x{group[0]}"
        plan.add(ready, lambda group=group: total(*chip(2, group)).astype(jnp.bfloat16))
        plan.send(step, lambda ready=ready: plan.get(ready), 2)
        for n, z in enumerate(group):
            crossed[z] = (step, n)

    def column(group):
        parts = [
            total(*chip(0, (z,)), pick(crossed, z), *([pick(neared, z)] if z == 8 else [])) for z in group
        ]
        return jnp.concatenate(parts, axis=0).astype(jnp.bfloat16)

    for group in near_groups:
        step = f"{name}z{group[0]}"
        plan.send(step, lambda group=group: column(group), 4)
        for n, z in enumerate(group):
            neared[z - 4] = (step, n)
    plan.send(f"{name}z8", lambda: column((8,)), 8)

    def result():
        last = plan.tied(name, plan.get(f"{name}z8"))
        return total(last, pick(neared, 0), pick(crossed, 0), *chip(0, (0,)))

    plan.add(name, result)


def state_steps(plan, name, value, span, rate, known=None):
    low = jnp.bfloat16

    def message(n):
        mask = round_masks()[n]
        lower = lax.rem(lax.div(lax.axis_index(DP), mask), 2) == 0
        now = plan.get(f"{name}in{n}")
        got = plan.get(f"{name}{n}")
        other = got[:, :NSTATE].astype(jnp.float32)
        own_span, other_span, before, behind = plan.get(f"{known or name}spans{n}")
        first = ~lower if known else lower
        far = jnp.where(first, 0.0, other)
        decay = lambda steps: jnp.exp2(rate()[None] * steps[:, None, :])
        result = far if n == 0 else now[1] + decay(behind if known else before) * far
        through = jnp.where(first, other_span, own_span)
        value = jnp.where(first, other, now[0]) + decay(through) * jnp.where(first, now[0], other)
        return value, result

    def spans(n):
        if n == 0:
            own, before, behind = span(), jnp.zeros_like(span()), jnp.zeros_like(span())
        else:
            own, other, before, behind = plan.get(f"{name}spans{n - 1}")
            lower = lax.rem(lax.div(lax.axis_index(DP), round_masks()[n - 1]), 2) == 0
            before = before + jnp.where(lower, 0.0, other)
            behind = behind + jnp.where(lower, other, 0.0)
            own = own + other
        with jax.named_scope(f"{name}span{n}"):
            other = exchanged(plan.tied(f"{name}span{n}", own), round_masks()[n])
        return own, other, before, behind

    count = len(round_masks())
    for n in range(count):
        plan.add(f"{name}in{n}", lambda n=n: message(n - 1) if n else (value(), None))
        plan.send(f"{name}{n}", lambda n=n: plan.get(f"{name}in{n}")[0].astype(low), round_masks()[n])
        if not known:
            plan.add(f"{name}spans{n}", lambda n=n: spans(n))
    plan.add(name, lambda: message(count - 1)[1])


def pack_steps(plan, name, blocks):
    def sums(n):
        if n == 0:
            return blocks()
        before = sums_of(n - 1)
        half = before.shape[0] // 2
        return before[:half].astype(jnp.float32) + plan.get(f"{name}{n - 1}").astype(jnp.float32)

    def sums_of(n):
        return plan.get(f"{name}sum{n}")

    def sent_half(n):
        block = sums_of(n)
        return block[block.shape[0] // 2 :].astype(jnp.bfloat16)

    for n in range(len(round_masks()) + 1):
        plan.add(f"{name}sum{n}", lambda n=n: sums(n))
    for n, mask in enumerate(round_masks()):
        plan.send(f"{name}{n}", lambda n=n: sent_half(n), mask)
    plan.add(name, lambda: sums_of(len(round_masks()))[0])


WAITS = dict(
    a12=(N.a4, N.a8, N.ax0, N.bx0),
    ax4=(N.a4, N.a8, N.ax0, N.bx0),
    ax8=(N.a4, N.a8, N.ax0, N.bx0),
    b4=(N.a12,),
    b8=(N.a12,),
    ax12=(N.ax4, N.ax8, N.a12),
    as0=(N.ax4, N.ax8, N.a12),
    as2=(N.b4, N.b8),
    bx4=(N.as0, N.as2, N.ae),
    bx8=(N.inner, N.ax12),
    b12=(N.inner, N.ax12),
    bx12=(N.inner, N.bx4),
    bs0=(N.inner,),
    end=(N.bx8,),
    f1=(N.bx12,),
    gate=(N.f0,),
    readout=(N.gate,),
    outB=(N.r0,),
    branch=(N.outB,),
    back0=(N.branch,),
    taps=(N.grad_normed,),
    c=(N.inner,),
    grad_gated=(N.outC,),
    back1=(N.Bx4,),
    grad_pre=(N.Bx0,),
    grad_mixed=(N.Bz4,),
    Bz8=(N.Ap4,),
    down=(N.Ap4,),
    Ax0=(N.Ap4,),
    yn=(N.Ax4, N.Bz8),
    y0=(N.ax0,),
)
GROUPS = dict(
    a=((0,), (4,), (8,), (12,)),
    b=((0,), (4,), (8,), (12,)),
    c=(),
    C=(),
    B=((4, 12), (0, 8)),
    A=((4, 12), (0, 8)),
    Cz=(),
    Bz=((4, 12),),
    Az=((12,), (4,)),
)


def local(
    tokens, segments, cotangent, norm_gain, w_in, conv_w, conv_b, w_x, w_dt, dt_bias, a_log, d_skip, w_out
):
    seqs, rows, part = tokens.shape
    features, channels = part * 2, w_in.shape[2]
    devices = lax.axis_size(DP)
    shard = channels // devices
    taps = conv_w.shape[0]
    reach = taps - 1
    block = min(512, channels)
    count = seqs * rows
    low = jnp.bfloat16
    plan = Plan(WAITS)
    get, add, tied = plan.get, plan.add, plan.tied
    first_half = lax.axis_index(TENSOR) == 0

    def natural(own, other):
        return jnp.concatenate(
            [jnp.where(first_half, own, other), jnp.where(first_half, other, own)], axis=-1
        )

    def up_any(x, weights):
        if isinstance(weights, list):
            return up(x, weights, jnp.float32)
        return dot(x, weights, ((1,), (0,)))

    def pieces_of(weights):
        return weights if isinstance(weights, list) else [(weights, None)] * devices

    proj_rows = w_x.shape[1]
    small = jnp.concatenate(
        [
            w_x.T,
            a_log.T,
            conv_w,
            conv_b[None],
            dt_bias[None],
            d_skip[None],
            norm_gain.reshape(-1, shard),
        ],
        axis=0,
    )
    rest_rows = small.shape[0] - proj_rows
    rest_rows += -rest_rows % NSTATE
    small = jnp.pad(small, ((0, channels // LANES * NSTATE - small.shape[0]), (0, 0)))
    small = small.reshape(-1, NSTATE, LANES).transpose(1, 0, 2).reshape(NSTATE, channels)
    steps = jnp.pad(w_dt, ((0, NSTATE - w_dt.shape[0]), (0, 0)))
    shard_x = jnp.concatenate([w_in[:, 0], small, steps], axis=0)
    shard_gate, shard_out = w_in[:, 1], w_out.T
    gather_steps(plan, N.a, lambda: shard_x, GROUPS[N.a], shard_x.shape[0])
    for name, held in ((N.b, shard_gate), (N.c, shard_out)):
        if GROUPS[name]:
            gather_steps(plan, name, lambda held=held: held, GROUPS[name], LANES)
        else:
            add(name, lambda name=name, held=held: lax.all_gather(tied(name, held), DP, axis=0, tiled=True))

    def small_weights():
        extra = jnp.stack([get(N.aown), get(N.ae)])
        w_x_t, rest, dt_full = assemble(tied(N.small, extra), proj_rows, rest_rows)
        a_mat = -jnp.exp(rest[:NSTATE])
        gain = rest[NSTATE + taps + 3]
        others = [rest[NSTATE + taps + i][None] for i in range(3)]
        return w_x_t, dt_full, a_mat, a_mat * LOG2E, rest[NSTATE : NSTATE + taps], gain, *others

    add(N.small, small_weights)

    marks_own = segments + 1
    marks_before = shifted(marks_own[:, rows - reach :], DP, 1)
    marks = jnp.concatenate([marks_before, marks_own], axis=1)
    tap_masks = [
        (marks[:, k : k + rows] == marks_own).astype(jnp.float32)[:, :, None] for k in range(taps)
    ]
    tail = shifted(tokens[:, rows - reach :], DP, 1)
    wanted = [cotangent.reshape(count, part), tokens.reshape(count, part)]
    wanted.append(tail.reshape(seqs * reach, part))
    wanted = jnp.concatenate(wanted, axis=0)
    wanted = jnp.pad(wanted, ((0, -wanted.shape[0] % 16), (0, 0)))
    tokens_f = tokens.reshape(count, part).astype(jnp.float32)
    plan.swap(N.y0, lambda: wanted)
    add(N.rows, lambda: natural(wanted, get(N.y0)))

    def normed():
        x_rows = get(N.rows)[count:].astype(jnp.float32)
        scale = lax.rsqrt(jnp.mean(x_rows * x_rows, axis=1, keepdims=True) + EPSILON)
        return (x_rows * scale * get(N.small)[5][None]).astype(low), scale

    add(N.normed, normed)
    add(N.cot, lambda: get(N.rows)[:count])

    add(N.inner, lambda: up(tied(N.inner, get(N.normed)[0]), get(N.a), low))

    def extended():
        inner = get(N.inner)
        before = inner[count : count + seqs * reach].reshape(seqs, reach, channels)
        now = inner[:count].reshape(seqs, rows, channels)
        return jnp.concatenate([before, now], axis=1).astype(jnp.float32)

    add(N.extended, extended)

    def mixed():
        taps_f, bias_f = get(N.small)[4], get(N.small)[6]
        result = bias_f[None]
        for k in range(taps):
            result = result + taps_f[k][None, None] * get(N.extended)[:, k : k + rows] * tap_masks[k]
        return result

    add(N.mixed, mixed)
    add(N.conv, lambda: jax.nn.silu(get(N.mixed)).astype(low))
    add(N.conv_flat, lambda: get(N.conv).reshape(count, channels))
    add(N.part, lambda: dot(get(N.conv_flat), get(N.small)[0], ((1,), (1,))))
    plan.swap(N.yp, lambda: get(N.part))
    add(N.proj, lambda: get(N.part) + get(N.yp))
    add(N.rank, lambda: get(N.proj)[:, :RANK].astype(low))

    def broadcast():
        columns = get(N.proj)[:, RANK:].reshape(seqs, rows, 2 * NSTATE, 1)
        return jnp.broadcast_to(columns, (seqs, rows, 2 * NSTATE, LANES))

    add(N.bc, broadcast)

    def pre():
        product = dot(get(N.rank), get(N.small)[1], ((1,), (0,)))
        return (product + get(N.small)[7]).reshape(seqs, rows, channels)

    add(N.pre, pre)
    add(N.delta, lambda: jax.nn.softplus(get(N.pre)))
    add(N.step, lambda: jnp.where(tap_masks[reach - 1] > 0, get(N.delta), RESET))
    add(N.flow, lambda: get(N.delta) * get(N.conv).astype(jnp.float32))
    add(N.span, lambda: jnp.sum(get(N.step), axis=1))

    def rate():
        return get(N.small)[3]

    add(N.end, lambda: forward_end(get(N.step), tied(N.end, get(N.flow)), get(N.bc), rate(), block))
    state_steps(plan, N.f, lambda: get(N.end), lambda: get(N.span), rate)
    add(N.enter, lambda: get(N.f))
    add(
        N.readout,
        lambda: forward_main(
            get(N.step), get(N.flow), get(N.bc), rate(), tied(N.readout, get(N.enter)), block
        ),
    )
    add(N.ssm, lambda: get(N.readout) + get(N.small)[8][None] * get(N.conv).astype(jnp.float32))

    def gate():
        own = tied(N.gate, get(N.normed)[0][:count])
        return up_any(own, get(N.b)).reshape(seqs, rows, channels)

    add(N.gate, gate)
    add(N.silu_gate, lambda: jax.nn.silu(get(N.gate)))
    add(N.gated, lambda: (get(N.ssm) * get(N.silu_gate)).astype(low).reshape(count, channels))
    def scatter(name, x, y, groups, near):
        if groups:
            add(f"out{name}", lambda: outer(x(), y()))
            scatter_steps(plan, name, f"out{name}", groups, near)
        else:
            add(f"out{name}", lambda: dot(x(), y(), ((0,), (0,))).astype(low))
            add(f"{name}rs", lambda: lax.psum_scatter(get(f"out{name}"), DP, scatter_dimension=0, tiled=True))
            add(name, lambda: tied(name, get(f"{name}rs")).astype(jnp.float32))

    scatter(N.C, lambda: get(N.cot), lambda: tied(N.outC, get(N.gated)), GROUPS[N.C], GROUPS[N.Cz])
    add(N.grad_gated, lambda: up_any(tied(N.grad_gated, get(N.cot)), get(N.c)))
    add(N.grad_gated3, lambda: get(N.grad_gated).reshape(seqs, rows, channels))
    add(N.grad_ssm, lambda: tied(N.grad_ssm, get(N.grad_gated3)) * get(N.silu_gate))

    def grad_gate():
        slope = silu_slope(get(N.gate))
        result = tied(N.grad_gate, get(N.grad_gated3)) * get(N.ssm) * slope
        return result.astype(low).reshape(count, channels)

    add(N.grad_gate, grad_gate)

    add(
        N.rend,
        lambda: reverse_end(get(N.step), tied(N.rend, get(N.grad_ssm)), get(N.bc), rate(), block),
    )
    state_steps(plan, N.r, lambda: get(N.rend), None, rate, N.f)
    scatter(N.B, lambda: get(N.normed)[0][:count], lambda: tied(N.outB, get(N.grad_gate)), GROUPS[N.B], GROUPS[N.Bz])
    add(N.branch, lambda: down([(tied(N.branch, get(N.gated)), pieces_of(get(N.c)))], low))
    plan.swap(N.yb, lambda: get(N.branch)[1])

    def back(n):
        into = get(f"back{n - 1}") if n else ()
        leave = tied(f"back{n}", get(N.r))
        inputs = [get(N.step), get(N.delta), get(N.flow)]
        inputs += [get(N.conv).astype(jnp.float32), get(N.grad_ssm), get(N.bc), rate()]
        inputs += [get(N.small)[2], get(N.enter), leave]
        return reverse_main(*inputs, block, n, into)

    for n in range(seqs):
        add(f"back{n}", lambda n=n: back(n))

    def back_all(n):
        result = get(f"back{seqs - 1}")[n]
        return result.reshape(seqs, rows, channels) if n < 2 else result

    add(N.grad_pre, lambda: tied(N.grad_pre, back_all(0)) * jax.nn.sigmoid(get(N.pre)))
    add(N.grad_pre_low, lambda: get(N.grad_pre).astype(low).reshape(count, channels))

    def proj_part():
        grad_rank = dot(get(N.grad_pre_low), get(N.small)[1], ((1,), (1,)))
        grad_bc = jnp.sum(back_all(2), axis=-1).reshape(count, 2 * NSTATE)
        return jnp.concatenate([grad_rank, grad_bc], axis=1)

    add(N.gpart, proj_part)
    plan.swap(N.yg, lambda: get(N.gpart))
    add(N.grad_proj, lambda: (get(N.gpart) + get(N.yg)).astype(low))

    def grad_mixed():
        product = dot(tied(N.grad_mixed, get(N.grad_proj)), get(N.small)[0], ((1,), (0,)))
        grad_conv = back_all(1) + get(N.small)[8][None] * get(N.grad_ssm)
        grad_conv = grad_conv + product.reshape(seqs, rows, channels)
        return grad_conv * silu_slope(get(N.mixed))

    add(N.grad_mixed, grad_mixed)

    def grad_ext():
        grads = tied(N.grad_ext, get(N.grad_mixed))
        result = jnp.zeros((seqs, rows + reach, channels), jnp.float32)
        for k in range(taps):
            term = get(N.small)[4][k][None, None] * grads * tap_masks[k]
            result = result + jnp.pad(term, ((0, 0), (k, reach - k), (0, 0)))
        return result

    add(N.grad_ext, grad_ext)
    add(N.returned, lambda: shifted(get(N.grad_ext)[:, :reach], DP, -1))

    def grad_inner():
        returned = jnp.pad(get(N.returned), ((0, 0), (rows - reach, 0), (0, 0)))
        result = get(N.grad_ext)[:, reach:] + returned
        return result.astype(low).reshape(count, channels)

    add(N.grad_inner, grad_inner)
    scatter(N.A, lambda: get(N.normed)[0][:count], lambda: tied(N.outA, get(N.grad_inner)), GROUPS[N.A], GROUPS[N.Az])

    def grad_rows():
        pairs = [(tied(N.down, get(N.grad_inner)), get(N.a)), (get(N.grad_gate), pieces_of(get(N.b)))]
        return down(pairs, low)

    add(N.down, grad_rows)
    plan.swap(N.yn, lambda: get(N.down)[1])
    add(N.grad_normed, lambda: tied(N.grad_normed, get(N.down)[0] + get(N.yn).astype(jnp.float32)))
    column = lax.axis_index(TENSOR) * part
    scale = get(N.normed)[1][:count]
    add(N.weighted, lambda: get(N.grad_normed) * lax.dynamic_slice_in_dim(get(N.small)[5], column, part, 0)[None])
    add(N.row_part, lambda: jnp.sum(get(N.weighted) * tokens_f, axis=1, keepdims=True))
    plan.swap(N.yt, lambda: get(N.row_part))

    def input_grad():
        row_total = get(N.row_part) + get(N.yt)
        grads = scale * get(N.weighted) - tokens_f * (scale * scale * scale) * (row_total / features)
        return (cotangent.reshape(count, part).astype(jnp.float32) + grads).reshape(seqs, rows, part)

    def block_out():
        branch = tied(N.block_out, get(N.branch)[0]) + get(N.yb).astype(jnp.float32)
        return (tokens_f + branch).astype(low).reshape(seqs, rows, part)

    def small_grads():
        own, other = get(N.down)
        grads = natural(own, other.astype(jnp.float32))
        x_rows = get(N.rows)[count : 2 * count].astype(jnp.float32)
        grad_gain = jnp.sum(grads * x_rows * scale, axis=0)
        grads = tied(N.taps, get(N.grad_mixed))
        rest = [
            jnp.sum(grads * get(N.extended)[:, k : k + rows] * tap_masks[k], axis=(0, 1))
            for k in range(taps)
        ]
        rest.append(jnp.sum(grads, axis=(0, 1)))
        rest.append(jnp.sum(tied(N.shift, get(N.grad_pre)), axis=(0, 1)))
        conv = get(N.conv).astype(jnp.float32)
        rest.append(jnp.sum(tied(N.skip, get(N.grad_ssm)) * conv, axis=(0, 1)))
        rest.append(grad_gain)
        grad_alog = jnp.sum(back_all(3), axis=0) * get(N.small)[2]
        rest = jnp.concatenate([grad_alog, jnp.stack(rest)], axis=0)
        rest = jnp.pad(rest, ((0, -rest.shape[0] % 16), (0, 0)))
        grad_x_t = dot(tied(N.grad_x, get(N.grad_proj)), get(N.conv_flat), ((0,), (0,)))
        grad_dt = dot(tied(N.grad_dt, get(N.rank)), get(N.grad_pre_low), ((0,), (0,)))
        return deal(grad_x_t, grad_dt, rest)

    pack_steps(plan, N.k, small_grads)
    input_grad, block_out = input_grad(), block_out()
    packed = get(N.k)
    grad_dt = packed[proj_rows : proj_rows + RANK].reshape(devices, -1, shard)
    grad_dt = grad_dt.transpose(1, 0, 2).reshape(-1, channels)
    rest = packed[proj_rows + RANK :]
    by_channel = rest[NSTATE:]
    gain_part = by_channel[taps + 3]
    grad_gain = gain_part + swapped(gain_part, TENSOR)
    grad_in = jnp.stack([get(N.A), get(N.B)], axis=1)
    return (
        block_out,
        input_grad,
        grad_gain,
        grad_in,
        by_channel[:taps],
        by_channel[taps],
        packed[:proj_rows].T,
        grad_dt,
        by_channel[taps + 1],
        rest[:NSTATE].T,
        by_channel[taps + 2],
        get(N.C).T,
    )


def solution(mesh):
    both = (TENSOR, DP)
    devices, halves = mesh.shape[DP], mesh.shape[TENSOR]

    def run(tokens, segments, cotangent, norm_gain, w_in, *others):
        trees = devices == 16 and halves == 2 and w_in.shape[0] == devices * LANES
        trees = trees and w_in.shape[2] == halves * devices * LANES
        return sharded(local if trees else local_whole)(
            tokens, segments, cotangent, norm_gain, w_in, *others
        )

    def sharded(function):
        return jax.shard_map(
            function,
            mesh=mesh,
            in_specs=(
                P(None, DP, TENSOR),
                P(None, DP),
                P(None, DP, TENSOR),
                P(DP),
                P(DP, None, TENSOR),
                P(None, both),
                P(both),
                P(both, None),
                P(DP, TENSOR),
                P(both),
                P(both, None),
                P(both),
                P(TENSOR, DP),
            ),
            out_specs=(
                P(None, DP, TENSOR),
                P(None, DP, TENSOR),
                P(DP),
                P(DP, None, TENSOR),
                P(None, both),
                P(both),
                P(both, None),
                P(DP, TENSOR),
                P(both),
                P(both, None),
                P(both),
                P(TENSOR, DP),
            ),
            check_vma=False,
        )

    return run
```

time: 6570 us -> 492 us (0.07)
  local copies, waits for them, and re-layouts: 3350 us -> 41.9 us
  other arithmetic: 1950 us -> 81.3 us
  waiting for transfers between devices: 777 us -> 167 us
  blocking collectives: 236 us -> 0 us
  matrix products: 135 us -> 15.3 us
  Pallas kernels: 0 us -> 102 us
    pad x832 -> x3, local copies, waits for them, and re-layouts: 2540 us -> 0.79 us  [the longest x1 0.77 us: local(): steps = jnp.pad(w_dt, ((0, NSTATE - w_dt.shape[0]), (0, 0)))]
    add x809 -> x11, other arithmetic: 1040 us -> 5.99 us  [the longest x2 2.07 us: message(): now[1] + decay(behind if known else before) * far]
    reduce_scatter x9 -> x1, waiting for transfers between devices: 660 us -> 0.02 us  [scatter(): lax.psum_scatter(get(f'out{name}'), DP, scatter_dimension=0, tiled=True)]
    concatenate x418 -> x9, other arithmetic: 405 us -> 12.1 us  [the longest x4 6.36 us: core(): return jnp.concatenate([plan.tied(name, first), *others], axis=0)]
    while x2322 -> x0, local copies, waits for them, and re-layouts: 314 us -> none
    mul x288 -> x0, local copies, waits for them, and re-layouts: 245 us -> none  [the longest x96 78.6 us: advance(): inflow = flow_blk[:, None, :] * b_blk[:, :, None]]
    reduce_sum x54 -> x6, other arithmetic: 176 us -> 10.6 us  [the longest x1 3.71 us: proj_part(): grad_bc = jnp.sum(back_all(2), axis=-1).reshape(count, 2 * NSTATE)]
    ppermute x0 -> x54, waiting for transfers between devices: none -> 165 us  [the longest x47 151 us: exchanged(): lax.ppermute(block, DP, [(i, i ^ mask) for i in range(lax.axis_size(DP))])]
where the time goes in v1:
time: 492 us; the launch traced here: 486 us
  waiting for transfers between devices  167 us (34%)
  Pallas kernels  102 us (21%)
  other arithmetic  81.3 us (17%)
  starting transfers between devices  61.9 us (13%)
  local copies, waits for them, and re-layouts  41.9 us (9%)
  between operations  16.6 us (3%)
  matrix products  15.3 us (3%)
    ppermute x47, waiting for transfers between devices, exchanged(): lax.ppermute(block, DP, [(i, i ^ mask) for i in range(lax.axis_size(DP))])  151 us
    ppermute x47, starting transfers between devices, exchanged(): lax.ppermute(block, DP, [(i, i ^ mask) for i in range(lax.axis_size(DP))])  48.3 us
    pallas_call x2, Pallas kernels, reverse_main(): pl.pallas_call(functools.partial(reverse_kernel, len(into)), grid=(channe...  35.4 us
    unnamed x288, local copies, waits for them, and re-layouts  27.8 us
    pallas_call x2, Pallas kernels, down(): pl.pallas_call(functools.partial(down_kernel, len(pairs)), grid=(channels...  18.6 us
    dot_general x8, matrix products, dot(): lax.dot_general(left, right, (dims, ((), ())), preferred_element_type=jnp...  15.3 us
    ppermute x7, waiting for transfers between devices, swapped(): return lax.ppermute(block, axis, [(0, 1), (1, 0)])  14.1 us
    pallas_call x2, Pallas kernels, up(): pl.pallas_call(up_kernel, grid=(channels // width,), in_specs=[pl.BlockSp...  11.8 us
  transfers between devices with their start and end apart: 59, of which 29 were waited for; matrix products, arithmetic and copies ran while one was open for 23% of the time, Pallas kernels for 20%

profile of v1, /device:TPU:0, one launch (start us, length us, event | category | flops | bytes accessed | tf_op | source)
XLA Modules:
  0.0 485.7 jit_solution(6503472736404663442)
XLA Ops:
  27.3 15.8 %collective-permute-done.4.refs_2_.refs_20_ = bf16[128,2048]{1,0:T(8,128)(2,1)} collective-permute-done((bf16[128,2048]{1,0:T(8,128)(2,1)S(1)}, bf16[128,2048]{1,0:T(8,128)(2,1)}, u32[]{:S(2)}, u32[]{:S(2)}) %collective-permute-start.4) | collective-permute-done | bytes 524320 | tf_op jit(solution)/shard_map/a12/bx0/ppermute | solution.py:502
  43.1 5.2 %collective-permute-done.2.refs_8_.refs_10_ = bf16[160,2048]{1,0:T(8,128)(2,1)S(1)} collective-permute-done((bf16[160,2048]{1,0:T(8,128)(2,1)S(1)}, bf16[160,2048]{1,0:T(8,128)(2,1)S(1)}, u32[]{:S(2)}, u32[]{:S(2)}) %collective-permute-start.2) | collective-permute-done | bytes 655392 | tf_op jit(solution)/shard_map/a8/ppermute | solution.py:502
  56.1 10.6 %collective-permute-done.5.refs_12_.refs_14_ = bf16[160,2048]{1,0:T(8,128)(2,1)S(1)} collective-permute-done((bf16[160,2048]{1,0:T(8,128)(2,1)S(1)}, bf16[160,2048]{1,0:T(8,128)(2,1)S(1)}, u32[]{:S(2)}, u32[]{:S(2)}) %collective-permute-start.5) | collective-permute-done | bytes 655392 | tf_op jit(solution)/shard_map/a12/ppermute | solution.py:502
  69.2 9.1 %collective-permute-done.6.refs_6_.refs_8_ = bf16[160,2048]{1,0:T(8,128)(2,1)S(1)} collective-permute-done((bf16[160,2048]{1,0:T(8,128)(2,1)S(1)}, bf16[160,2048]{1,0:T(8,128)(2,1)S(1)}, u32[]{:S(2)}, u32[]{:S(2)}) %collective-permute-start.6) | collective-permute-done | bytes 655392 | tf_op jit(solution)/shard_map/ax4/ppermute | solution.py:502
  85.4 7.6 %collective-permute-done.14.refs_8_.refs_26_ = bf16[128,2048]{1,0:T(8,128)(2,1)} collective-permute-done((bf16[128,2048]{1,0:T(8,128)(2,1)S(1)}, bf16[128,2048]{1,0:T(8,128)(2,1)}, u32[]{:S(2)}, u32[]{:S(2)}) %collective-permute-start.14) | collective-permute-done | bytes 524320 | tf_op jit(solution)/shard_map/as2/b8/ppermute | solution.py:502
  110.5 5.3 %up.2 = bf16[272,2048]{1,0:T(8,128)(2,1)S(1)} custom-call(bf16[272,2048]{1,0:T(8,128)(2,1)S(1)} %fusion.2.x_ref, bf16[160,2048]{1,0:T(8,128)(2,1)S(1)} %pad_maximum_fusion.8.refs_0_.refs_2_, bf16[512,2048]{1,0:T(8,128)(2,1)S(1)} %collective-permute-done.12.refs_1_.refs_5_.refs_9_.refs_13_.refs_3_.refs_7_.refs_11_.refs_15_, bf16[160,2048]{1,0:T(8,128)(2,1)S(1)} %copy-done.29, ...), custom_call_target="tpu_custom_call" | custom-call | tf_op jit(solution)/shard_map/up/pallas_call | solution.py:320
  130.5 6.5 %collective-permute-start.20 = (bf16[128,2048]{1,0:T(8,128)(2,1)}, bf16[128,2048]{1,0:T(8,128)(2,1)}, u32[]{:S(2)}, u32[]{:S(2)}) collective-permute-start(bf16[128,2048]{1,0:T(8,128)(2,1)} %collective-permute-done.14.refs_8_.refs_26_), channel_id=1, source_target_pairs={{0,8},{2,10},{4,12},{6,14},{8,0},{10,2},{12,4},{14,6},{16,24},{18,... | collective-permute-start | bytes 1572872 | tf_op jit(solution)/shard_map/f1/bx12/b12/ppermute | solution.py:502
  147.0 13.8 %collective-permute-done.24 = f32[2,2048]{1,0:T(2,128)S(1)} collective-permute-done((f32[2,2048]{1,0:T(2,128)S(1)}, f32[2,2048]{1,0:T(2,128)S(1)}, u32[]{:S(2)}, u32[]{:S(2)}) %collective-permute-start.24) | collective-permute-done | bytes 16416 | tf_op jit(solution)/shard_map/fspan1/ppermute | solution.py:502
  164.8 6.7 %forward_end.1 = f32[2,16,2048]{2,1,0:T(8,128)S(1)} custom-call(f32[2,16,8,2048]{3,2,1,0:T(8,128)S(1)} %get-tuple-element.193.step_ref, f32[2,16,8,2048]{3,2,1,0:T(8,128)S(1)} %bitcast.189, f32[2,128,32,128]{3,2,1,0:T(8,128)S(1)} %broadcast_in_dim.94.b_ref.bc_ref.c_ref, f32[16,2048]{1,0:T(8,128)S(1)} %get-tuple-element.202.rate_ref), custom_call_target="tpu_custom_call" | custom-call | tf_op jit(solution)/shard_map/forward_end/pallas_call | solution.py:226
  173.9 11.9 %collective-permute-done.22.refs_14_.refs_32_ = bf16[128,2048]{1,0:T(8,128)(2,1)S(1)} collective-permute-done((bf16[128,2048]{1,0:T(8,128)(2,1)}, bf16[128,2048]{1,0:T(8,128)(2,1)S(1)}, u32[]{:S(2)}, u32[]{:S(2)}) %collective-permute-start.22) | collective-permute-done | bytes 524320 | tf_op jit(solution)/shard_map/f1/bx12/ppermute | solution.py:502
  195.9 4.2 collective-permute-done.25
  202.3 11.2 %collective-permute-done.27 = bf16[2,16,2048]{2,1,0:T(8,128)(2,1)S(1)} collective-permute-done((bf16[2,16,2048]{2,1,0:T(8,128)(2,1)S(1)}, bf16[2,16,2048]{2,1,0:T(8,128)(2,1)S(1)}, u32[]{:S(2)}, u32[]{:S(2)}) %collective-permute-start.27) | collective-permute-done | bytes 131104 | tf_op jit(solution)/shard_map/f3/ppermute | solution.py:502
  213.8 6.5 %up.3 = f32[256,2048]{1,0:T(8,128)S(1)} custom-call(bf16[256,2048]{1,0:T(8,128)(2,1)S(1)} %slice.461.x_ref, bf16[128,2048]{1,0:T(8,128)(2,1)S(1)} %bitcast.187, bf16[512,2048]{1,0:T(8,128)(2,1)S(1)} %collective-permute-done.28.refs_1_.refs_5_.refs_9_.refs_13_.refs_19_.refs_23_.refs_27_.refs_31_, bf16[128,2048]{1,0:T(8,128)(2,1)} %collective-permute-done.4.refs_2_.refs_20_, ...), custom_call_target="tpu_custom_call" | custom-call | tf_op jit(solution)/shard_map/up/pallas_call | solution.py:320
  220.4 11.7 %forward_main.1 = f32[2,16,8,2048]{3,2,1,0:T(8,128)S(1)} custom-call(f32[2,16,8,2048]{3,2,1,0:T(8,128)S(1)} %copy-done.6, f32[2,16,8,2048]{3,2,1,0:T(8,128)S(1)} %fusion.88.flow_ref, f32[2,128,32,128]{3,2,1,0:T(8,128)S(1)} %broadcast_in_dim.94.b_ref.bc_ref.c_ref, f32[16,2048]{1,0:T(8,128)S(1)} %get-tuple-element.202.rate_ref, ...), custom_call_target="tpu_custom_call" | custom-call | tf_op jit(solution)/shard_map/forward_main/pallas_call | solution.py:252
  234.1 5.8 %convolution_convert_fusion = bf16[2048,2048]{1,0:T(8,128)(2,1)} fusion(bf16[256,2048]{1,0:T(8,128)(2,1)S(1)} %copy-done.83, bf16[256,2048]{1,0:T(8,128)(2,1)S(1)} %bitcast.177), kind=kOutput, calls=%fused_computation | convolution fusion | flops 2151677952 | bytes 10485760 | tf_op jit(solution)/shard_map/dot_general | solution.py:531
  240.9 5.9 %fusion.70 = f32[256,2048]{1,0:T(8,128)S(1)} fusion(bf16[256,2048]{1,0:T(8,128)(2,1)S(1)} %copy-done.83, bf16[2048,2048]{1,0:T(8,128)(2,1)} %all-gather.2.cloned.1.call-done.refs_1_.refs_2_.refs_3_.refs_4_.refs_5_.refs_6_.refs_7_.refs_8_.refs_9_.refs_10_.refs_11_.refs_12_.refs_13_.refs_14_.refs_15_.refs_16_), kind=kOutput, calls=%fused_computation.213 | convolution fusion | flops 2147483648 | bytes 11534336 | tf_op jit(solution)/shard_map/dot_general | solution.py:531
  251.0 6.9 %reverse_end.1 = f32[2,16,2048]{2,1,0:T(8,128)S(1)} custom-call(f32[2,16,8,2048]{3,2,1,0:T(8,128)S(1)} %copy-done.7, f32[2,16,8,2048]{3,2,1,0:T(8,128)S(1)} %multiply_multiply_fusion.3.grad_ref, f32[2,128,32,128]{3,2,1,0:T(8,128)S(1)} %copy-done.1, f32[16,2048]{1,0:T(8,128)S(1)} %get-tuple-element.202.rate_ref), custom_call_target="tpu_custom_call" | custom-call | tf_op jit(solution)/shard_map/reverse_end/pallas_call | solution.py:239
  259.5 5.0 %outer.2 = (bf16[512,2048]{1,0:T(8,128)(2,1)S(1)}, bf16[512,2048]{1,0:T(8,128)(2,1)}, bf16[512,2048]{1,0:T(8,128)(2,1)}, bf16[512,2048]{1,0:T(8,128)(2,1)}) custom-call(bf16[256,2048]{1,0:T(8,128)(2,1)S(1)} %slice.461.x_ref, bf16[256,2048]{1,0:T(8,128)(2,1)S(1)} %bitcast.179), custom_call_target="tpu_custom_call" | custom-call | tf_op jit(solution)/shard_map/outer/pallas_call | solution.py:407
  280.8 8.1 %down.2 = (f32[256,1024]{1,0:T(8,128)S(1)}, bf16[256,1024]{1,0:T(8,128)(2,1)}) custom-call(bf16[256,2048]{1,0:T(8,128)(2,1)S(1)} %bitcast.178, bf16[2048,2048]{1,0:T(8,128)(2,1)} %all-gather.2.cloned.1.call-done.refs_1_.refs_2_.refs_3_.refs_4_.refs_5_.refs_6_.refs_7_.refs_8_.refs_9_.refs_10_.refs_11_.refs_12_.refs_13_.refs_14_.refs_15_.refs_16_, ...), custom_call_target="tpu_custom_call" | custom-call | tf_op jit(solution)/shard_map/down/pallas_call | solution.py:367
  290.5 6.9 %collective-permute-done.34 = bf16[2,16,2048]{2,1,0:T(8,128)(2,1)} collective-permute-done((bf16[2,16,2048]{2,1,0:T(8,128)(2,1)}, bf16[2,16,2048]{2,1,0:T(8,128)(2,1)}, u32[]{:S(2)}, u32[]{:S(2)}) %collective-permute-start.34) | collective-permute-done | bytes 131104 | tf_op jit(solution)/shard_map/r3/ppermute | solution.py:502
  299.3 17.9 %reverse_main.2 = (f32[2,16,8,2048]{3,2,1,0:T(8,128)}, f32[2,16,8,2048]{3,2,1,0:T(8,128)}, f32[2,128,32,128]{3,2,1,0:T(8,128)}, f32[2,16,2048]{2,1,0:T(8,128)}) custom-call(f32[2,16,8,2048]{3,2,1,0:T(8,128)} %copy-done.5, f32[2,16,8,2048]{3,2,1,0:T(8,128)} %get-tuple-element.192.delta_ref, f32[2,16,8,2048]{3,2,1,0:T(8,128)} %copy-done.12, ...), custom_call_target="tpu_custom_call" | custom-call | tf_op jit(solution)/shard_map/reverse_main/pallas_call | solution.py:273
  320.4 17.5 %reverse_main.3 = (f32[2,16,8,2048]{3,2,1,0:T(8,128)}, f32[2,16,8,2048]{3,2,1,0:T(8,128)}, f32[2,128,32,128]{3,2,1,0:T(8,128)}, f32[2,16,2048]{2,1,0:T(8,128)}) custom-call(f32[2,16,8,2048]{3,2,1,0:T(8,128)} %copy-done.5, ...), custom_call_target="tpu_custom_call", output_to_operand_aliasing={{0}: (10, {}), {1}: (11, {}), {2}: (12, {}), {3}: (13, {})} | custom-call | tf_op jit(solution)/shard_map/reverse_main/pallas_call | solution.py:273
  337.9 5.9 %collective-permute-done.37 = bf16[256,2048]{1,0:T(8,128)(2,1)} collective-permute-done((bf16[256,2048]{1,0:T(8,128)(2,1)S(1)}, bf16[256,2048]{1,0:T(8,128)(2,1)}, u32[]{:S(2)}, u32[]{:S(2)}) %collective-permute-start.37) | collective-permute-done | bytes 1048608 | tf_op jit(solution)/shard_map/Bx0/ppermute | solution.py:502
  352.7 4.2 collective-permute-done.38
  364.8 5.4 %outer.3 = (bf16[512,2048]{1,0:T(8,128)(2,1)S(1)}, bf16[512,2048]{1,0:T(8,128)(2,1)}, bf16[512,2048]{1,0:T(8,128)(2,1)}, bf16[512,2048]{1,0:T(8,128)(2,1)}) custom-call(bf16[256,2048]{1,0:T(8,128)(2,1)S(1)} %slice.461.x_ref, bf16[256,2048]{1,0:T(8,128)(2,1)S(1)} %bitcast.181), custom_call_target="tpu_custom_call" | custom-call | tf_op jit(solution)/shard_map/outer/pallas_call | solution.py:407
  377.2 4.4 add_convert_fusion
  391.9 10.5 %down.3 = (f32[256,1024]{1,0:T(8,128)}, bf16[256,1024]{1,0:T(8,128)(2,1)S(1)}) custom-call(bf16[256,2048]{1,0:T(8,128)(2,1)} %bitcast.182, bf16[256,2048]{1,0:T(8,128)(2,1)} %bitcast.180, bf16[160,2048]{1,0:T(8,128)(2,1)S(1)} %copy-done.27, bf16[512,2048]{1,0:T(8,128)(2,1)} %copy-done.2, bf16[160,2048]{1,0:T(8,128)(2,1)S(1)} %copy-done.30, ...), custom_call_target="tpu_custom_call" | custom-call | tf_op jit(solution)/shard_map/down/pallas_call | solution.py:367
  402.5 10.4 %collective-permute-done.44 = bf16[128,2048]{1,0:T(8,128)(2,1)} collective-permute-done((bf16[128,2048]{1,0:T(8,128)(2,1)}, bf16[128,2048]{1,0:T(8,128)(2,1)}, u32[]{:S(2)}, u32[]{:S(2)}) %collective-permute-start.44) | collective-permute-done | bytes 524320 | tf_op jit(solution)/shard_map/yn/Bz8/ppermute | solution.py:502
  418.2 7.7 %collective-permute-done.45 = bf16[256,1024]{1,0:T(8,128)(2,1)S(1)} collective-permute-done((bf16[256,1024]{1,0:T(8,128)(2,1)S(1)}, bf16[256,1024]{1,0:T(8,128)(2,1)S(1)}, u32[]{:S(2)}, u32[]{:S(2)}) %collective-permute-start.45) | collective-permute-done | bytes 524320 | tf_op jit(solution)/shard_map/yn/ppermute | solution.py:498
  444.0 6.0 %collective-permute-done.48 = bf16[4,320,128]{2,1,0:T(8,128)(2,1)S(1)} collective-permute-done((bf16[4,320,128]{2,1,0:T(8,128)(2,1)S(1)}, bf16[4,320,128]{2,1,0:T(8,128)(2,1)S(1)}, u32[]{:S(2)}, u32[]{:S(2)}) %collective-permute-start.48) | collective-permute-done | bytes 327712 | tf_op jit(solution)/shard_map/k1/ppermute | solution.py:502
  450.7 6.5 %collective-permute-done.56 = bf16[128,2048]{1,0:T(8,128)(2,1)S(1)} collective-permute-done((bf16[128,2048]{1,0:T(8,128)(2,1)S(1)}, bf16[128,2048]{1,0:T(8,128)(2,1)S(1)}, u32[]{:S(2)}, u32[]{:S(2)}) %collective-permute-start.56) | collective-permute-done | bytes 524320 | tf_op jit(solution)/shard_map/Az4/ppermute | solution.py:502
  457.1 7.7 %collective-permute-done.55 = bf16[128,2048]{1,0:T(8,128)(2,1)S(1)} collective-permute-done((bf16[128,2048]{1,0:T(8,128)(2,1)S(1)}, bf16[128,2048]{1,0:T(8,128)(2,1)S(1)}, u32[]{:S(2)}, u32[]{:S(2)}) %collective-permute-start.55) | collective-permute-done | bytes 524320 | tf_op jit(solution)/shard_map/Az8/ppermute | solution.py:502
  (511 shorter events, 200.2 us)
Async XLA Ops:
  7.2 233.7 %all-gather.2.cloned.1.call-start = ((), (), s32[]{:S(2)}) async-start(), calls=%async_computation.1 | async-start | bytes 8912896 | tf_op jit(solution)/shard_map/all_gather | solution.py:1072
  14.0 29.1 %collective-permute-start.3 = (bf16[160,2048]{1,0:T(8,128)(2,1)S(1)}, bf16[160,2048]{1,0:T(8,128)(2,1)S(1)}, u32[]{:S(2)}, u32[]{:S(2)}) collective-permute-start(bf16[160,2048]{1,0:T(8,128)(2,1)S(1)} %pad_maximum_fusion.8.refs_0_.refs_2_), channel_id=1, source_target_pairs={{0,4},{2,6},{4,0},{6,2},{8,12},{10,14},{12,8},{14,10},{16,20},{18,... | collective-permute-start | bytes 1966088 | tf_op jit(solution)/shard_map/y0/ax0/ppermute | solution.py:502
  17.0 31.2 %collective-permute-start.2 = (bf16[160,2048]{1,0:T(8,128)(2,1)S(1)}, bf16[160,2048]{1,0:T(8,128)(2,1)S(1)}, u32[]{:S(2)}, u32[]{:S(2)}) collective-permute-start(bf16[160,2048]{1,0:T(8,128)(2,1)S(1)} %pad_maximum_fusion.8.refs_0_.refs_2_), channel_id=1, source_target_pairs={{0,16},{2,18},{4,20},{6,22},{8,24},{10,26},{12,28},{14,30},{16,0},... | collective-permute-start | bytes 1966088 | tf_op jit(solution)/shard_map/a8/ppermute | solution.py:502
  19.6 28.8 %collective-permute-start.1 = (bf16[160,2048]{1,0:T(8,128)(2,1)S(1)}, bf16[160,2048]{1,0:T(8,128)(2,1)S(1)}, u32[]{:S(2)}, u32[]{:S(2)}) collective-permute-start(bf16[160,2048]{1,0:T(8,128)(2,1)S(1)} %pad_maximum_fusion.8.refs_0_.refs_2_), channel_id=1, source_target_pairs={{0,8},{2,10},{4,12},{6,14},{8,0},{10,2},{12,4},{14,6},{16,24},{18,... | collective-permute-start | bytes 1966088 | tf_op jit(solution)/shard_map/a4/ppermute | solution.py:502
  21.5 21.6 %collective-permute-start.4 = (bf16[128,2048]{1,0:T(8,128)(2,1)S(1)}, bf16[128,2048]{1,0:T(8,128)(2,1)}, u32[]{:S(2)}, u32[]{:S(2)}) collective-permute-start(bf16[128,2048]{1,0:T(8,128)(2,1)S(1)} %bitcast.183), channel_id=1, source_target_pairs={{0,4},{2,6},{4,0},{6,2},{8,12},{10,14},{12,8},{14,10},{16,20},{18,... | collective-permute-start | bytes 1572872 | tf_op jit(solution)/shard_map/a12/bx0/ppermute | solution.py:502
  48.4 20.7 %collective-permute-start.7 = (bf16[160,2048]{1,0:T(8,128)(2,1)S(1)}, bf16[160,2048]{1,0:T(8,128)(2,1)S(1)}, u32[]{:S(2)}, u32[]{:S(2)}) collective-permute-start(bf16[160,2048]{1,0:T(8,128)(2,1)S(1)} %collective-permute-done.2.refs_8_.refs_10_), channel_id=1, source_target_pairs={{0,4},{2,6},{4,0},{6,2},{8,12},{10,14},{12,8},{14,10},{16,20},{18,... | collective-permute-start | bytes 1966088 | tf_op jit(solution)/shard_map/ax8/ppermute | solution.py:502
  48.9 17.8 %collective-permute-start.5 = (bf16[160,2048]{1,0:T(8,128)(2,1)S(1)}, bf16[160,2048]{1,0:T(8,128)(2,1)S(1)}, u32[]{:S(2)}, u32[]{:S(2)}) collective-permute-start(bf16[160,2048]{1,0:T(8,128)(2,1)S(1)} %collective-permute-done.2.refs_8_.refs_10_), channel_id=1, source_target_pairs={{0,8},{2,10},{4,12},{6,14},{8,0},{10,2},{12,4},{14,6},{16,24},{18,... | collective-permute-start | bytes 1966088 | tf_op jit(solution)/shard_map/a12/ppermute | solution.py:502
  51.2 27.1 %collective-permute-start.6 = (bf16[160,2048]{1,0:T(8,128)(2,1)S(1)}, bf16[160,2048]{1,0:T(8,128)(2,1)S(1)}, u32[]{:S(2)}, u32[]{:S(2)}) collective-permute-start(bf16[160,2048]{1,0:T(8,128)(2,1)S(1)} %collective-permute-done.1.refs_4_.refs_6_), channel_id=1, source_target_pairs={{0,4},{2,6},{4,0},{6,2},{8,12},{10,14},{12,8},{14,10},{16,20},{18,... | collective-permute-start | bytes 1966088 | tf_op jit(solution)/shard_map/ax4/ppermute | solution.py:502
  53.2 48.9 %collective-permute-start.11 = (bf16[528,1024]{1,0:T(8,128)(2,1)}, bf16[528,1024]{1,0:T(8,128)(2,1)}, u32[]{:S(2)}, u32[]{:S(2)}) collective-permute-start(bf16[528,1024]{1,0:T(8,128)(2,1)} %fusion.16), channel_id=1, source_target_pairs={{0,1},{1,0},{2,3},{3,2},{4,5},{5,4},{6,7},{7,6},{8,9},{9,8},{10,11... | collective-permute-start | bytes 3244040 | tf_op jit(solution)/shard_map/y0/ppermute | solution.py:498
  66.8 26.2 %collective-permute-start.14 = (bf16[128,2048]{1,0:T(8,128)(2,1)S(1)}, bf16[128,2048]{1,0:T(8,128)(2,1)}, u32[]{:S(2)}, u32[]{:S(2)}) collective-permute-start(bf16[128,2048]{1,0:T(8,128)(2,1)S(1)} %bitcast.184), channel_id=1, source_target_pairs={{0,16},{2,18},{4,20},{6,22},{8,24},{10,26},{12,28},{14,30},{16,0},... | collective-permute-start | bytes 1572872 | tf_op jit(solution)/shard_map/as2/b8/ppermute | solution.py:502
  67.4 25.6 %collective-permute-start.13 = (bf16[128,2048]{1,0:T(8,128)(2,1)S(1)}, bf16[128,2048]{1,0:T(8,128)(2,1)}, u32[]{:S(2)}, u32[]{:S(2)}) collective-permute-start(bf16[128,2048]{1,0:T(8,128)(2,1)S(1)} %bitcast.185), channel_id=1, source_target_pairs={{0,8},{2,10},{4,12},{6,14},{8,0},{10,2},{12,4},{14,6},{16,24},{18,... | collective-permute-start | bytes 1572872 | tf_op jit(solution)/shard_map/as2/b4/ppermute | solution.py:502
  81.7 26.2 %collective-permute-start.12 = (bf16[512,2048]{1,0:T(8,128)(2,1)}, bf16[512,2048]{1,0:T(8,128)(2,1)S(1)}, u32[]{:S(2)}, u32[]{:S(2)}) collective-permute-start(bf16[512,2048]{1,0:T(8,128)(2,1)} %pad_maximum_fusion.1), channel_id=1, source_target_pairs={{0,2},{2,0},{4,6},{6,4},{8,10},{10,8},{12,14},{14,12},{16,18},{18,... | collective-permute-start | bytes 6291464 | tf_op jit(solution)/shard_map/as0/ppermute | solution.py:502
  116.9 256.5 %reduce-scatter.2.cloned.1.call-start = ((), (), s32[]{:S(2)}) async-start(), calls=%async_computation.2 | async-start | bytes 8912896 | tf_op jit(solution)/shard_map/reduce_scatter | solution.py:1175
  130.5 31.3 %collective-permute-start.20 = (bf16[128,2048]{1,0:T(8,128)(2,1)}, bf16[128,2048]{1,0:T(8,128)(2,1)}, u32[]{:S(2)}, u32[]{:S(2)}) collective-permute-start(bf16[128,2048]{1,0:T(8,128)(2,1)} %collective-permute-done.14.refs_8_.refs_26_), channel_id=1, source_target_pairs={{0,8},{2,10},{4,12},{6,14},{8,0},{10,2},{12,4},{14,6},{16,24},{18,... | collective-permute-start | bytes 1572872 | tf_op jit(solution)/shard_map/f1/bx12/b12/ppermute | solution.py:502
  137.0 26.1 %collective-permute-start.17 = (bf16[128,2048]{1,0:T(8,128)(2,1)}, bf16[128,2048]{1,0:T(8,128)(2,1)}, u32[]{:S(2)}, u32[]{:S(2)}) collective-permute-start(bf16[128,2048]{1,0:T(8,128)(2,1)} %collective-permute-done.14.refs_8_.refs_26_), channel_id=1, source_target_pairs={{0,4},{2,6},{4,0},{6,2},{8,12},{10,14},{12,8},{14,10},{16,20},{18,... | collective-permute-start | bytes 1572872 | tf_op jit(solution)/shard_map/bx8/ppermute | solution.py:502
  137.9 23.9 %collective-permute-start.21 = (bf16[128,2048]{1,0:T(8,128)(2,1)}, bf16[128,2048]{1,0:T(8,128)(2,1)}, u32[]{:S(2)}, u32[]{:S(2)}) collective-permute-start(bf16[128,2048]{1,0:T(8,128)(2,1)} %collective-permute-done.13.refs_4_.refs_22_), channel_id=1, source_target_pairs={{0,4},{2,6},{4,0},{6,2},{8,12},{10,14},{12,8},{14,10},{16,20},{18,... | collective-permute-start | bytes 1572872 | tf_op jit(solution)/shard_map/f1/bx12/bx4/ppermute | solution.py:502
  161.4 33.8 %collective-permute-start.26 = (f32[2,2048]{1,0:T(2,128)S(1)}, f32[2,2048]{1,0:T(2,128)S(1)}, u32[]{:S(2)}, u32[]{:S(2)}) collective-permute-start(f32[2,2048]{1,0:T(2,128)S(1)} %get-tuple-element.221), channel_id=1, source_target_pairs={{0,8},{2,10},{4,12},{6,14},{8,0},{10,2},{12,4},{14,6},{16,24},{18,... | collective-permute-start | bytes 49160 | tf_op jit(solution)/shard_map/fspan2/ppermute | solution.py:502
  161.8 24.1 %collective-permute-start.22 = (bf16[128,2048]{1,0:T(8,128)(2,1)}, bf16[128,2048]{1,0:T(8,128)(2,1)S(1)}, u32[]{:S(2)}, u32[]{:S(2)}) collective-permute-start(bf16[128,2048]{1,0:T(8,128)(2,1)} %collective-permute-done.20.refs_12_.refs_30_), channel_id=1, source_target_pairs={{0,4},{2,6},{4,0},{6,2},{8,12},{10,14},{12,8},{14,10},{16,20},{18,... | collective-permute-start | bytes 1572872 | tf_op jit(solution)/shard_map/f1/bx12/ppermute | solution.py:502
  173.2 40.5 %collective-permute-start.28 = (bf16[512,2048]{1,0:T(8,128)(2,1)S(1)}, bf16[512,2048]{1,0:T(8,128)(2,1)S(1)}, u32[]{:S(2)}, u32[]{:S(2)}) collective-permute-start(bf16[512,2048]{1,0:T(8,128)(2,1)S(1)} %pad_maximum_fusion.3), channel_id=1, source_target_pairs={{0,2},{2,0},{4,6},{6,4},{8,10},{10,8},{12,14},{14,12},{16,18},{18,... | collective-permute-start | bytes 6291464 | tf_op jit(solution)/shard_map/bs0/ppermute | solution.py:502
  189.8 23.9 %collective-permute-start.29 = (bf16[512,2048]{1,0:T(8,128)(2,1)S(1)}, bf16[512,2048]{1,0:T(8,128)(2,1)S(1)}, u32[]{:S(2)}, u32[]{:S(2)}) collective-permute-start(bf16[512,2048]{1,0:T(8,128)(2,1)S(1)} %pad_maximum_fusion.4), channel_id=1, source_target_pairs={{0,2},{2,0},{4,6},{6,4},{8,10},{10,8},{12,14},{14,12},{16,18},{18,... | collective-permute-start | bytes 6291464 | tf_op jit(solution)/shard_map/bs2/ppermute | solution.py:502
  267.5 49.7 %collective-permute-start.39 = (bf16[512,2048]{1,0:T(8,128)(2,1)}, bf16[512,2048]{1,0:T(8,128)(2,1)}, u32[]{:S(2)}, u32[]{:S(2)}) collective-permute-start(bf16[512,2048]{1,0:T(8,128)(2,1)} %get-tuple-element.106), channel_id=1, source_target_pairs={{0,2},{2,0},{4,6},{6,4},{8,10},{10,8},{12,14},{14,12},{16,18},{18,... | collective-permute-start | bytes 6291464 | tf_op jit(solution)/shard_map/Bz4/Bs0/ppermute | solution.py:502
  275.6 41.5 %collective-permute-start.36 = (bf16[256,2048]{1,0:T(8,128)(2,1)}, bf16[256,2048]{1,0:T(8,128)(2,1)}, u32[]{:S(2)}, u32[]{:S(2)}) collective-permute-start(bf16[256,2048]{1,0:T(8,128)(2,1)} %get-tuple-element.183), channel_id=1, source_target_pairs={{0,4},{2,6},{4,0},{6,2},{8,12},{10,14},{12,8},{14,10},{16,20},{18,... | collective-permute-start | bytes 3145736 | tf_op jit(solution)/shard_map/Bx4/ppermute | solution.py:502
  289.8 54.0 %collective-permute-start.37 = (bf16[256,2048]{1,0:T(8,128)(2,1)S(1)}, bf16[256,2048]{1,0:T(8,128)(2,1)}, u32[]{:S(2)}, u32[]{:S(2)}) collective-permute-start(bf16[256,2048]{1,0:T(8,128)(2,1)S(1)} %copy-done.89), channel_id=1, source_target_pairs={{0,4},{2,6},{4,0},{6,2},{8,12},{10,14},{12,8},{14,10},{16,20},{18,... | collective-permute-start | bytes 3145736 | tf_op jit(solution)/shard_map/Bx0/ppermute | solution.py:502
  320.4 36.6 %collective-permute-start.40 = (bf16[256,2048]{1,0:T(8,128)(2,1)}, bf16[256,2048]{1,0:T(8,128)(2,1)}, u32[]{:S(2)}, u32[]{:S(2)}) collective-permute-start(bf16[256,2048]{1,0:T(8,128)(2,1)} %pad_maximum_fusion.7), channel_id=1, source_target_pairs={{0,8},{2,10},{4,12},{6,14},{8,0},{10,2},{12,4},{14,6},{16,24},{18,... | collective-permute-start | bytes 3145736 | tf_op jit(solution)/shard_map/Bz4/ppermute | solution.py:502
  373.4 41.5 %collective-permute-start.52 = (bf16[512,2048]{1,0:T(8,128)(2,1)}, bf16[512,2048]{1,0:T(8,128)(2,1)}, u32[]{:S(2)}, u32[]{:S(2)}) collective-permute-start(bf16[512,2048]{1,0:T(8,128)(2,1)} %get-tuple-element.118), channel_id=1, source_target_pairs={{0,2},{2,0},{4,6},{6,4},{8,10},{10,8},{12,14},{14,12},{16,18},{18,... | collective-permute-start | bytes 6291464 | tf_op jit(solution)/shard_map/Az8/As0/ppermute | solution.py:502
  375.9 42.3 %collective-permute-start.31 = (bf16[256,1024]{1,0:T(8,128)(2,1)}, bf16[256,1024]{1,0:T(8,128)(2,1)}, u32[]{:S(2)}, u32[]{:S(2)}) collective-permute-start(bf16[256,1024]{1,0:T(8,128)(2,1)} %get-tuple-element.93), channel_id=1, source_target_pairs={{0,1},{1,0},{2,3},{3,2},{4,5},{5,4},{6,7},{7,6},{8,9},{9,8},{10,11... | collective-permute-start | bytes 1572872 | tf_op jit(solution)/shard_map/yb/ppermute | solution.py:498
  381.7 31.3 %collective-permute-start.43 = (bf16[256,2048]{1,0:T(8,128)(2,1)}, bf16[256,2048]{1,0:T(8,128)(2,1)}, u32[]{:S(2)}, u32[]{:S(2)}) collective-permute-start(bf16[256,2048]{1,0:T(8,128)(2,1)} %get-tuple-element.181), channel_id=1, source_target_pairs={{0,4},{2,6},{4,0},{6,2},{8,12},{10,14},{12,8},{14,10},{16,20},{18,... | collective-permute-start | bytes 3145736 | tf_op jit(solution)/shard_map/yn/Ax4/ppermute | solution.py:502
  386.7 26.3 %collective-permute-start.44 = (bf16[128,2048]{1,0:T(8,128)(2,1)}, bf16[128,2048]{1,0:T(8,128)(2,1)}, u32[]{:S(2)}, u32[]{:S(2)}) collective-permute-start(bf16[128,2048]{1,0:T(8,128)(2,1)} %add_convert_fusion.7), channel_id=1, source_target_pairs={{0,16},{2,18},{4,20},{6,22},{8,24},{10,26},{12,28},{14,30},{16,0},... | collective-permute-start | bytes 1572872 | tf_op jit(solution)/shard_map/yn/Bz8/ppermute | solution.py:502
  414.5 24.4 %collective-permute-start.53 = (bf16[256,2048]{1,0:T(8,128)(2,1)}, bf16[256,2048]{1,0:T(8,128)(2,1)}, u32[]{:S(2)}, u32[]{:S(2)}) collective-permute-start(bf16[256,2048]{1,0:T(8,128)(2,1)} %get-tuple-element.119), channel_id=1, source_target_pairs={{0,4},{2,6},{4,0},{6,2},{8,12},{10,14},{12,8},{14,10},{16,20},{18,... | collective-permute-start | bytes 3145736 | tf_op jit(solution)/shard_map/Az8/Ax0/ppermute | solution.py:502
  418.2 20.7 %collective-permute-start.54 = (bf16[128,2048]{1,0:T(8,128)(2,1)}, bf16[128,2048]{1,0:T(8,128)(2,1)}, u32[]{:S(2)}, u32[]{:S(2)}) collective-permute-start(bf16[128,2048]{1,0:T(8,128)(2,1)} %get-tuple-element.176), channel_id=1, source_target_pairs={{0,8},{2,10},{4,12},{6,14},{8,0},{10,2},{12,4},{14,6},{16,24},{18,... | collective-permute-start | bytes 1572872 | tf_op jit(solution)/shard_map/Az8/Az12/ppermute | solution.py:502
  435.4 21.7 %collective-permute-start.56 = (bf16[128,2048]{1,0:T(8,128)(2,1)S(1)}, bf16[128,2048]{1,0:T(8,128)(2,1)S(1)}, u32[]{:S(2)}, u32[]{:S(2)}) collective-permute-start(bf16[128,2048]{1,0:T(8,128)(2,1)S(1)} %copy-done.96), channel_id=1, source_target_pairs={{0,8},{2,10},{4,12},{6,14},{8,0},{10,2},{12,4},{14,6},{16,24},{18,... | collective-permute-start | bytes 1572872 | tf_op jit(solution)/shard_map/Az4/ppermute | solution.py:502
  440.7 24.2 %collective-permute-start.55 = (bf16[128,2048]{1,0:T(8,128)(2,1)S(1)}, bf16[128,2048]{1,0:T(8,128)(2,1)S(1)}, u32[]{:S(2)}, u32[]{:S(2)}) collective-permute-start(bf16[128,2048]{1,0:T(8,128)(2,1)S(1)} %add_convert_fusion.5), channel_id=1, source_target_pairs={{0,16},{2,18},{4,20},{6,22},{8,24},{10,26},{12,28},{14,30},{16,0},... | collective-permute-start | bytes 1572872 | tf_op jit(solution)/shard_map/Az8/ppermute | solution.py:502
  (169 other events, 1730.3 us)
Sparse Core Ops, SparseCore 0:
  117.0 100.2 all-gather.1
  241.0 124.3 reduce-scatter.1

commit v2 on v1

--- a/solution.py
+++ b/solution.py
@@ -979,14 +979,10 @@
     as0=(N.ax4, N.ax8, N.a12),
     as2=(N.b4, N.b8),
     bx4=(N.as0, N.as2, N.ae),
-    bx8=(N.inner, N.ax12),
-    b12=(N.inner, N.ax12),
-    bx12=(N.inner, N.bx4),
-    bs0=(N.inner,),
-    end=(N.bx8,),
-    f1=(N.bx12,),
-    gate=(N.f0,),
-    readout=(N.gate,),
+    b12=(N.inner,),
+    bx12=(N.f1,),
+    bs0=(N.f1,),
+    gate=(N.readout,),
     outB=(N.r0,),
     branch=(N.outB,),
     back0=(N.branch,),
@@ -994,13 +990,16 @@
     c=(N.inner,),
     grad_gated=(N.outC,),
     back1=(N.Bx4,),
-    grad_pre=(N.Bx0,),
-    grad_mixed=(N.Bz4,),
+    grad_mixed=(N.Bx0, N.Bz12, N.yb),
     Bz8=(N.Ap4,),
-    down=(N.Ap4,),
+    down=(N.Ap4, N.As0),
     Ax0=(N.Ap4,),
     yn=(N.Ax4, N.Bz8),
     y0=(N.ax0,),
+    bs2=(N.readout,),
+    grad_pre=(N.Bx4,),
+    Az12=(N.As0,),
+    ae=(N.ax8,),
 )
 GROUPS = dict(
     a=((0,), (4,), (8,), (12,)),
@@ -1010,7 +1009,7 @@
     B=((4, 12), (0, 8)),
     A=((4, 12), (0, 8)),
     Cz=(),
-    Bz=((4, 12),),
+    Bz=((12,), (4,)),
     Az=((12,), (4,)),
 )
 
@@ -1172,7 +1171,12 @@
             scatter_steps(plan, name, f"out{name}", groups, near)
         else:
             add(f"out{name}", lambda: dot(x(), y(), ((0,), (0,))).astype(low))
-            add(f"{name}rs", lambda: lax.psum_scatter(get(f"out{name}"), DP, scatter_dimension=0, tiled=True))
+            add(
+                f"{name}rs",
+                lambda: lax.psum_scatter(
+                    tied(f"{name}rs", get(f"out{name}")), DP, scatter_dimension=0, tiled=True
+                ),
+            )
             add(name, lambda: tied(name, get(f"{name}rs")).astype(jnp.float32))
 
     scatter(N.C, lambda: get(N.cot), lambda: tied(N.outC, get(N.gated)), GROUPS[N.C], GROUPS[N.Cz])

time: 492 us -> 464 us (0.943)
  waiting for transfers between devices: 167 us -> 135 us
  starting transfers between devices: 61.9 us -> 67.2 us
    ppermute x47 -> x48, waiting for transfers between devices: 151 us -> 120 us  [exchanged(): lax.ppermute(block, DP, [(i, i ^ mask) for i in range(lax.axis_size(DP))])]
    ppermute x47 -> x48, starting transfers between devices: 48.3 us -> 52.6 us  [exchanged(): lax.ppermute(block, DP, [(i, i ^ mask) for i in range(lax.axis_size(DP))])]
    convert_element_type x3 -> x4, other arithmetic: 7.53 us -> 10.7 us  [column(): return jnp.concatenate(parts, axis=0).astype(jnp.bfloat16)]
    unnamed x288 -> x268, local copies, waits for them, and re-layouts: 27.8 us -> 28.8 us
  transfers between devices with their start and end apart: 59 -> 60, of which waited for: 29 -> 28; matrix products, arithmetic and copies ran while one was open for 23% -> 24% of each run, Pallas kernels for 20% -> 21%
where the time goes in v2:
time: 464 us; the launch traced here: 457 us
  waiting for transfers between devices  135 us (29%)
  Pallas kernels  101 us (22%)
  other arithmetic  77.5 us (17%)
  starting transfers between devices  67.2 us (14%)
  local copies, waits for them, and re-layouts  42.2 us (9%)
  matrix products  17.4 us (4%)
  between operations  16.6 us (4%)
    ppermute x48, waiting for transfers between devices, exchanged(): lax.ppermute(block, DP, [(i, i ^ mask) for i in range(lax.axis_size(DP))])  120 us
    ppermute x48, starting transfers between devices, exchanged(): lax.ppermute(block, DP, [(i, i ^ mask) for i in range(lax.axis_size(DP))])  52.6 us
    pallas_call x2, Pallas kernels, reverse_main(): pl.pallas_call(functools.partial(reverse_kernel, len(into)), grid=(channe...  35.6 us
    unnamed x268, local copies, waits for them, and re-layouts  28.8 us
    pallas_call x2, Pallas kernels, down(): pl.pallas_call(functools.partial(down_kernel, len(pairs)), grid=(channels...  18.2 us
    dot_general x8, matrix products, dot(): lax.dot_general(left, right, (dims, ((), ())), preferred_element_type=jnp...  17.4 us
    ppermute x7, waiting for transfers between devices, swapped(): return lax.ppermute(block, axis, [(0, 1), (1, 0)])  14.4 us
    pallas_call x1, Pallas kernels, forward_main(): pl.pallas_call(forward_kernel, grid=(seqs, channels // width), in_specs=[...  11.6 us
  transfers between devices with their start and end apart: 60, of which 28 were waited for; matrix products, arithmetic and copies ran while one was open for 24% of the time, Pallas kernels for 21%

profile of v2, /device:TPU:0, one launch (start us, length us, event | category | flops | bytes accessed | tf_op | source)
XLA Modules:
  0.0 457.4 jit_solution(2421177163763521908)
XLA Ops:
  27.3 15.8 %collective-permute-done.4.refs_2_.refs_20_ = bf16[128,2048]{1,0:T(8,128)(2,1)} collective-permute-done((bf16[128,2048]{1,0:T(8,128)(2,1)S(1)}, bf16[128,2048]{1,0:T(8,128)(2,1)}, u32[]{:S(2)}, u32[]{:S(2)}) %collective-permute-start.4) | collective-permute-done | bytes 524320 | tf_op jit(solution)/shard_map/a12/bx0/ppermute | solution.py:502
  43.1 5.2 %collective-permute-done.2.refs_8_.refs_10_ = bf16[160,2048]{1,0:T(8,128)(2,1)S(1)} collective-permute-done((bf16[160,2048]{1,0:T(8,128)(2,1)S(1)}, bf16[160,2048]{1,0:T(8,128)(2,1)S(1)}, u32[]{:S(2)}, u32[]{:S(2)}) %collective-permute-start.2) | collective-permute-done | bytes 655392 | tf_op jit(solution)/shard_map/a8/ppermute | solution.py:502
  56.1 10.6 %collective-permute-done.5.refs_12_.refs_14_ = bf16[160,2048]{1,0:T(8,128)(2,1)S(1)} collective-permute-done((bf16[160,2048]{1,0:T(8,128)(2,1)S(1)}, bf16[160,2048]{1,0:T(8,128)(2,1)S(1)}, u32[]{:S(2)}, u32[]{:S(2)}) %collective-permute-start.5) | collective-permute-done | bytes 655392 | tf_op jit(solution)/shard_map/a12/ppermute | solution.py:502
  69.2 9.1 %collective-permute-done.6.refs_6_.refs_8_ = bf16[160,2048]{1,0:T(8,128)(2,1)S(1)} collective-permute-done((bf16[160,2048]{1,0:T(8,128)(2,1)S(1)}, bf16[160,2048]{1,0:T(8,128)(2,1)S(1)}, u32[]{:S(2)}, u32[]{:S(2)}) %collective-permute-start.6) | collective-permute-done | bytes 655392 | tf_op jit(solution)/shard_map/ax4/ppermute | solution.py:502
  85.4 7.5 %collective-permute-done.14.refs_8_.refs_26_ = bf16[128,2048]{1,0:T(8,128)(2,1)S(1)} collective-permute-done((bf16[128,2048]{1,0:T(8,128)(2,1)S(1)}, bf16[128,2048]{1,0:T(8,128)(2,1)S(1)}, u32[]{:S(2)}, u32[]{:S(2)}) %collective-permute-start.14) | collective-permute-done | bytes 524320 | tf_op jit(solution)/shard_map/as2/b8/ppermute | solution.py:502
  110.8 5.3 %up.2 = bf16[272,2048]{1,0:T(8,128)(2,1)S(1)} custom-call(bf16[272,2048]{1,0:T(8,128)(2,1)S(1)} %fusion.2.x_ref, bf16[160,2048]{1,0:T(8,128)(2,1)S(1)} %pad_maximum_fusion.7.refs_0_.refs_2_, bf16[512,2048]{1,0:T(8,128)(2,1)S(1)} %collective-permute-done.12.refs_1_.refs_5_.refs_9_.refs_13_.refs_3_.refs_7_.refs_11_.refs_15_, bf16[160,2048]{1,0:T(8,128)(2,1)S(1)} %copy-done.28, ...), custom_call_target="tpu_custom_call" | custom-call | tf_op jit(solution)/shard_map/up/pallas_call | solution.py:320
  120.1 4.0 collective-permute-start.27
  130.4 4.3 collective-permute-start.24
  143.2 6.7 %forward_end.1 = f32[2,16,2048]{2,1,0:T(8,128)S(1)} custom-call(f32[2,16,8,2048]{3,2,1,0:T(8,128)S(1)} %get-tuple-element.195.step_ref, f32[2,16,8,2048]{3,2,1,0:T(8,128)S(1)} %copy-done.11, f32[2,128,32,128]{3,2,1,0:T(8,128)S(1)} %broadcast_in_dim.94.b_ref.bc_ref.c_ref, f32[16,2048]{1,0:T(8,128)S(1)} %get-tuple-element.204.rate_ref), custom_call_target="tpu_custom_call" | custom-call | tf_op jit(solution)/shard_map/forward_end/pallas_call | solution.py:226
  166.9 12.5 %collective-permute-done.23 = bf16[2,16,2048]{2,1,0:T(8,128)(2,1)S(1)} collective-permute-done((bf16[2,16,2048]{2,1,0:T(8,128)(2,1)S(1)}, bf16[2,16,2048]{2,1,0:T(8,128)(2,1)S(1)}, u32[]{:S(2)}, u32[]{:S(2)}) %collective-permute-start.23) | collective-permute-done | bytes 131104 | tf_op jit(solution)/shard_map/f3/ppermute | solution.py:502
  179.6 11.6 %forward_main.1 = f32[2,16,8,2048]{3,2,1,0:T(8,128)S(1)} custom-call(f32[2,16,8,2048]{3,2,1,0:T(8,128)S(1)} %copy-done.6, f32[2,16,8,2048]{3,2,1,0:T(8,128)S(1)} %copy-done.11, f32[2,128,32,128]{3,2,1,0:T(8,128)S(1)} %broadcast_in_dim.94.b_ref.bc_ref.c_ref, f32[16,2048]{1,0:T(8,128)S(1)} %get-tuple-element.204.rate_ref, f32[2,16,2048]{2,1,0:T(8,128)S(1)} %fusion.26.enter_ref), custom_call_target="tpu_custom_call" | custom-call | tf_op jit(solution)/shard_map/forward_main/pallas_call | solution.py:252
  198.1 5.9 %up.3 = f32[256,2048]{1,0:T(8,128)S(1)} custom-call(bf16[256,2048]{1,0:T(8,128)(2,1)S(1)} %slice.453.x_ref, bf16[128,2048]{1,0:T(8,128)(2,1)S(1)} %bitcast.181, bf16[512,2048]{1,0:T(8,128)(2,1)S(1)} %collective-permute-done.25.refs_1_.refs_5_.refs_9_.refs_13_.refs_19_.refs_23_.refs_27_.refs_31_, bf16[128,2048]{1,0:T(8,128)(2,1)} %collective-permute-done.4.refs_2_.refs_20_, ...), custom_call_target="tpu_custom_call" | custom-call | tf_op jit(solution)/shard_map/up/pallas_call | solution.py:320
  205.4 5.8 %convolution_convert_fusion = bf16[2048,2048]{1,0:T(8,128)(2,1)} fusion(bf16[256,2048]{1,0:T(8,128)(2,1)S(1)} %fusion.23, bf16[256,2048]{1,0:T(8,128)(2,1)S(1)} %bitcast.171), kind=kOutput, calls=%fused_computation | convolution fusion | flops 2151677952 | bytes 10485760 | tf_op jit(solution)/shard_map/dot_general | solution.py:531
  213.5 5.9 %fusion.71 = f32[256,2048]{1,0:T(8,128)S(1)} fusion(bf16[256,2048]{1,0:T(8,128)(2,1)S(1)} %copy-done.88, bf16[2048,2048]{1,0:T(8,128)(2,1)} %all-gather.2.cloned.1.call-done.refs_1_.refs_2_.refs_3_.refs_4_.refs_5_.refs_6_.refs_7_.refs_8_.refs_9_.refs_10_.refs_11_.refs_12_.refs_13_.refs_14_.refs_15_.refs_16_), kind=kOutput, calls=%fused_computation.213 | convolution fusion | flops 2147483648 | bytes 11534336 | tf_op jit(solution)/shard_map/dot_general | solution.py:531
  223.3 6.9 %reverse_end.1 = f32[2,16,2048]{2,1,0:T(8,128)S(1)} custom-call(f32[2,16,8,2048]{3,2,1,0:T(8,128)S(1)} %copy-done.7, f32[2,16,8,2048]{3,2,1,0:T(8,128)S(1)} %multiply_multiply_fusion.3.grad_ref, f32[2,128,32,128]{3,2,1,0:T(8,128)S(1)} %copy-done.1, f32[16,2048]{1,0:T(8,128)S(1)} %get-tuple-element.204.rate_ref), custom_call_target="tpu_custom_call" | custom-call | tf_op jit(solution)/shard_map/reverse_end/pallas_call | solution.py:239
  231.6 5.1 %outer.2 = (bf16[512,2048]{1,0:T(8,128)(2,1)S(1)}, bf16[512,2048]{1,0:T(8,128)(2,1)}, bf16[512,2048]{1,0:T(8,128)(2,1)}, bf16[512,2048]{1,0:T(8,128)(2,1)}) custom-call(bf16[256,2048]{1,0:T(8,128)(2,1)S(1)} %slice.453.x_ref, bf16[256,2048]{1,0:T(8,128)(2,1)S(1)} %bitcast.173), custom_call_target="tpu_custom_call" | custom-call | tf_op jit(solution)/shard_map/outer/pallas_call | solution.py:407
  239.2 3.9 collective-permute-done.32
  243.4 3.9 add_convert_fusion.2
  252.2 7.8 %down.2 = (f32[256,1024]{1,0:T(8,128)S(1)}, bf16[256,1024]{1,0:T(8,128)(2,1)}) custom-call(bf16[256,2048]{1,0:T(8,128)(2,1)S(1)} %bitcast.172, bf16[2048,2048]{1,0:T(8,128)(2,1)} %all-gather.2.cloned.1.call-done.refs_1_.refs_2_.refs_3_.refs_4_.refs_5_.refs_6_.refs_7_.refs_8_.refs_9_.refs_10_.refs_11_.refs_12_.refs_13_.refs_14_.refs_15_.refs_16_, ...), custom_call_target="tpu_custom_call" | custom-call | tf_op jit(solution)/shard_map/down/pallas_call | solution.py:367
  261.6 6.1 %collective-permute-done.34 = bf16[2,16,2048]{2,1,0:T(8,128)(2,1)} collective-permute-done((bf16[2,16,2048]{2,1,0:T(8,128)(2,1)}, bf16[2,16,2048]{2,1,0:T(8,128)(2,1)}, u32[]{:S(2)}, u32[]{:S(2)}) %collective-permute-start.34) | collective-permute-done | bytes 131104 | tf_op jit(solution)/shard_map/r3/ppermute | solution.py:502
  269.6 17.9 %reverse_main.2 = (f32[2,16,8,2048]{3,2,1,0:T(8,128)}, f32[2,16,8,2048]{3,2,1,0:T(8,128)}, f32[2,128,32,128]{3,2,1,0:T(8,128)}, f32[2,16,2048]{2,1,0:T(8,128)}) custom-call(f32[2,16,8,2048]{3,2,1,0:T(8,128)} %copy-done.5, f32[2,16,8,2048]{3,2,1,0:T(8,128)} %get-tuple-element.194.delta_ref, f32[2,16,8,2048]{3,2,1,0:T(8,128)} %fusion.6.flow_ref, ...), custom_call_target="tpu_custom_call" | custom-call | tf_op jit(solution)/shard_map/reverse_main/pallas_call | solution.py:273
  290.8 17.7 %reverse_main.3 = (f32[2,16,8,2048]{3,2,1,0:T(8,128)}, f32[2,16,8,2048]{3,2,1,0:T(8,128)}, f32[2,128,32,128]{3,2,1,0:T(8,128)}, f32[2,16,2048]{2,1,0:T(8,128)}) custom-call(f32[2,16,8,2048]{3,2,1,0:T(8,128)} %copy-done.5, ...), custom_call_target="tpu_custom_call", output_to_operand_aliasing={{0}: (10, {}), {1}: (11, {}), {2}: (12, {}), {3}: (13, {})} | custom-call | tf_op jit(solution)/shard_map/reverse_main/pallas_call | solution.py:273
  316.8 3.9 collective-permute-done.37
  330.9 5.3 %outer.3 = (bf16[512,2048]{1,0:T(8,128)(2,1)S(1)}, bf16[512,2048]{1,0:T(8,128)(2,1)}, bf16[512,2048]{1,0:T(8,128)(2,1)}, bf16[512,2048]{1,0:T(8,128)(2,1)}) custom-call(bf16[256,2048]{1,0:T(8,128)(2,1)S(1)} %slice.453.x_ref, bf16[256,2048]{1,0:T(8,128)(2,1)S(1)} %bitcast.175), custom_call_target="tpu_custom_call" | custom-call | tf_op jit(solution)/shard_map/outer/pallas_call | solution.py:407
  344.9 4.4 add_convert_fusion
  349.4 5.1 %collective-permute-start.44 = (bf16[256,2048]{1,0:T(8,128)(2,1)}, bf16[256,2048]{1,0:T(8,128)(2,1)}, u32[]{:S(2)}, u32[]{:S(2)}) collective-permute-start(bf16[256,2048]{1,0:T(8,128)(2,1)} %get-tuple-element.183), channel_id=1, source_target_pairs={{0,4},{2,6},{4,0},{6,2},{8,12},{10,14},{12,8},{14,10},{16,20},{18,... | collective-permute-start | bytes 3145736 | tf_op jit(solution)/shard_map/yn/Ax4/ppermute | solution.py:502
  361.3 10.4 %down.3 = (f32[256,1024]{1,0:T(8,128)}, bf16[256,1024]{1,0:T(8,128)(2,1)S(1)}) custom-call(bf16[256,2048]{1,0:T(8,128)(2,1)} %bitcast.176, bf16[256,2048]{1,0:T(8,128)(2,1)} %bitcast.174, bf16[160,2048]{1,0:T(8,128)(2,1)S(1)} %copy-done.26, bf16[512,2048]{1,0:T(8,128)(2,1)} %copy-done.2, bf16[160,2048]{1,0:T(8,128)(2,1)S(1)} %copy-done.29, ...), custom_call_target="tpu_custom_call" | custom-call | tf_op jit(solution)/shard_map/down/pallas_call | solution.py:367
  371.7 11.9 %collective-permute-done.45 = bf16[128,2048]{1,0:T(8,128)(2,1)} collective-permute-done((bf16[128,2048]{1,0:T(8,128)(2,1)}, bf16[128,2048]{1,0:T(8,128)(2,1)}, u32[]{:S(2)}, u32[]{:S(2)}) %collective-permute-start.45) | collective-permute-done | bytes 524320 | tf_op jit(solution)/shard_map/yn/Bz8/ppermute | solution.py:502
  389.1 8.0 %collective-permute-done.46 = bf16[256,1024]{1,0:T(8,128)(2,1)S(1)} collective-permute-done((bf16[256,1024]{1,0:T(8,128)(2,1)S(1)}, bf16[256,1024]{1,0:T(8,128)(2,1)S(1)}, u32[]{:S(2)}, u32[]{:S(2)}) %collective-permute-start.46) | collective-permute-done | bytes 524320 | tf_op jit(solution)/shard_map/yn/ppermute | solution.py:498
  414.6 5.7 %collective-permute-done.49 = bf16[4,320,128]{2,1,0:T(8,128)(2,1)S(1)} collective-permute-done((bf16[4,320,128]{2,1,0:T(8,128)(2,1)S(1)}, bf16[4,320,128]{2,1,0:T(8,128)(2,1)S(1)}, u32[]{:S(2)}, u32[]{:S(2)}) %collective-permute-start.49) | collective-permute-done | bytes 327712 | tf_op jit(solution)/shard_map/k1/ppermute | solution.py:502
  421.2 4.9 %collective-permute-done.56 = bf16[128,2048]{1,0:T(8,128)(2,1)S(1)} collective-permute-done((bf16[128,2048]{1,0:T(8,128)(2,1)S(1)}, bf16[128,2048]{1,0:T(8,128)(2,1)S(1)}, u32[]{:S(2)}, u32[]{:S(2)}) %collective-permute-start.56) | collective-permute-done | bytes 524320 | tf_op jit(solution)/shard_map/Az4/ppermute | solution.py:502
  426.2 10.3 %collective-permute-done.55 = bf16[128,2048]{1,0:T(8,128)(2,1)S(1)} collective-permute-done((bf16[128,2048]{1,0:T(8,128)(2,1)S(1)}, bf16[128,2048]{1,0:T(8,128)(2,1)S(1)}, u32[]{:S(2)}, u32[]{:S(2)}) %collective-permute-start.55) | collective-permute-done | bytes 524320 | tf_op jit(solution)/shard_map/Az8/ppermute | solution.py:502
  (491 shorter events, 191.2 us)
Async XLA Ops:
  7.2 205.1 %all-gather.2.cloned.1.call-start = ((), (), s32[]{:S(2)}) async-start(), calls=%async_computation.1 | async-start | bytes 8912896 | tf_op jit(solution)/shard_map/all_gather | solution.py:1071
  14.0 29.1 %collective-permute-start.3 = (bf16[160,2048]{1,0:T(8,128)(2,1)S(1)}, bf16[160,2048]{1,0:T(8,128)(2,1)S(1)}, u32[]{:S(2)}, u32[]{:S(2)}) collective-permute-start(bf16[160,2048]{1,0:T(8,128)(2,1)S(1)} %pad_maximum_fusion.7.refs_0_.refs_2_), channel_id=1, source_target_pairs={{0,4},{2,6},{4,0},{6,2},{8,12},{10,14},{12,8},{14,10},{16,20},{18,... | collective-permute-start | bytes 1966088 | tf_op jit(solution)/shard_map/y0/ax0/ppermute | solution.py:502
  17.0 31.2 %collective-permute-start.2 = (bf16[160,2048]{1,0:T(8,128)(2,1)S(1)}, bf16[160,2048]{1,0:T(8,128)(2,1)S(1)}, u32[]{:S(2)}, u32[]{:S(2)}) collective-permute-start(bf16[160,2048]{1,0:T(8,128)(2,1)S(1)} %pad_maximum_fusion.7.refs_0_.refs_2_), channel_id=1, source_target_pairs={{0,16},{2,18},{4,20},{6,22},{8,24},{10,26},{12,28},{14,30},{16,0},... | collective-permute-start | bytes 1966088 | tf_op jit(solution)/shard_map/a8/ppermute | solution.py:502
  19.6 28.8 %collective-permute-start.1 = (bf16[160,2048]{1,0:T(8,128)(2,1)S(1)}, bf16[160,2048]{1,0:T(8,128)(2,1)S(1)}, u32[]{:S(2)}, u32[]{:S(2)}) collective-permute-start(bf16[160,2048]{1,0:T(8,128)(2,1)S(1)} %pad_maximum_fusion.7.refs_0_.refs_2_), channel_id=1, source_target_pairs={{0,8},{2,10},{4,12},{6,14},{8,0},{10,2},{12,4},{14,6},{16,24},{18,... | collective-permute-start | bytes 1966088 | tf_op jit(solution)/shard_map/a4/ppermute | solution.py:502
  21.5 21.6 %collective-permute-start.4 = (bf16[128,2048]{1,0:T(8,128)(2,1)S(1)}, bf16[128,2048]{1,0:T(8,128)(2,1)}, u32[]{:S(2)}, u32[]{:S(2)}) collective-permute-start(bf16[128,2048]{1,0:T(8,128)(2,1)S(1)} %bitcast.177), channel_id=1, source_target_pairs={{0,4},{2,6},{4,0},{6,2},{8,12},{10,14},{12,8},{14,10},{16,20},{18,... | collective-permute-start | bytes 1572872 | tf_op jit(solution)/shard_map/a12/bx0/ppermute | solution.py:502
  48.4 20.7 %collective-permute-start.7 = (bf16[160,2048]{1,0:T(8,128)(2,1)S(1)}, bf16[160,2048]{1,0:T(8,128)(2,1)S(1)}, u32[]{:S(2)}, u32[]{:S(2)}) collective-permute-start(bf16[160,2048]{1,0:T(8,128)(2,1)S(1)} %collective-permute-done.2.refs_8_.refs_10_), channel_id=1, source_target_pairs={{0,4},{2,6},{4,0},{6,2},{8,12},{10,14},{12,8},{14,10},{16,20},{18,... | collective-permute-start | bytes 1966088 | tf_op jit(solution)/shard_map/ax8/ppermute | solution.py:502
  48.9 17.9 %collective-permute-start.5 = (bf16[160,2048]{1,0:T(8,128)(2,1)S(1)}, bf16[160,2048]{1,0:T(8,128)(2,1)S(1)}, u32[]{:S(2)}, u32[]{:S(2)}) collective-permute-start(bf16[160,2048]{1,0:T(8,128)(2,1)S(1)} %collective-permute-done.2.refs_8_.refs_10_), channel_id=1, source_target_pairs={{0,8},{2,10},{4,12},{6,14},{8,0},{10,2},{12,4},{14,6},{16,24},{18,... | collective-permute-start | bytes 1966088 | tf_op jit(solution)/shard_map/a12/ppermute | solution.py:502
  51.2 27.1 %collective-permute-start.6 = (bf16[160,2048]{1,0:T(8,128)(2,1)S(1)}, bf16[160,2048]{1,0:T(8,128)(2,1)S(1)}, u32[]{:S(2)}, u32[]{:S(2)}) collective-permute-start(bf16[160,2048]{1,0:T(8,128)(2,1)S(1)} %collective-permute-done.1.refs_4_.refs_6_), channel_id=1, source_target_pairs={{0,4},{2,6},{4,0},{6,2},{8,12},{10,14},{12,8},{14,10},{16,20},{18,... | collective-permute-start | bytes 1966088 | tf_op jit(solution)/shard_map/ax4/ppermute | solution.py:502
  53.2 48.9 %collective-permute-start.11 = (bf16[528,1024]{1,0:T(8,128)(2,1)}, bf16[528,1024]{1,0:T(8,128)(2,1)}, u32[]{:S(2)}, u32[]{:S(2)}) collective-permute-start(bf16[528,1024]{1,0:T(8,128)(2,1)} %fusion.17), channel_id=1, source_target_pairs={{0,1},{1,0},{2,3},{3,2},{4,5},{5,4},{6,7},{7,6},{8,9},{9,8},{10,11... | collective-permute-start | bytes 3244040 | tf_op jit(solution)/shard_map/y0/ppermute | solution.py:498
  66.8 26.1 %collective-permute-start.14 = (bf16[128,2048]{1,0:T(8,128)(2,1)S(1)}, bf16[128,2048]{1,0:T(8,128)(2,1)S(1)}, u32[]{:S(2)}, u32[]{:S(2)}) collective-permute-start(bf16[128,2048]{1,0:T(8,128)(2,1)S(1)} %bitcast.178), channel_id=1, source_target_pairs={{0,16},{2,18},{4,20},{6,22},{8,24},{10,26},{12,28},{14,30},{16,0},... | collective-permute-start | bytes 1572872 | tf_op jit(solution)/shard_map/as2/b8/ppermute | solution.py:502
  67.4 25.5 %collective-permute-start.13 = (bf16[128,2048]{1,0:T(8,128)(2,1)S(1)}, bf16[128,2048]{1,0:T(8,128)(2,1)}, u32[]{:S(2)}, u32[]{:S(2)}) collective-permute-start(bf16[128,2048]{1,0:T(8,128)(2,1)S(1)} %bitcast.179), channel_id=1, source_target_pairs={{0,8},{2,10},{4,12},{6,14},{8,0},{10,2},{12,4},{14,6},{16,24},{18,... | collective-permute-start | bytes 1572872 | tf_op jit(solution)/shard_map/as2/b4/ppermute | solution.py:502
  81.7 27.2 %collective-permute-start.12 = (bf16[512,2048]{1,0:T(8,128)(2,1)}, bf16[512,2048]{1,0:T(8,128)(2,1)S(1)}, u32[]{:S(2)}, u32[]{:S(2)}) collective-permute-start(bf16[512,2048]{1,0:T(8,128)(2,1)} %pad_maximum_fusion.1), channel_id=1, source_target_pairs={{0,2},{2,0},{4,6},{6,4},{8,10},{10,8},{12,14},{14,12},{16,18},{18,... | collective-permute-start | bytes 6291464 | tf_op jit(solution)/shard_map/as0/ppermute | solution.py:502
  117.2 224.2 %reduce-scatter.2.cloned.1.call-start = ((), (), s32[]{:S(2)}) async-start(), calls=%async_computation.2 | async-start | bytes 8912896 | tf_op jit(solution)/shard_map/reduce_scatter | solution.py:1176
  120.1 71.1 %collective-permute-start.27 = (bf16[128,2048]{1,0:T(8,128)(2,1)}, bf16[128,2048]{1,0:T(8,128)(2,1)}, u32[]{:S(2)}, u32[]{:S(2)}) collective-permute-start(bf16[128,2048]{1,0:T(8,128)(2,1)} %copy-done.42), channel_id=1, source_target_pairs={{0,4},{2,6},{4,0},{6,2},{8,12},{10,14},{12,8},{14,10},{16,20},{18,... | collective-permute-start | bytes 1572872 | tf_op jit(solution)/shard_map/bs2/bx8/ppermute | solution.py:502
  130.4 60.9 %collective-permute-start.26 = (bf16[128,2048]{1,0:T(8,128)(2,1)}, bf16[128,2048]{1,0:T(8,128)(2,1)}, u32[]{:S(2)}, u32[]{:S(2)}) collective-permute-start(bf16[128,2048]{1,0:T(8,128)(2,1)} %collective-permute-done.13.refs_4_.refs_22_), channel_id=1, source_target_pairs={{0,4},{2,6},{4,0},{6,2},{8,12},{10,14},{12,8},{14,10},{16,20},{18,... | collective-permute-start | bytes 1572872 | tf_op jit(solution)/shard_map/bs2/bx4/ppermute | solution.py:502
  130.4 29.8 %collective-permute-start.24 = (bf16[128,2048]{1,0:T(8,128)(2,1)S(1)}, bf16[128,2048]{1,0:T(8,128)(2,1)}, u32[]{:S(2)}, u32[]{:S(2)}) collective-permute-start(bf16[128,2048]{1,0:T(8,128)(2,1)S(1)} %copy-done.43), channel_id=1, source_target_pairs={{0,8},{2,10},{4,12},{6,14},{8,0},{10,2},{12,4},{14,6},{16,24},{18,... | collective-permute-start | bytes 1572872 | tf_op jit(solution)/shard_map/bs0/b12/ppermute | solution.py:502
  160.2 31.0 %collective-permute-start.28 = (bf16[128,2048]{1,0:T(8,128)(2,1)}, bf16[128,2048]{1,0:T(8,128)(2,1)S(1)}, u32[]{:S(2)}, u32[]{:S(2)}) collective-permute-start(bf16[128,2048]{1,0:T(8,128)(2,1)} %collective-permute-done.24.refs_12_.refs_30_), channel_id=1, source_target_pairs={{0,4},{2,6},{4,0},{6,2},{8,12},{10,14},{12,8},{14,10},{16,20},{18,... | collective-permute-start | bytes 1572872 | tf_op jit(solution)/shard_map/bs2/bx12/ppermute | solution.py:502
  166.9 28.4 %collective-permute-start.25 = (bf16[512,2048]{1,0:T(8,128)(2,1)}, bf16[512,2048]{1,0:T(8,128)(2,1)S(1)}, u32[]{:S(2)}, u32[]{:S(2)}) collective-permute-start(bf16[512,2048]{1,0:T(8,128)(2,1)} %pad_maximum_fusion.3), channel_id=1, source_target_pairs={{0,2},{2,0},{4,6},{6,4},{8,10},{10,8},{12,14},{14,12},{16,18},{18,... | collective-permute-start | bytes 6291464 | tf_op jit(solution)/shard_map/bs0/ppermute | solution.py:502
  239.1 48.6 %collective-permute-start.39 = (bf16[512,2048]{1,0:T(8,128)(2,1)}, bf16[512,2048]{1,0:T(8,128)(2,1)}, u32[]{:S(2)}, u32[]{:S(2)}) collective-permute-start(bf16[512,2048]{1,0:T(8,128)(2,1)} %get-tuple-element.107), channel_id=1, source_target_pairs={{0,2},{2,0},{4,6},{6,4},{8,10},{10,8},{12,14},{14,12},{16,18},{18,... | collective-permute-start | bytes 6291464 | tf_op jit(solution)/shard_map/Bz12/Bs0/ppermute | solution.py:502
  247.3 40.4 %collective-permute-start.36 = (bf16[256,2048]{1,0:T(8,128)(2,1)}, bf16[256,2048]{1,0:T(8,128)(2,1)}, u32[]{:S(2)}, u32[]{:S(2)}) collective-permute-start(bf16[256,2048]{1,0:T(8,128)(2,1)} %get-tuple-element.185), channel_id=1, source_target_pairs={{0,4},{2,6},{4,0},{6,2},{8,12},{10,14},{12,8},{14,10},{16,20},{18,... | collective-permute-start | bytes 3145736 | tf_op jit(solution)/shard_map/Bx4/ppermute | solution.py:502
  249.9 17.8 %collective-permute-start.34 = (bf16[2,16,2048]{2,1,0:T(8,128)(2,1)}, bf16[2,16,2048]{2,1,0:T(8,128)(2,1)}, u32[]{:S(2)}, u32[]{:S(2)}) collective-permute-start(bf16[2,16,2048]{2,1,0:T(8,128)(2,1)} %fusion.46), channel_id=1, source_target_pairs={{0,16},{2,18},{4,20},{6,22},{8,24},{10,26},{12,28},{14,30},{16,0},... | collective-permute-start | bytes 393224 | tf_op jit(solution)/shard_map/r3/ppermute | solution.py:502
  260.0 60.7 %collective-permute-start.31 = (bf16[256,1024]{1,0:T(8,128)(2,1)}, bf16[256,1024]{1,0:T(8,128)(2,1)}, u32[]{:S(2)}, u32[]{:S(2)}) collective-permute-start(bf16[256,1024]{1,0:T(8,128)(2,1)} %get-tuple-element.94), channel_id=1, source_target_pairs={{0,1},{1,0},{2,3},{3,2},{4,5},{5,4},{6,7},{7,6},{8,9},{9,8},{10,11... | collective-permute-start | bytes 1572872 | tf_op jit(solution)/shard_map/yb/ppermute | solution.py:498
  287.6 33.1 %collective-permute-start.38 = (bf16[256,2048]{1,0:T(8,128)(2,1)}, bf16[256,2048]{1,0:T(8,128)(2,1)}, u32[]{:S(2)}, u32[]{:S(2)}) collective-permute-start(bf16[256,2048]{1,0:T(8,128)(2,1)} %get-tuple-element.184), channel_id=1, source_target_pairs={{0,4},{2,6},{4,0},{6,2},{8,12},{10,14},{12,8},{14,10},{16,20},{18,... | collective-permute-start | bytes 3145736 | tf_op jit(solution)/shard_map/Bx0/ppermute | solution.py:502
  290.8 29.9 %collective-permute-start.40 = (bf16[128,2048]{1,0:T(8,128)(2,1)}, bf16[128,2048]{1,0:T(8,128)(2,1)}, u32[]{:S(2)}, u32[]{:S(2)}) collective-permute-start(bf16[128,2048]{1,0:T(8,128)(2,1)} %get-tuple-element.181), channel_id=1, source_target_pairs={{0,8},{2,10},{4,12},{6,14},{8,0},{10,2},{12,4},{14,6},{16,24},{18,... | collective-permute-start | bytes 1572872 | tf_op jit(solution)/shard_map/Bz12/ppermute | solution.py:502
  341.4 19.8 %collective-permute-start.43 = (bf16[512,2048]{1,0:T(8,128)(2,1)}, bf16[512,2048]{1,0:T(8,128)(2,1)}, u32[]{:S(2)}, u32[]{:S(2)}) collective-permute-start(bf16[512,2048]{1,0:T(8,128)(2,1)} %get-tuple-element.111), channel_id=1, source_target_pairs={{0,2},{2,0},{4,6},{6,4},{8,10},{10,8},{12,14},{14,12},{16,18},{18,... | collective-permute-start | bytes 6291464 | tf_op jit(solution)/shard_map/As0/ppermute | solution.py:502
  349.4 34.2 %collective-permute-start.44 = (bf16[256,2048]{1,0:T(8,128)(2,1)}, bf16[256,2048]{1,0:T(8,128)(2,1)}, u32[]{:S(2)}, u32[]{:S(2)}) collective-permute-start(bf16[256,2048]{1,0:T(8,128)(2,1)} %get-tuple-element.183), channel_id=1, source_target_pairs={{0,4},{2,6},{4,0},{6,2},{8,12},{10,14},{12,8},{14,10},{16,20},{18,... | collective-permute-start | bytes 3145736 | tf_op jit(solution)/shard_map/yn/Ax4/ppermute | solution.py:502
  357.2 26.4 %collective-permute-start.45 = (bf16[128,2048]{1,0:T(8,128)(2,1)}, bf16[128,2048]{1,0:T(8,128)(2,1)}, u32[]{:S(2)}, u32[]{:S(2)}) collective-permute-start(bf16[128,2048]{1,0:T(8,128)(2,1)} %add_convert_fusion.8), channel_id=1, source_target_pairs={{0,16},{2,18},{4,20},{6,22},{8,24},{10,26},{12,28},{14,30},{16,0},... | collective-permute-start | bytes 1572872 | tf_op jit(solution)/shard_map/yn/Bz8/ppermute | solution.py:502
  358.6 45.1 %collective-permute-start.57 = (bf16[128,2048]{1,0:T(8,128)(2,1)}, bf16[128,2048]{1,0:T(8,128)(2,1)}, u32[]{:S(2)}, u32[]{:S(2)}) collective-permute-start(bf16[128,2048]{1,0:T(8,128)(2,1)} %get-tuple-element.180), channel_id=1, source_target_pairs={{0,8},{2,10},{4,12},{6,14},{8,0},{10,2},{12,4},{14,6},{16,24},{18,... | collective-permute-start | bytes 1572872 | tf_op jit(solution)/shard_map/Bz4/ppermute | solution.py:502
  385.4 24.8 %collective-permute-start.53 = (bf16[256,2048]{1,0:T(8,128)(2,1)}, bf16[256,2048]{1,0:T(8,128)(2,1)}, u32[]{:S(2)}, u32[]{:S(2)}) collective-permute-start(bf16[256,2048]{1,0:T(8,128)(2,1)} %get-tuple-element.120), channel_id=1, source_target_pairs={{0,4},{2,6},{4,0},{6,2},{8,12},{10,14},{12,8},{14,10},{16,20},{18,... | collective-permute-start | bytes 3145736 | tf_op jit(solution)/shard_map/Az8/Ax0/ppermute | solution.py:502
  389.1 21.1 %collective-permute-start.54 = (bf16[128,2048]{1,0:T(8,128)(2,1)}, bf16[128,2048]{1,0:T(8,128)(2,1)}, u32[]{:S(2)}, u32[]{:S(2)}) collective-permute-start(bf16[128,2048]{1,0:T(8,128)(2,1)} %get-tuple-element.121), channel_id=1, source_target_pairs={{0,8},{2,10},{4,12},{6,14},{8,0},{10,2},{12,4},{14,6},{16,24},{18,... | collective-permute-start | bytes 1572872 | tf_op jit(solution)/shard_map/Az8/Az12/ppermute | solution.py:502
  406.0 20.2 %collective-permute-start.56 = (bf16[128,2048]{1,0:T(8,128)(2,1)S(1)}, bf16[128,2048]{1,0:T(8,128)(2,1)S(1)}, u32[]{:S(2)}, u32[]{:S(2)}) collective-permute-start(bf16[128,2048]{1,0:T(8,128)(2,1)S(1)} %copy-done.99), channel_id=1, source_target_pairs={{0,8},{2,10},{4,12},{6,14},{8,0},{10,2},{12,4},{14,6},{16,24},{18,... | collective-permute-start | bytes 1572872 | tf_op jit(solution)/shard_map/Az4/ppermute | solution.py:502
  411.9 24.5 %collective-permute-start.55 = (bf16[128,2048]{1,0:T(8,128)(2,1)S(1)}, bf16[128,2048]{1,0:T(8,128)(2,1)S(1)}, u32[]{:S(2)}, u32[]{:S(2)}) collective-permute-start(bf16[128,2048]{1,0:T(8,128)(2,1)S(1)} %add_convert_fusion.6), channel_id=1, source_target_pairs={{0,16},{2,18},{4,20},{6,22},{8,24},{10,26},{12,28},{14,30},{16,0},... | collective-permute-start | bytes 1572872 | tf_op jit(solution)/shard_map/Az8/ppermute | solution.py:502
  (160 other events, 1600.1 us)
Sparse Core Ops, SparseCore 0:
  117.3 93.8 all-gather.1
  215.3 124.1 reduce-scatter.1

commit v3 on v2

--- a/solution.py
+++ b/solution.py
@@ -994,12 +994,13 @@
     Bz8=(N.Ap4,),
     down=(N.Ap4, N.As0),
     Ax0=(N.Ap4,),
-    yn=(N.Ax4, N.Bz8),
+    yn=(N.Ax4,),
     y0=(N.ax0,),
     bs2=(N.readout,),
     grad_pre=(N.Bx4,),
     Az12=(N.As0,),
     ae=(N.ax8,),
+    grad_normed=(N.Bz8,),
 )
 GROUPS = dict(
     a=((0,), (4,), (8,), (12,)),

time: 464 us -> 459 us (0.989)
  waiting for transfers between devices: 135 us -> 125 us
    ppermute x7, waiting for transfers between devices: 14.4 us -> 7 us  [swapped(): return lax.ppermute(block, axis, [(0, 1), (1, 0)])]
    unnamed x268 -> x272, local copies, waits for them, and re-layouts: 28.8 us -> 29 us
  transfers between devices with their start and end apart: 60 -> 60, of which waited for: 28 -> 28; matrix products, arithmetic and copies ran while one was open for 24% -> 25% of each run, Pallas kernels for 21% -> 21%
where the time goes in v3:
time: 459 us; the launch traced here: 452 us
  waiting for transfers between devices  125 us (27%)
  Pallas kernels  101 us (22%)
  other arithmetic  78.3 us (17%)
  starting transfers between devices  70 us (15%)
  local copies, waits for them, and re-layouts  45.4 us (10%)
  between operations  16.5 us (4%)
  matrix products  16.4 us (4%)
    ppermute x48, waiting for transfers between devices, exchanged(): lax.ppermute(block, DP, [(i, i ^ mask) for i in range(lax.axis_size(DP))])  116 us
    ppermute x48, starting transfers between devices, exchanged(): lax.ppermute(block, DP, [(i, i ^ mask) for i in range(lax.axis_size(DP))])  55.5 us
    pallas_call x2, Pallas kernels, reverse_main(): pl.pallas_call(functools.partial(reverse_kernel, len(into)), grid=(channe...  35.6 us
    unnamed x272, local copies, waits for them, and re-layouts  29 us
    pallas_call x2, Pallas kernels, down(): pl.pallas_call(functools.partial(down_kernel, len(pairs)), grid=(channels...  18.1 us
    dot_general x8, matrix products, dot(): lax.dot_general(left, right, (dims, ((), ())), preferred_element_type=jnp...  16.4 us
    pallas_call x1, Pallas kernels, forward_main(): pl.pallas_call(forward_kernel, grid=(seqs, channels // width), in_specs=[...  11.6 us
    pallas_call x2, Pallas kernels, up(): pl.pallas_call(up_kernel, grid=(channels // width,), in_specs=[pl.BlockSp...  11.3 us
  transfers between devices with their start and end apart: 60, of which 28 were waited for; matrix products, arithmetic and copies ran while one was open for 25% of the time, Pallas kernels for 21%

profile of v3, /device:TPU:0, one launch (start us, length us, event | category | flops | bytes accessed | tf_op | source)
XLA Modules:
  0.0 452.0 jit_solution(4670934503841482878)
XLA Ops:
  27.3 15.8 %collective-permute-done.4.refs_2_.refs_20_ = bf16[128,2048]{1,0:T(8,128)(2,1)} collective-permute-done((bf16[128,2048]{1,0:T(8,128)(2,1)S(1)}, bf16[128,2048]{1,0:T(8,128)(2,1)}, u32[]{:S(2)}, u32[]{:S(2)}) %collective-permute-start.4) | collective-permute-done | bytes 524320 | tf_op jit(solution)/shard_map/a12/bx0/ppermute | solution.py:502
  43.1 5.2 %collective-permute-done.2.refs_8_.refs_10_ = bf16[160,2048]{1,0:T(8,128)(2,1)S(1)} collective-permute-done((bf16[160,2048]{1,0:T(8,128)(2,1)S(1)}, bf16[160,2048]{1,0:T(8,128)(2,1)S(1)}, u32[]{:S(2)}, u32[]{:S(2)}) %collective-permute-start.2) | collective-permute-done | bytes 655392 | tf_op jit(solution)/shard_map/a8/ppermute | solution.py:502
  56.1 10.6 %collective-permute-done.5.refs_12_.refs_14_ = bf16[160,2048]{1,0:T(8,128)(2,1)S(1)} collective-permute-done((bf16[160,2048]{1,0:T(8,128)(2,1)S(1)}, bf16[160,2048]{1,0:T(8,128)(2,1)S(1)}, u32[]{:S(2)}, u32[]{:S(2)}) %collective-permute-start.5) | collective-permute-done | bytes 655392 | tf_op jit(solution)/shard_map/a12/ppermute | solution.py:502
  69.2 9.1 %collective-permute-done.6.refs_6_.refs_8_ = bf16[160,2048]{1,0:T(8,128)(2,1)S(1)} collective-permute-done((bf16[160,2048]{1,0:T(8,128)(2,1)S(1)}, bf16[160,2048]{1,0:T(8,128)(2,1)S(1)}, u32[]{:S(2)}, u32[]{:S(2)}) %collective-permute-start.6) | collective-permute-done | bytes 655392 | tf_op jit(solution)/shard_map/ax4/ppermute | solution.py:502
  85.4 7.5 %collective-permute-done.14.refs_8_.refs_26_ = bf16[128,2048]{1,0:T(8,128)(2,1)S(1)} collective-permute-done((bf16[128,2048]{1,0:T(8,128)(2,1)S(1)}, bf16[128,2048]{1,0:T(8,128)(2,1)S(1)}, u32[]{:S(2)}, u32[]{:S(2)}) %collective-permute-start.14) | collective-permute-done | bytes 524320 | tf_op jit(solution)/shard_map/as2/b8/ppermute | solution.py:502
  110.8 5.3 %up.2 = bf16[272,2048]{1,0:T(8,128)(2,1)S(1)} custom-call(bf16[272,2048]{1,0:T(8,128)(2,1)S(1)} %fusion.2.x_ref, bf16[160,2048]{1,0:T(8,128)(2,1)S(1)} %pad_maximum_fusion.7.refs_0_.refs_2_, bf16[512,2048]{1,0:T(8,128)(2,1)S(1)} %collective-permute-done.12.refs_1_.refs_5_.refs_9_.refs_13_.refs_3_.refs_7_.refs_11_.refs_15_, bf16[160,2048]{1,0:T(8,128)(2,1)S(1)} %copy-done.28, ...), custom_call_target="tpu_custom_call" | custom-call | tf_op jit(solution)/shard_map/up/pallas_call | solution.py:320
  120.2 4.0 collective-permute-start.27
  130.4 4.3 collective-permute-start.24
  143.3 6.7 %forward_end.1 = f32[2,16,2048]{2,1,0:T(8,128)S(1)} custom-call(f32[2,16,8,2048]{3,2,1,0:T(8,128)S(1)} %get-tuple-element.195.step_ref, f32[2,16,8,2048]{3,2,1,0:T(8,128)S(1)} %copy-done.11, f32[2,128,32,128]{3,2,1,0:T(8,128)S(1)} %broadcast_in_dim.94.b_ref.bc_ref.c_ref, f32[16,2048]{1,0:T(8,128)S(1)} %get-tuple-element.204.rate_ref), custom_call_target="tpu_custom_call" | custom-call | tf_op jit(solution)/shard_map/forward_end/pallas_call | solution.py:226
  166.9 12.5 %collective-permute-done.23 = bf16[2,16,2048]{2,1,0:T(8,128)(2,1)S(1)} collective-permute-done((bf16[2,16,2048]{2,1,0:T(8,128)(2,1)S(1)}, bf16[2,16,2048]{2,1,0:T(8,128)(2,1)S(1)}, u32[]{:S(2)}, u32[]{:S(2)}) %collective-permute-start.23) | collective-permute-done | bytes 131104 | tf_op jit(solution)/shard_map/f3/ppermute | solution.py:502
  179.6 11.6 %forward_main.1 = f32[2,16,8,2048]{3,2,1,0:T(8,128)S(1)} custom-call(f32[2,16,8,2048]{3,2,1,0:T(8,128)S(1)} %copy-done.6, f32[2,16,8,2048]{3,2,1,0:T(8,128)S(1)} %copy-done.11, f32[2,128,32,128]{3,2,1,0:T(8,128)S(1)} %broadcast_in_dim.94.b_ref.bc_ref.c_ref, f32[16,2048]{1,0:T(8,128)S(1)} %get-tuple-element.204.rate_ref, f32[2,16,2048]{2,1,0:T(8,128)S(1)} %fusion.26.enter_ref), custom_call_target="tpu_custom_call" | custom-call | tf_op jit(solution)/shard_map/forward_main/pallas_call | solution.py:252
  198.2 5.9 %up.3 = f32[256,2048]{1,0:T(8,128)S(1)} custom-call(bf16[256,2048]{1,0:T(8,128)(2,1)S(1)} %slice.453.x_ref, bf16[128,2048]{1,0:T(8,128)(2,1)S(1)} %bitcast.181, bf16[512,2048]{1,0:T(8,128)(2,1)S(1)} %collective-permute-done.25.refs_1_.refs_5_.refs_9_.refs_13_.refs_19_.refs_23_.refs_27_.refs_31_, bf16[128,2048]{1,0:T(8,128)(2,1)} %collective-permute-done.4.refs_2_.refs_20_, ...), custom_call_target="tpu_custom_call" | custom-call | tf_op jit(solution)/shard_map/up/pallas_call | solution.py:320
  205.5 5.8 %convolution_convert_fusion = bf16[2048,2048]{1,0:T(8,128)(2,1)} fusion(bf16[256,2048]{1,0:T(8,128)(2,1)S(1)} %fusion.23, bf16[256,2048]{1,0:T(8,128)(2,1)S(1)} %bitcast.171), kind=kOutput, calls=%fused_computation | convolution fusion | flops 2151677952 | bytes 10485760 | tf_op jit(solution)/shard_map/dot_general | solution.py:531
  213.5 5.9 %fusion.71 = f32[256,2048]{1,0:T(8,128)S(1)} fusion(bf16[256,2048]{1,0:T(8,128)(2,1)S(1)} %copy-done.89, bf16[2048,2048]{1,0:T(8,128)(2,1)} %all-gather.2.cloned.1.call-done.refs_1_.refs_2_.refs_3_.refs_4_.refs_5_.refs_6_.refs_7_.refs_8_.refs_9_.refs_10_.refs_11_.refs_12_.refs_13_.refs_14_.refs_15_.refs_16_), kind=kOutput, calls=%fused_computation.213 | convolution fusion | flops 2147483648 | bytes 11534336 | tf_op jit(solution)/shard_map/dot_general | solution.py:531
  223.3 6.9 %reverse_end.1 = f32[2,16,2048]{2,1,0:T(8,128)S(1)} custom-call(f32[2,16,8,2048]{3,2,1,0:T(8,128)S(1)} %copy-done.7, f32[2,16,8,2048]{3,2,1,0:T(8,128)S(1)} %multiply_multiply_fusion.3.grad_ref, f32[2,128,32,128]{3,2,1,0:T(8,128)S(1)} %copy-done.1, f32[16,2048]{1,0:T(8,128)S(1)} %get-tuple-element.204.rate_ref), custom_call_target="tpu_custom_call" | custom-call | tf_op jit(solution)/shard_map/reverse_end/pallas_call | solution.py:239
  231.7 5.1 %outer.2 = (bf16[512,2048]{1,0:T(8,128)(2,1)S(1)}, bf16[512,2048]{1,0:T(8,128)(2,1)}, bf16[512,2048]{1,0:T(8,128)(2,1)}, bf16[512,2048]{1,0:T(8,128)(2,1)}) custom-call(bf16[256,2048]{1,0:T(8,128)(2,1)S(1)} %slice.453.x_ref, bf16[256,2048]{1,0:T(8,128)(2,1)S(1)} %bitcast.173), custom_call_target="tpu_custom_call" | custom-call | tf_op jit(solution)/shard_map/outer/pallas_call | solution.py:407
  239.1 3.9 collective-permute-done.32
  243.4 3.9 add_convert_fusion.2
  252.1 7.8 %down.2 = (f32[256,1024]{1,0:T(8,128)S(1)}, bf16[256,1024]{1,0:T(8,128)(2,1)}) custom-call(bf16[256,2048]{1,0:T(8,128)(2,1)S(1)} %bitcast.172, bf16[2048,2048]{1,0:T(8,128)(2,1)} %all-gather.2.cloned.1.call-done.refs_1_.refs_2_.refs_3_.refs_4_.refs_5_.refs_6_.refs_7_.refs_8_.refs_9_.refs_10_.refs_11_.refs_12_.refs_13_.refs_14_.refs_15_.refs_16_, ...), custom_call_target="tpu_custom_call" | custom-call | tf_op jit(solution)/shard_map/down/pallas_call | solution.py:367
  261.5 6.1 %collective-permute-done.34 = bf16[2,16,2048]{2,1,0:T(8,128)(2,1)} collective-permute-done((bf16[2,16,2048]{2,1,0:T(8,128)(2,1)}, bf16[2,16,2048]{2,1,0:T(8,128)(2,1)}, u32[]{:S(2)}, u32[]{:S(2)}) %collective-permute-start.34) | collective-permute-done | bytes 131104 | tf_op jit(solution)/shard_map/r3/ppermute | solution.py:502
  269.5 17.9 %reverse_main.2 = (f32[2,16,8,2048]{3,2,1,0:T(8,128)}, f32[2,16,8,2048]{3,2,1,0:T(8,128)}, f32[2,128,32,128]{3,2,1,0:T(8,128)}, f32[2,16,2048]{2,1,0:T(8,128)}) custom-call(f32[2,16,8,2048]{3,2,1,0:T(8,128)} %copy-done.5, f32[2,16,8,2048]{3,2,1,0:T(8,128)} %get-tuple-element.194.delta_ref, f32[2,16,8,2048]{3,2,1,0:T(8,128)} %fusion.6.flow_ref, ...), custom_call_target="tpu_custom_call" | custom-call | tf_op jit(solution)/shard_map/reverse_main/pallas_call | solution.py:273
  290.6 17.7 %reverse_main.3 = (f32[2,16,8,2048]{3,2,1,0:T(8,128)}, f32[2,16,8,2048]{3,2,1,0:T(8,128)}, f32[2,128,32,128]{3,2,1,0:T(8,128)}, f32[2,16,2048]{2,1,0:T(8,128)}) custom-call(f32[2,16,8,2048]{3,2,1,0:T(8,128)} %copy-done.5, ...), custom_call_target="tpu_custom_call", output_to_operand_aliasing={{0}: (10, {}), {1}: (11, {}), {2}: (12, {}), {3}: (13, {})} | custom-call | tf_op jit(solution)/shard_map/reverse_main/pallas_call | solution.py:273
  316.6 3.8 collective-permute-done.37
  322.2 4.3 multiply_multiply_fusion.2
  331.3 5.3 %outer.3 = (bf16[512,2048]{1,0:T(8,128)(2,1)S(1)}, bf16[512,2048]{1,0:T(8,128)(2,1)}, bf16[512,2048]{1,0:T(8,128)(2,1)}, bf16[512,2048]{1,0:T(8,128)(2,1)}) custom-call(bf16[256,2048]{1,0:T(8,128)(2,1)S(1)} %slice.453.x_ref, bf16[256,2048]{1,0:T(8,128)(2,1)S(1)} %bitcast.175), custom_call_target="tpu_custom_call" | custom-call | tf_op jit(solution)/shard_map/outer/pallas_call | solution.py:407
  346.9 4.2 add_convert_fusion
  351.1 3.7 collective-permute-start.44
  359.1 10.3 %down.3 = (f32[256,1024]{1,0:T(8,128)}, bf16[256,1024]{1,0:T(8,128)(2,1)S(1)}) custom-call(bf16[256,2048]{1,0:T(8,128)(2,1)} %bitcast.176, bf16[256,2048]{1,0:T(8,128)(2,1)} %bitcast.174, bf16[160,2048]{1,0:T(8,128)(2,1)S(1)} %copy-done.26, bf16[512,2048]{1,0:T(8,128)(2,1)} %copy-done.2, bf16[160,2048]{1,0:T(8,128)(2,1)S(1)} %copy-done.29, ...), custom_call_target="tpu_custom_call" | custom-call | tf_op jit(solution)/shard_map/down/pallas_call | solution.py:367
  369.4 9.4 %collective-permute-done.44 = bf16[256,2048]{1,0:T(8,128)(2,1)S(1)} collective-permute-done((bf16[256,2048]{1,0:T(8,128)(2,1)S(1)}, bf16[256,2048]{1,0:T(8,128)(2,1)S(1)}, u32[]{:S(2)}, u32[]{:S(2)}) %collective-permute-start.44) | collective-permute-done | bytes 1048608 | tf_op jit(solution)/shard_map/yn/Ax4/ppermute | solution.py:502
  380.0 3.6 collective-permute-done.46
  410.9 4.7 %collective-permute-done.49 = bf16[4,320,128]{2,1,0:T(8,128)(2,1)S(1)} collective-permute-done((bf16[4,320,128]{2,1,0:T(8,128)(2,1)S(1)}, bf16[4,320,128]{2,1,0:T(8,128)(2,1)S(1)}, u32[]{:S(2)}, u32[]{:S(2)}) %collective-permute-start.49) | collective-permute-done | bytes 327712 | tf_op jit(solution)/shard_map/k1/ppermute | solution.py:502
  420.0 10.9 %collective-permute-done.55 = bf16[128,2048]{1,0:T(8,128)(2,1)S(1)} collective-permute-done((bf16[128,2048]{1,0:T(8,128)(2,1)S(1)}, bf16[128,2048]{1,0:T(8,128)(2,1)S(1)}, u32[]{:S(2)}, u32[]{:S(2)}) %collective-permute-start.55) | collective-permute-done | bytes 524320 | tf_op jit(solution)/shard_map/Az8/ppermute | solution.py:502
  (496 shorter events, 196.0 us)
Async XLA Ops:
  7.2 205.1 %all-gather.2.cloned.1.call-start = ((), (), s32[]{:S(2)}) async-start(), calls=%async_computation.1 | async-start | bytes 8912896 | tf_op jit(solution)/shard_map/all_gather | solution.py:1072
  14.0 29.1 %collective-permute-start.3 = (bf16[160,2048]{1,0:T(8,128)(2,1)S(1)}, bf16[160,2048]{1,0:T(8,128)(2,1)S(1)}, u32[]{:S(2)}, u32[]{:S(2)}) collective-permute-start(bf16[160,2048]{1,0:T(8,128)(2,1)S(1)} %pad_maximum_fusion.7.refs_0_.refs_2_), channel_id=1, source_target_pairs={{0,4},{2,6},{4,0},{6,2},{8,12},{10,14},{12,8},{14,10},{16,20},{18,... | collective-permute-start | bytes 1966088 | tf_op jit(solution)/shard_map/y0/ax0/ppermute | solution.py:502
  17.0 31.2 %collective-permute-start.2 = (bf16[160,2048]{1,0:T(8,128)(2,1)S(1)}, bf16[160,2048]{1,0:T(8,128)(2,1)S(1)}, u32[]{:S(2)}, u32[]{:S(2)}) collective-permute-start(bf16[160,2048]{1,0:T(8,128)(2,1)S(1)} %pad_maximum_fusion.7.refs_0_.refs_2_), channel_id=1, source_target_pairs={{0,16},{2,18},{4,20},{6,22},{8,24},{10,26},{12,28},{14,30},{16,0},... | collective-permute-start | bytes 1966088 | tf_op jit(solution)/shard_map/a8/ppermute | solution.py:502
  19.6 28.8 %collective-permute-start.1 = (bf16[160,2048]{1,0:T(8,128)(2,1)S(1)}, bf16[160,2048]{1,0:T(8,128)(2,1)S(1)}, u32[]{:S(2)}, u32[]{:S(2)}) collective-permute-start(bf16[160,2048]{1,0:T(8,128)(2,1)S(1)} %pad_maximum_fusion.7.refs_0_.refs_2_), channel_id=1, source_target_pairs={{0,8},{2,10},{4,12},{6,14},{8,0},{10,2},{12,4},{14,6},{16,24},{18,... | collective-permute-start | bytes 1966088 | tf_op jit(solution)/shard_map/a4/ppermute | solution.py:502
  21.5 21.6 %collective-permute-start.4 = (bf16[128,2048]{1,0:T(8,128)(2,1)S(1)}, bf16[128,2048]{1,0:T(8,128)(2,1)}, u32[]{:S(2)}, u32[]{:S(2)}) collective-permute-start(bf16[128,2048]{1,0:T(8,128)(2,1)S(1)} %bitcast.177), channel_id=1, source_target_pairs={{0,4},{2,6},{4,0},{6,2},{8,12},{10,14},{12,8},{14,10},{16,20},{18,... | collective-permute-start | bytes 1572872 | tf_op jit(solution)/shard_map/a12/bx0/ppermute | solution.py:502
  48.4 20.7 %collective-permute-start.7 = (bf16[160,2048]{1,0:T(8,128)(2,1)S(1)}, bf16[160,2048]{1,0:T(8,128)(2,1)S(1)}, u32[]{:S(2)}, u32[]{:S(2)}) collective-permute-start(bf16[160,2048]{1,0:T(8,128)(2,1)S(1)} %collective-permute-done.2.refs_8_.refs_10_), channel_id=1, source_target_pairs={{0,4},{2,6},{4,0},{6,2},{8,12},{10,14},{12,8},{14,10},{16,20},{18,... | collective-permute-start | bytes 1966088 | tf_op jit(solution)/shard_map/ax8/ppermute | solution.py:502
  48.9 17.9 %collective-permute-start.5 = (bf16[160,2048]{1,0:T(8,128)(2,1)S(1)}, bf16[160,2048]{1,0:T(8,128)(2,1)S(1)}, u32[]{:S(2)}, u32[]{:S(2)}) collective-permute-start(bf16[160,2048]{1,0:T(8,128)(2,1)S(1)} %collective-permute-done.2.refs_8_.refs_10_), channel_id=1, source_target_pairs={{0,8},{2,10},{4,12},{6,14},{8,0},{10,2},{12,4},{14,6},{16,24},{18,... | collective-permute-start | bytes 1966088 | tf_op jit(solution)/shard_map/a12/ppermute | solution.py:502
  51.2 27.1 %collective-permute-start.6 = (bf16[160,2048]{1,0:T(8,128)(2,1)S(1)}, bf16[160,2048]{1,0:T(8,128)(2,1)S(1)}, u32[]{:S(2)}, u32[]{:S(2)}) collective-permute-start(bf16[160,2048]{1,0:T(8,128)(2,1)S(1)} %collective-permute-done.1.refs_4_.refs_6_), channel_id=1, source_target_pairs={{0,4},{2,6},{4,0},{6,2},{8,12},{10,14},{12,8},{14,10},{16,20},{18,... | collective-permute-start | bytes 1966088 | tf_op jit(solution)/shard_map/ax4/ppermute | solution.py:502
  53.2 48.9 %collective-permute-start.11 = (bf16[528,1024]{1,0:T(8,128)(2,1)}, bf16[528,1024]{1,0:T(8,128)(2,1)}, u32[]{:S(2)}, u32[]{:S(2)}) collective-permute-start(bf16[528,1024]{1,0:T(8,128)(2,1)} %fusion.17), channel_id=1, source_target_pairs={{0,1},{1,0},{2,3},{3,2},{4,5},{5,4},{6,7},{7,6},{8,9},{9,8},{10,11... | collective-permute-start | bytes 3244040 | tf_op jit(solution)/shard_map/y0/ppermute | solution.py:498
  66.8 26.1 %collective-permute-start.14 = (bf16[128,2048]{1,0:T(8,128)(2,1)S(1)}, bf16[128,2048]{1,0:T(8,128)(2,1)S(1)}, u32[]{:S(2)}, u32[]{:S(2)}) collective-permute-start(bf16[128,2048]{1,0:T(8,128)(2,1)S(1)} %bitcast.178), channel_id=1, source_target_pairs={{0,16},{2,18},{4,20},{6,22},{8,24},{10,26},{12,28},{14,30},{16,0},... | collective-permute-start | bytes 1572872 | tf_op jit(solution)/shard_map/as2/b8/ppermute | solution.py:502
  67.4 25.5 %collective-permute-start.13 = (bf16[128,2048]{1,0:T(8,128)(2,1)S(1)}, bf16[128,2048]{1,0:T(8,128)(2,1)}, u32[]{:S(2)}, u32[]{:S(2)}) collective-permute-start(bf16[128,2048]{1,0:T(8,128)(2,1)S(1)} %bitcast.179), channel_id=1, source_target_pairs={{0,8},{2,10},{4,12},{6,14},{8,0},{10,2},{12,4},{14,6},{16,24},{18,... | collective-permute-start | bytes 1572872 | tf_op jit(solution)/shard_map/as2/b4/ppermute | solution.py:502
  81.7 27.3 %collective-permute-start.12 = (bf16[512,2048]{1,0:T(8,128)(2,1)}, bf16[512,2048]{1,0:T(8,128)(2,1)S(1)}, u32[]{:S(2)}, u32[]{:S(2)}) collective-permute-start(bf16[512,2048]{1,0:T(8,128)(2,1)} %pad_maximum_fusion.1), channel_id=1, source_target_pairs={{0,2},{2,0},{4,6},{6,4},{8,10},{10,8},{12,14},{14,12},{16,18},{18,... | collective-permute-start | bytes 6291464 | tf_op jit(solution)/shard_map/as0/ppermute | solution.py:502
  117.2 224.5 %reduce-scatter.2.cloned.1.call-start = ((), (), s32[]{:S(2)}) async-start(), calls=%async_computation.2 | async-start | bytes 8912896 | tf_op jit(solution)/shard_map/reduce_scatter | solution.py:1177
  120.2 71.1 %collective-permute-start.27 = (bf16[128,2048]{1,0:T(8,128)(2,1)}, bf16[128,2048]{1,0:T(8,128)(2,1)}, u32[]{:S(2)}, u32[]{:S(2)}) collective-permute-start(bf16[128,2048]{1,0:T(8,128)(2,1)} %copy-done.42), channel_id=1, source_target_pairs={{0,4},{2,6},{4,0},{6,2},{8,12},{10,14},{12,8},{14,10},{16,20},{18,... | collective-permute-start | bytes 1572872 | tf_op jit(solution)/shard_map/bs2/bx8/ppermute | solution.py:502
  130.4 60.8 %collective-permute-start.26 = (bf16[128,2048]{1,0:T(8,128)(2,1)}, bf16[128,2048]{1,0:T(8,128)(2,1)}, u32[]{:S(2)}, u32[]{:S(2)}) collective-permute-start(bf16[128,2048]{1,0:T(8,128)(2,1)} %collective-permute-done.13.refs_4_.refs_22_), channel_id=1, source_target_pairs={{0,4},{2,6},{4,0},{6,2},{8,12},{10,14},{12,8},{14,10},{16,20},{18,... | collective-permute-start | bytes 1572872 | tf_op jit(solution)/shard_map/bs2/bx4/ppermute | solution.py:502
  130.4 29.8 %collective-permute-start.24 = (bf16[128,2048]{1,0:T(8,128)(2,1)S(1)}, bf16[128,2048]{1,0:T(8,128)(2,1)}, u32[]{:S(2)}, u32[]{:S(2)}) collective-permute-start(bf16[128,2048]{1,0:T(8,128)(2,1)S(1)} %copy-done.43), channel_id=1, source_target_pairs={{0,8},{2,10},{4,12},{6,14},{8,0},{10,2},{12,4},{14,6},{16,24},{18,... | collective-permute-start | bytes 1572872 | tf_op jit(solution)/shard_map/bs0/b12/ppermute | solution.py:502
  160.3 31.0 %collective-permute-start.28 = (bf16[128,2048]{1,0:T(8,128)(2,1)}, bf16[128,2048]{1,0:T(8,128)(2,1)S(1)}, u32[]{:S(2)}, u32[]{:S(2)}) collective-permute-start(bf16[128,2048]{1,0:T(8,128)(2,1)} %collective-permute-done.24.refs_12_.refs_30_), channel_id=1, source_target_pairs={{0,4},{2,6},{4,0},{6,2},{8,12},{10,14},{12,8},{14,10},{16,20},{18,... | collective-permute-start | bytes 1572872 | tf_op jit(solution)/shard_map/bs2/bx12/ppermute | solution.py:502
  166.9 28.4 %collective-permute-start.25 = (bf16[512,2048]{1,0:T(8,128)(2,1)}, bf16[512,2048]{1,0:T(8,128)(2,1)S(1)}, u32[]{:S(2)}, u32[]{:S(2)}) collective-permute-start(bf16[512,2048]{1,0:T(8,128)(2,1)} %pad_maximum_fusion.3), channel_id=1, source_target_pairs={{0,2},{2,0},{4,6},{6,4},{8,10},{10,8},{12,14},{14,12},{16,18},{18,... | collective-permute-start | bytes 6291464 | tf_op jit(solution)/shard_map/bs0/ppermute | solution.py:502
  239.1 48.4 %collective-permute-start.39 = (bf16[512,2048]{1,0:T(8,128)(2,1)}, bf16[512,2048]{1,0:T(8,128)(2,1)}, u32[]{:S(2)}, u32[]{:S(2)}) collective-permute-start(bf16[512,2048]{1,0:T(8,128)(2,1)} %get-tuple-element.108), channel_id=1, source_target_pairs={{0,2},{2,0},{4,6},{6,4},{8,10},{10,8},{12,14},{14,12},{16,18},{18,... | collective-permute-start | bytes 6291464 | tf_op jit(solution)/shard_map/Bz12/Bs0/ppermute | solution.py:502
  247.2 40.3 %collective-permute-start.36 = (bf16[256,2048]{1,0:T(8,128)(2,1)}, bf16[256,2048]{1,0:T(8,128)(2,1)}, u32[]{:S(2)}, u32[]{:S(2)}) collective-permute-start(bf16[256,2048]{1,0:T(8,128)(2,1)} %get-tuple-element.185), channel_id=1, source_target_pairs={{0,4},{2,6},{4,0},{6,2},{8,12},{10,14},{12,8},{14,10},{16,20},{18,... | collective-permute-start | bytes 3145736 | tf_op jit(solution)/shard_map/Bx4/ppermute | solution.py:502
  249.9 17.7 %collective-permute-start.34 = (bf16[2,16,2048]{2,1,0:T(8,128)(2,1)}, bf16[2,16,2048]{2,1,0:T(8,128)(2,1)}, u32[]{:S(2)}, u32[]{:S(2)}) collective-permute-start(bf16[2,16,2048]{2,1,0:T(8,128)(2,1)} %fusion.46), channel_id=1, source_target_pairs={{0,16},{2,18},{4,20},{6,22},{8,24},{10,26},{12,28},{14,30},{16,0},... | collective-permute-start | bytes 393224 | tf_op jit(solution)/shard_map/r3/ppermute | solution.py:502
  260.0 60.5 %collective-permute-start.31 = (bf16[256,1024]{1,0:T(8,128)(2,1)}, bf16[256,1024]{1,0:T(8,128)(2,1)}, u32[]{:S(2)}, u32[]{:S(2)}) collective-permute-start(bf16[256,1024]{1,0:T(8,128)(2,1)} %get-tuple-element.95), channel_id=1, source_target_pairs={{0,1},{1,0},{2,3},{3,2},{4,5},{5,4},{6,7},{7,6},{8,9},{9,8},{10,11... | collective-permute-start | bytes 1572872 | tf_op jit(solution)/shard_map/yb/ppermute | solution.py:498
  287.4 33.1 %collective-permute-start.38 = (bf16[256,2048]{1,0:T(8,128)(2,1)}, bf16[256,2048]{1,0:T(8,128)(2,1)}, u32[]{:S(2)}, u32[]{:S(2)}) collective-permute-start(bf16[256,2048]{1,0:T(8,128)(2,1)} %get-tuple-element.184), channel_id=1, source_target_pairs={{0,4},{2,6},{4,0},{6,2},{8,12},{10,14},{12,8},{14,10},{16,20},{18,... | collective-permute-start | bytes 3145736 | tf_op jit(solution)/shard_map/Bx0/ppermute | solution.py:502
  290.6 29.9 %collective-permute-start.40 = (bf16[128,2048]{1,0:T(8,128)(2,1)}, bf16[128,2048]{1,0:T(8,128)(2,1)}, u32[]{:S(2)}, u32[]{:S(2)}) collective-permute-start(bf16[128,2048]{1,0:T(8,128)(2,1)} %get-tuple-element.181), channel_id=1, source_target_pairs={{0,8},{2,10},{4,12},{6,14},{8,0},{10,2},{12,4},{14,6},{16,24},{18,... | collective-permute-start | bytes 1572872 | tf_op jit(solution)/shard_map/Bz12/ppermute | solution.py:502
  341.7 16.7 %collective-permute-start.43 = (bf16[512,2048]{1,0:T(8,128)(2,1)}, bf16[512,2048]{1,0:T(8,128)(2,1)}, u32[]{:S(2)}, u32[]{:S(2)}) collective-permute-start(bf16[512,2048]{1,0:T(8,128)(2,1)} %get-tuple-element.112), channel_id=1, source_target_pairs={{0,2},{2,0},{4,6},{6,4},{8,10},{10,8},{12,14},{14,12},{16,18},{18,... | collective-permute-start | bytes 6291464 | tf_op jit(solution)/shard_map/As0/ppermute | solution.py:502
  344.1 35.8 %collective-permute-start.57 = (bf16[128,2048]{1,0:T(8,128)(2,1)}, bf16[128,2048]{1,0:T(8,128)(2,1)S(1)}, u32[]{:S(2)}, u32[]{:S(2)}) collective-permute-start(bf16[128,2048]{1,0:T(8,128)(2,1)} %get-tuple-element.180), channel_id=1, source_target_pairs={{0,8},{2,10},{4,12},{6,14},{8,0},{10,2},{12,4},{14,6},{16,24},{18,... | collective-permute-start | bytes 1572872 | tf_op jit(solution)/shard_map/Bz4/ppermute | solution.py:502
  351.1 27.6 %collective-permute-start.44 = (bf16[256,2048]{1,0:T(8,128)(2,1)S(1)}, bf16[256,2048]{1,0:T(8,128)(2,1)S(1)}, u32[]{:S(2)}, u32[]{:S(2)}) collective-permute-start(bf16[256,2048]{1,0:T(8,128)(2,1)S(1)} %get-tuple-element.183), channel_id=1, source_target_pairs={{0,4},{2,6},{4,0},{6,2},{8,12},{10,14},{12,8},{14,10},{16,20},{18,... | collective-permute-start | bytes 3145736 | tf_op jit(solution)/shard_map/yn/Ax4/ppermute | solution.py:502
  357.3 26.2 %collective-permute-start.46 = (bf16[128,2048]{1,0:T(8,128)(2,1)}, bf16[128,2048]{1,0:T(8,128)(2,1)S(1)}, u32[]{:S(2)}, u32[]{:S(2)}) collective-permute-start(bf16[128,2048]{1,0:T(8,128)(2,1)} %add_convert_fusion.8), channel_id=1, source_target_pairs={{0,16},{2,18},{4,20},{6,22},{8,24},{10,26},{12,28},{14,30},{16,0},... | collective-permute-start | bytes 1572872 | tf_op jit(solution)/shard_map/Bz8/ppermute | solution.py:502
  358.1 44.5 %collective-permute-start.53 = (bf16[256,2048]{1,0:T(8,128)(2,1)}, bf16[256,2048]{1,0:T(8,128)(2,1)}, u32[]{:S(2)}, u32[]{:S(2)}) collective-permute-start(bf16[256,2048]{1,0:T(8,128)(2,1)} %get-tuple-element.122), channel_id=1, source_target_pairs={{0,4},{2,6},{4,0},{6,2},{8,12},{10,14},{12,8},{14,10},{16,20},{18,... | collective-permute-start | bytes 3145736 | tf_op jit(solution)/shard_map/Az8/Ax0/ppermute | solution.py:502
  388.9 31.0 %collective-permute-start.56 = (bf16[128,2048]{1,0:T(8,128)(2,1)}, bf16[128,2048]{1,0:T(8,128)(2,1)}, u32[]{:S(2)}, u32[]{:S(2)}) collective-permute-start(bf16[128,2048]{1,0:T(8,128)(2,1)} %get-tuple-element.179), channel_id=1, source_target_pairs={{0,8},{2,10},{4,12},{6,14},{8,0},{10,2},{12,4},{14,6},{16,24},{18,... | collective-permute-start | bytes 1572872 | tf_op jit(solution)/shard_map/Az4/ppermute | solution.py:502
  405.9 25.1 %collective-permute-start.55 = (bf16[128,2048]{1,0:T(8,128)(2,1)S(1)}, bf16[128,2048]{1,0:T(8,128)(2,1)S(1)}, u32[]{:S(2)}, u32[]{:S(2)}) collective-permute-start(bf16[128,2048]{1,0:T(8,128)(2,1)S(1)} %add_convert_fusion.6), channel_id=1, source_target_pairs={{0,16},{2,18},{4,20},{6,22},{8,24},{10,26},{12,28},{14,30},{16,0},... | collective-permute-start | bytes 1572872 | tf_op jit(solution)/shard_map/Az8/ppermute | solution.py:502
  415.8 17.0 %collective-permute-start.50 = (bf16[2,320,128]{2,1,0:T(8,128)(2,1)S(1)}, bf16[2,320,128]{2,1,0:T(8,128)(2,1)S(1)}, u32[]{:S(2)}, u32[]{:S(2)}) collective-permute-start(bf16[2,320,128]{2,1,0:T(8,128)(2,1)S(1)} %slice.619), channel_id=1, source_target_pairs={{0,8},{2,10},{4,12},{6,14},{8,0},{10,2},{12,4},{14,6},{16,24},{18,... | collective-permute-start | bytes 491528 | tf_op jit(solution)/shard_map/k2/ppermute | solution.py:502
  (162 other events, 1567.6 us)
Sparse Core Ops, SparseCore 0:
  117.3 93.8 all-gather.1
  215.3 124.1 reduce-scatter.1
